TPU v7x, 128 devices: a whole 4x4x4 slice. The times are simulated.
128 devices in a mesh: leaf: 4 (over z_hi, core), col: 32 (over y, x, z_lo).
Axes of the slice: x: 4, y: 4, z: 4 (z_hi: 2, z_lo: 2; z = z_hi * 2 + z_lo), core: 2. Of those that a mesh axis runs over, the one named last changes fastest.
Arguments:
- child_panels: bfloat16 [4, 32, 2048, 1536], P('leaf', 'col'), may hold values from -0.078125 to 0.078125
- child_fronts: float32 [4, 32, 16, 2048, 128], P('leaf', 'col'), may hold values from -0.01 to 0.09
- parent_front: float32 [4096, 4096], P('leaf', 'col'), may hold values from -0.06 to 8
- block_maps: int32 [4, 32, 16], replicated, may hold values from 0 to 31, as said below
- right_sides: float32 [4096, 128], P('leaf'), may hold values from -16 to 16
Outputs:
- factor: float32 [4096, 4096], P('leaf', 'col')
- whitened: float32 [128, 128], replicated
- condensed: float32 [4096, 128], P('leaf')
Inputs may be any that keep to these rules, and one draw needn't show every extreme that they name: `block_maps`: each subtree's 16 entries are increasing and distinct, with exactly 4 of them in each range of 8 consecutive parent blocks starting at a multiple of 8.
All inputs are finite; a program needn't handle non-finite values.
Results may differ from a plain program's by a relative error of at most 0.0003.
Values sent between devices are 32-bit elements; how exact they have to be, the bound alone decides.
No kernel may reach another device: no remote copies, remote signals or barrier semaphores. Data moves between devices by JAX's collectives and lax.ppermute only.
A program may use at most 192 MiB of HBM per device.

v0:
```python
import jax
import jax.numpy as jnp
from jax import lax
from jax.sharding import PartitionSpec as P

NP = 1


def from_root(value, axis, root):
    mine = lax.axis_index(axis) == root
    return lax.psum(jnp.where(mine, value, jnp.zeros_like(value)), axis)


def per_device(child_panels, child_fronts, parent_front, block_maps, right_sides):
    leaves = lax.axis_size("leaf")
    columns = lax.axis_size("col")
    leaf_id = lax.axis_index("leaf")
    col_id = lax.axis_index("col")
    blocks_child = child_fronts.shape[2]
    block_size = child_fronts.shape[4]
    order_child = child_panels.shape[2]
    pivots = child_panels.shape[3]
    local_rows = parent_front.shape[0]
    local_cols = parent_front.shape[1]
    per_col = local_cols // block_size
    parent_blocks = per_col * columns
    range_blocks = parent_blocks // leaves
    highest = lax.Precision.HIGHEST
    child_panel = child_panels[0, 0]
    grouped = child_panel.reshape(blocks_child, block_size, pivots)
    update = child_fronts[0, 0] - jnp.einsum(
        "rk,bck->brc", child_panel, grouped, preferred_element_type=jnp.float32
    )
    leaf_lists = lax.dynamic_index_in_dim(block_maps, leaf_id, 0, keepdims=False)
    my_map = lax.dynamic_index_in_dim(leaf_lists, col_id, 0, keepdims=False)
    targets = jnp.arange(parent_blocks, dtype=jnp.int32)
    routing = (my_map[:, None] == targets[None, :]).astype(jnp.float32)
    outgoing = jnp.einsum("bq,brc->qrc", routing, update, precision=highest).reshape(
        columns, per_col, order_child, block_size
    )
    incoming = lax.all_to_all(outgoing, "col", split_axis=0, concat_axis=0, tiled=True)
    blocks_in = incoming.reshape(columns, per_col, blocks_child, block_size, block_size)
    placing = (leaf_lists[:, :, None] == targets[None, None, :]).astype(jnp.float32)
    whole = jnp.einsum("sbp,sqbij->piqj", placing, blocks_in, precision=highest).reshape(
        local_rows * leaves, local_cols
    )
    assembled = lax.psum_scatter(whole, "leaf", scatter_dimension=0, tiled=True)
    front_local = parent_front + assembled
    rhs_local = right_sides
    row_global = leaf_id * local_rows + jnp.arange(local_rows, dtype=jnp.int32)
    col_global = col_id * local_cols + jnp.arange(local_cols, dtype=jnp.int32)
    saved = jnp.zeros((local_rows, local_cols), jnp.float32)
    pivot_span = NP * block_size
    owner_col = 0 // per_col
    local_block = 0 % per_col
    owner = col_id == owner_col
    left = local_block * block_size
    right = left + block_size
    diagonal = from_root(front_local[0:block_size, left:right], "leaf", 0)
    rhs_block = from_root(rhs_local[0:block_size], "leaf", 0)
    diagonal = jnp.where(owner, diagonal, jnp.eye(block_size, dtype=jnp.float32))
    factor_block = jnp.tril(lax.linalg.cholesky(diagonal, symmetrize_input=False))
    column = front_local
    solved = lax.linalg.triangular_solve(
        factor_block, column, left_side=False, lower=True, transpose_a=True
    )
    placed = jnp.zeros((local_rows, block_size), jnp.float32).at[0:block_size].set(factor_block)
    panel = jnp.where(
        row_global[:, None] >= block_size, solved, jnp.where(row_global[:, None] >= 0, placed, 0.0)
    )
    y_block = lax.linalg.triangular_solve(factor_block, rhs_block, left_side=True, lower=True)
    panel, y_block = (from_root(panel, "col", owner_col), from_root(y_block, "col", owner_col))
    offset = col_id * per_col % range_blocks * block_size
    own_rows = lax.dynamic_slice_in_dim(panel, offset, local_cols, 0)
    shared = lax.all_gather(own_rows, "leaf", axis=0, tiled=True)
    own_panel = lax.dynamic_slice_in_dim(
        shared, col_id * per_col // range_blocks * local_cols, local_cols, 0
    )
    front_local = front_local - lax.dot_general(
        panel,
        own_panel,
        (((1,), (1,)), ((), ())),
        precision=highest,
        preferred_element_type=jnp.float32,
    )
    rhs_local = rhs_local - jnp.dot(
        panel, y_block, precision=highest, preferred_element_type=jnp.float32
    )
    saved = saved.at[:, left:right].set(jnp.where(owner, panel, saved))
    pivot_cols = col_global < pivot_span
    factor = jnp.where(
        pivot_cols[None, :], saved, jnp.where(row_global[:, None] >= pivot_span, front_local, 0.0)
    )
    condensed = jnp.where(row_global[:, None] >= pivot_span, rhs_local, 0.0)
    return (factor, y_block, condensed)


def solution(mesh):
    in_specs = (
        P("leaf", "col", None, None),
        P("leaf", "col", None, None, None),
        P("leaf", "col"),
        P(),
        P("leaf", None),
    )
    out_specs = (P("leaf", "col"), P(), P("leaf", None))
    return jax.shard_map(
        per_device, mesh=mesh, in_specs=in_specs, out_specs=out_specs, check_vma=False
    )
```

profile of v0, /device:TPU:97, one launch (start us, length us, event | category | flops | bytes accessed | tf_op | source)
XLA Modules:
  0.0 1222.0 jit_solution(5759184764659116530)
XLA Ops:
  7.2 17.6 %copy.14 = f32[1,1,16,2048,128]{3,4,2,1,0:T(8,128)} copy(f32[1,1,16,2048,128]{4,3,2,1,0:T(8,128)} %param.12) | data formatting | bytes 33554432 | tf_op args[1]
  24.8 25.9 %bitcast_subtract_fusion = f32[16,2048,128]{1,2,0:T(8,128)} fusion(f32[1,1,16,2048,128]{3,4,2,1,0:T(8,128)} %copy.14, bf16[16,128,1536]{2,1,0:T(8,128)(2,1)} %bitcast.48, bf16[1,1,2048,1536]{3,2,1,0:T(8,128)(2,1)} %param.11), kind=kOutput, calls=%fused_computation | convolution fusion | flops 12889096192 | bytes 46137344 | tf_op jit(solution)/shard_map/rk,bck->brc/dot_general | solution.py:31
  50.8 17.7 %copy.15 = f32[16,2048,128]{2,0,1:T(8,128)} copy(f32[16,2048,128]{1,2,0:T(8,128)} %bitcast_subtract_fusion) | data formatting | bytes 33554432 | tf_op jit(solution)/shard_map/sub | solution.py:31
  68.6 17.0 %convolution_bitcast_fusion = f32[32,1,2048,128]{3,0,2,1:T(8,128)S(1)} fusion(f32[16,2048,128]{2,0,1:T(8,128)} %copy.15, s32[16]{0:T(128)S(1)} %dynamic-slice_reduce_fusion), kind=kOutput, calls=%fused_computation.1 | convolution fusion | flops 1610613248 | bytes 50331712 | tf_op jit(solution)/shard_map/bq,brc->qrc/dot_general | solution.py:38
  85.6 36.8 %copy.16 = f32[32,1,2048,128]{3,2,1,0:T(8,128)} copy(f32[32,1,2048,128]{3,0,2,1:T(8,128)S(1)} %convolution_bitcast_fusion) | data formatting | bytes 67108864 | tf_op jit(solution)/shard_map/reshape | solution.py:38
  122.4 8.1 all-to-all-start
  130.5 541.1 %all-to-all-done = f32[32,1,2048,128]{3,2,1,0:T(8,128)} async-done(((f32[32,1,2048,128]{3,2,1,0:T(8,128)}), f32[32,1,2048,128]{3,2,1,0:T(8,128)}, u32[]{:S(2)}, u32[]{:S(2)}) %all-to-all-start) | async-done | bytes 33554464 | tf_op jit(solution)/shard_map/all_to_all | solution.py:41
  671.7 31.8 %copy.17 = f32[32,1,2048,128]{3,0,2,1:T(8,128)} copy(f32[32,1,2048,128]{3,2,1,0:T(8,128)} %all-to-all-done) | data formatting | bytes 67108864 | tf_op jit(solution)/shard_map/all_to_all | solution.py:41
  703.4 16.7 %convolution_bitcast_fusion.1 = f32[32,128,1,128]{3,0,1,2:T(8,128)S(1)} fusion(f32[32,16,128,128]{3,0,2,1:T(8,128)} %bitcast.46, s32[32,16]{0,1:T(8,128)S(1)} %dynamic-slice_bitcast_fusion), kind=kOutput, calls=%fused_computation.3 | convolution fusion | flops 3221241856 | bytes 35653632 | tf_op jit(solution)/shard_map/sbp,sqbij->piqj/dot_general | solution.py:44
  720.2 2.6 copy.18
  723.4 113.8 %reduce-scatter.2.cloned.1.call-done = f32[1024,128]{1,0:T(8,128)} async-done(((f32[4096,128]{1,0:T(8,128)}), f32[1024,128]{1,0:T(8,128)}) %reduce-scatter.2.cloned.1.call-update) | async-done | bytes 524304 | tf_op jit(solution)/shard_map/reduce_scatter | solution.py:47
  837.3 1.1 add.86
  839.3 41.0 %all-reduce.8.cloned.1.call-done = (f32[128,128]{1,0:T(8,128)}, f32[128,128]{1,0:T(8,128)}) async-done(((f32[128,128]{1,0:T(8,128)}, f32[128,128]{1,0:T(8,128)}), (f32[128,128]{1,0:T(8,128)}, f32[128,128]{1,0:T(8,128)})) %all-reduce.8.cloned.1.call-update) | async-done | bytes 131088 | tf_op jit(solution)/shard_map/psum | solution.py:11
  880.3 11.7 cholesky.16
  892.7 0.7 select_bitcast_fusion
  893.5 9.8 custom-call.7
  903.3 1.8 convolution_select_fusion.1
  905.0 1.4 fusion.1
  906.5 276.2 %all-reduce.6.cloned.1.call-done = (f32[1024,128]{1,0:T(8,128)}, f32[128,128]{1,0:T(8,128)}) async-done(((f32[1024,128]{1,0:T(8,128)}, f32[128,128]{1,0:T(8,128)}), (f32[1024,128]{1,0:T(8,128)}, f32[128,128]{1,0:T(8,128)})) %all-reduce.6.cloned.1.call-update) | async-done | bytes 589840 | tf_op jit(solution)/shard_map/psum | solution.py:11
  1182.7 2.4 fusion.2
  1185.1 0.8 constant_dynamic-slice_fusion
  1185.9 25.5 %all_gather.3 = f32[512,128]{1,0:T(8,128)S(1)} all-gather(f32[128,128]{1,0:T(8,128)S(1)} %constant_dynamic-slice_fusion), channel_id=1, replica_groups=mesh['leaf'=4,'col'=32] {'leaf'}, dimensions={0}, use_global_device_ids=true | all-gather | bytes 327680 | tf_op jit(solution)/shard_map/all_gather | solution.py:75
  1211.4 2.6 fusion.4
  1214.0 1.5 copy.24
  (22 shorter events, 2.6 us)
Async XLA Ops:
  7.2 61.3 %copy-start = (s32[4,32,16]{1,2,0:T(8,128)S(1)}, s32[4,32,16]{1,2,0:T(8,128)}, u32[]{:S(2)}) copy-start(s32[4,32,16]{1,2,0:T(8,128)} %param.14) | copy-start | bytes 24580
  122.4 549.3 %all-to-all-start = ((f32[32,1,2048,128]{3,2,1,0:T(8,128)}), f32[32,1,2048,128]{3,2,1,0:T(8,128)}, u32[]{:S(2)}, u32[]{:S(2)}) async-start(f32[32,1,2048,128]{3,2,1,0:T(8,128)} %copy.16), calls=%async_computation | async-start | bytes 67108864 | tf_op jit(solution)/shard_map/all_to_all | solution.py:41
  130.5 706.8 %reduce-scatter.2.cloned.1.call-start = ((), (), s32[]{:S(2)}) async-start(), calls=%async_computation.2 | async-start | bytes 2621440 | tf_op jit(solution)/shard_map/reduce_scatter | solution.py:47
  703.4 19.4 %copy-start.1 = (f32[1024,128]{1,0:T(8,128)S(1)}, f32[1024,128]{1,0:T(8,128)}, u32[]{:S(2)}) copy-start(f32[1024,128]{1,0:T(8,128)} %param.15) | copy-start | bytes 1572868
  703.4 133.8 %copy-start.2 = (f32[1024,128]{1,0:T(8,128)S(1)}, f32[1024,128]{1,0:T(8,128)}, u32[]{:S(2)}) copy-start(f32[1024,128]{1,0:T(8,128)} %param.13) | copy-start | bytes 1572868
  722.7 157.6 %all-reduce.8.cloned.1.call-start = ((), (), s32[]{:S(2)}) async-start(), calls=%async_computation.4 | async-start | bytes 262144 | tf_op jit(solution)/shard_map/psum | solution.py:11
  839.0 343.6 %all-reduce.6.cloned.1.call-start = ((), (), s32[]{:S(2)}) async-start(), calls=%async_computation.3 | async-start | bytes 1179648 | tf_op jit(solution)/shard_map/psum | solution.py:11
Sparse Core Ops, SparseCore 0:
  722.9 114.3 reduce-scatter.1
  840.5 39.7 all-reduce.7
  906.5 276.0 all-reduce.5
where the time goes:
time: 1230 us; the launch traced here: 1220 us
  waiting for transfers between devices  972 us (79%)
  local copies, waits for them, and re-layouts  109 us (9%)
  matrix products  67.8 us (6%)
  blocking collectives  25.5 us (2%)
  other arithmetic  25.3 us (2%)
  between operations  13.9 us (1%)
    all_to_all x1, waiting for transfers between devices, per_device(): lax.all_to_all(outgoing, 'col', split_axis=0, concat_axis=0, tiled=True)  541 us
    psum x2, waiting for transfers between devices, from_root(): return lax.psum(jnp.where(mine, value, jnp.zeros_like(value)), axis)  317 us
    reduce_scatter x1, waiting for transfers between devices, per_device(): assembled = lax.psum_scatter(whole, 'leaf', scatter_dimension=0, tiled=True)  114 us
    reshape x1, local copies, waits for them, and re-layouts, per_device(): jnp.einsum('bq,brc->qrc', routing, update, precision=highest)  36.8 us
    all_to_all x1, local copies, waits for them, and re-layouts, per_device(): lax.all_to_all(outgoing, 'col', split_axis=0, concat_axis=0, tiled=True)  31.8 us
    dot_general x1, matrix products, per_device(): jnp.einsum('rk,bck->brc', child_panel, grouped, preferred_element_type=jn...  25.9 us
    all_gather x1, blocking collectives, per_device(): shared = lax.all_gather(own_rows, 'leaf', axis=0, tiled=True)  25.5 us
  transfers between devices with their start and end apart: 4, of which 4 were waited for; matrix products, arithmetic and copies ran while one was open for 0% of the time, Pallas kernels for 0%

commit v1 on v0

v1 whole, which is shorter than its diff:
```python
import functools

import jax
import jax.numpy as jnp
from jax import lax
from jax.experimental import pallas as pl
from jax.experimental.pallas import tpu as pltpu
from jax.sharding import PartitionSpec as P

BLK = 128
SUB = 32
ORDER = (2, 1, 3, 0)
AXES = ("leaf", "col")
HIGHEST = lax.Precision.HIGHEST


def links(move):
    pairs = []
    for source in range(128):
        zl, x, y = source % 2, source // 2 % 4, source // 8 % 4
        core, zh = source // 32 % 2, source // 64
        c, v, u, w = move(core, y, x, 2 * zh + zl)
        v, u, w = v % 4, u % 4, w % 4
        pairs.append((source, ((w // 2 * 2 + c) * 4 + v) * 8 + u * 2 + w % 2))
    return pairs


def along(axis, hop):
    if axis == "y":
        return links(lambda c, y, x, z: (c, y + hop, x, z))
    if axis == "x":
        return links(lambda c, y, x, z: (c, y, x + hop, z))
    return links(lambda c, y, x, z: (c, y, x, z + hop))


SIBLING = links(lambda c, y, x, z: (1 - c, y, x, z))
SWAP = links(lambda c, y, x, z: (z % 2, y, x, z // 2 * 2 + c))


def send(value, pairs):
    return lax.ppermute(value, AXES, pairs)


def product(lhs, rhs):
    return lax.dot_general(lhs, rhs, (((1,), (1,)), ((), ())), preferred_element_type=jnp.float32)


def update_columns(sub, pos, panel, front, *outs):
    step = pl.program_id(0)
    pair = pair_of(step, pos)
    lhs = panel[:, sub * SUB : (sub + 1) * SUB, :].reshape(16 * SUB, panel.shape[2])
    rhs = panel[pl.ds(2 * pair, 2)].reshape(2 * BLK, panel.shape[2])
    result = product(lhs, rhs)
    for n, out in enumerate(outs):

        @pl.when(step // 2 == n)
        def _():
            for half in range(2):
                part = result[:, half * BLK : (half + 1) * BLK].reshape(16, SUB, BLK)
                out[half] = front[half] - part


def pair_of(step, pos):
    slot = jnp.where(step < 2, ORDER[0], jnp.where(step < 4, ORDER[1], jnp.where(step < 6, ORDER[2], ORDER[3])))
    return 2 * ((pos[0] + slot) % 4) + step % 2


def update_rows(sub, pos, panel, front, out2, out1, out3, out0, scratch):
    step = pl.program_id(0)
    lhs = panel[:, sub * SUB : (sub + 1) * SUB, :].reshape(16 * SUB, panel.shape[2])
    rhs = panel[pl.ds(2 * step, 2)].reshape(2 * BLK, panel.shape[2])
    scratch[...] = product(lhs, rhs)
    for slot, out in zip(ORDER, (out2, out1, out3, out0)):
        rows = (pos[0] + slot) % 4
        for half in range(2):
            part = scratch[pl.ds(rows * 4 * SUB, 4 * SUB), half * BLK : (half + 1) * BLK]
            out[:, half] = front[half, pl.ds(4 * rows, 4)] - part.reshape(4, SUB, BLK)


def make_update(flow, sub, pos, panel, front):
    pivots = panel.shape[2]
    flops = 2 * 512 * 2048 * pivots
    cost = pl.CostEstimate(flops=flops, bytes_accessed=14 << 20, transcendentals=0)
    params = pltpu.CompilerParams(vmem_limit_bytes=32 << 20)
    whole = pl.BlockSpec((16, BLK, pivots), lambda t, pos: (0, 0, 0))
    if flow == "y":
        front_spec = pl.BlockSpec((2, 16, SUB, BLK), lambda t, pos: (pair_of(t, pos), 0, sub, 0))
        out_specs = [
            pl.BlockSpec((2, 16, SUB, BLK), functools.partial(lambda n, t, pos: (jnp.clip(t - 2 * n, 0, 1), 0, 0, 0), n))
            for n in range(4)
        ]
        shape = (4, 16, SUB, BLK)
        body, scratch = update_columns, []
    else:
        front_spec = pl.BlockSpec((2, 16, SUB, BLK), lambda t, pos: (t, 0, sub, 0))
        out_specs = [pl.BlockSpec((4, 2, SUB, BLK), lambda t, pos: (0, t, 0, 0)) for _ in range(4)]
        shape = (4, 16, SUB, BLK)
        body, scratch = update_rows, [pltpu.VMEM((16 * SUB, 2 * BLK), jnp.float32)]
    return pl.pallas_call(
        functools.partial(body, sub),
        grid_spec=pltpu.PrefetchScalarGridSpec(
            num_scalar_prefetch=1,
            grid=(8,),
            in_specs=[whole, front_spec],
            out_specs=out_specs,
            scratch_shapes=scratch,
        ),
        out_shape=[jax.ShapeDtypeStruct(shape, jnp.float32)] * 4,
        compiler_params=params,
        cost_estimate=cost,
        name="update_" + flow,
    )(pos, panel, front)


def expand_columns(pos, maps, own, behind, far, ahead, out):
    y, x, z, core = pos[0], pos[1], pos[2], pos[3]
    out[...] = jnp.zeros_like(out)
    for s, chunk in enumerate((own, behind, far, ahead)):

        def column(k, carry):
            q = maps[s, 4 * y + k] - 8 * y
            j = (q // 2 + 4 - x) % 4
            for br in range(16):
                rows = br // 4
                p = maps[s, br] - 8 * rows
                to = (rows // 2 * 2 + q % 2 + 4 - z) % 4
                kept = jnp.where(core == rows % 2, 1, 0)
                out[kept, j, to, p] += chunk[k, br]
            return carry

        lax.fori_loop(0, 4, column, 0)


def expand_rows(pos, maps, own, behind, far, ahead, out):
    y, x, z, core = pos[0], pos[1], pos[2], pos[3]
    out[...] = jnp.zeros_like(out)
    for s, chunk in enumerate((own, behind, far, ahead)):

        def row(k, carry):
            p = maps[s, 4 * z + k] - 8 * z
            for bc in range(16):
                q = maps[s, bc]
                j = (q // 2 % 4 + 4 - x) % 4
                to = (bc // 4 + 4 - y) % 4
                kept = jnp.where(core == q % 2, 1, 0)
                out[kept, j, to, p] += chunk[k, bc]
            return carry

        lax.fori_loop(0, 4, row, 0)


def make_expand(flow, pos, maps, chunks):
    vmem = pl.BlockSpec(memory_space=pltpu.VMEM)
    smem = pl.BlockSpec(memory_space=pltpu.SMEM)
    return pl.pallas_call(
        expand_columns if flow == "y" else expand_rows,
        in_specs=[smem, smem] + [vmem] * 4,
        out_specs=vmem,
        out_shape=jax.ShapeDtypeStruct((2, 4, 4, 8, SUB, BLK), jnp.float32),
        compiler_params=pltpu.CompilerParams(vmem_limit_bytes=16 << 20),
        cost_estimate=pl.CostEstimate(flops=1 << 20, bytes_accessed=16 << 20, transcendentals=0),
        name="expand_" + flow,
    )(pos, maps, *chunks)


def pivot_column(pos, my_map, panel, front, parent, out):
    out[...] = jnp.zeros_like(out)

    @pl.when(my_map[0] == 0)
    def _():
        for group in range(4):
            lhs = panel[4 * group : 4 * group + 4].reshape(4 * BLK, panel.shape[2])
            result = product(lhs, panel[0]).reshape(4, BLK, BLK)
            for n in range(4):
                out[my_map[4 * group + n]] = front[4 * group + n] - result[n]

    @pl.when(pos[4] == 0)
    def _():
        out[pl.ds(8 * pos[5], 8)] += parent[...]


def make_pivot_column(pos, my_map, panel, front, parent):
    pivots = panel.shape[2]
    smem = pl.BlockSpec(memory_space=pltpu.SMEM)
    return pl.pallas_call(
        pivot_column,
        grid=(1,),
        in_specs=[
            smem,
            smem,
            pl.BlockSpec((16, BLK, pivots), lambda t: (0, 0, 0)),
            pl.BlockSpec((pl.squeezed, 16, BLK, BLK), lambda t: (0, 0, 0, 0)),
            pl.BlockSpec((8, BLK, BLK), lambda t: (0, 0, 0)),
        ],
        out_specs=pl.BlockSpec((32, BLK, BLK), lambda t: (0, 0, 0)),
        out_shape=jax.ShapeDtypeStruct((32, BLK, BLK), jnp.float32),
        compiler_params=pltpu.CompilerParams(vmem_limit_bytes=32 << 20),
        cost_estimate=pl.CostEstimate(flops=2 * 2048 * 128 * pivots, bytes_accessed=9 << 20, transcendentals=0),
        name="pivot_column",
    )(pos, my_map, panel, front, parent)


def per_device(child_panels, child_fronts, parent_front, block_maps, right_sides):
    leaf, col = lax.axis_index("leaf"), lax.axis_index("col")
    core, y, x = leaf % 2, col // 8, col // 2 % 4
    z = leaf // 2 * 2 + col % 2
    pos = jnp.stack([y, x, z, core, col, leaf]).astype(jnp.int32)
    panel = child_panels.reshape(16, BLK, child_panels.shape[3])
    front = child_fronts.reshape(16, 16, BLK, BLK)
    flat_maps = block_maps.reshape(128, 16)

    def map_at(core, y, x, z):
        index = ((z // 2 * 2 + core) * 4 + y) * 8 + x * 2 + z % 2
        return lax.dynamic_index_in_dim(flat_maps, index, 0, keepdims=False)

    my_map = map_at(core, y, x, z)
    maps_y = jnp.stack([map_at(core, (y + d) % 4, x, z) for d in (0, 3, 2, 1)])
    maps_z = jnp.stack([map_at(core, y, x, (z + d) % 4) for d in (0, 3, 2, 1)])

    column = make_pivot_column(pos, my_map, panel, front, parent_front.reshape(8, BLK, BLK))
    rhs_rows = jnp.where((leaf == 0) & (col == 0), right_sides[0:BLK], 0.0)
    summed = lax.psum(jnp.concatenate([column.reshape(4096, BLK), rhs_rows], axis=0), AXES)

    def scatter(slots, axis):
        own = slots[0]
        return (
            own
            + send(slots[2], along(axis, 2))
            + send(slots[1], along(axis, 1))
            + send(slots[3], along(axis, -1))
        )

    pieces = []
    for sub, flow in enumerate("yzyz"):
        here = y if flow == "y" else z
        s2, s1, s3, own = make_update(flow, sub, here.reshape(1).astype(jnp.int32), panel, front)
        far = send(s2, along(flow, 2))
        behind = send(s1, along(flow, 1))
        ahead = send(s3, along(flow, -1))
        maps = maps_y if flow == "y" else maps_z
        dense = make_expand(flow, pos, maps, (own, behind, far, ahead))
        other = send(dense[0], SIBLING)
        slots = [dense[1, j] + other[j] for j in range(4)]
        partial = scatter(slots, "x")
        piece = scatter([partial[k] for k in range(4)], "z" if flow == "y" else "y")
        if flow == "z":
            piece = send(piece, SWAP)
        pieces.append(piece)
    assembled = jnp.concatenate(pieces, axis=1).reshape(1024, BLK)

    pivot_block = summed[0:BLK]
    lower = jnp.tril(lax.linalg.cholesky(pivot_block, symmetrize_input=False))
    inverse = lax.linalg.triangular_solve(
        lower, jnp.eye(BLK, dtype=jnp.float32), left_side=True, lower=True
    )
    my_rows = lax.dynamic_slice_in_dim(summed, leaf * 1024, 1024, 0)
    col_rows = lax.dynamic_slice_in_dim(summed, col * BLK, BLK, 0)
    row_global = (leaf * 1024 + jnp.arange(1024, dtype=jnp.int32))[:, None]
    solved = lax.dot_general(my_rows, inverse, (((1,), (1,)), ((), ())), precision=HIGHEST)
    own_panel = lax.dot_general(col_rows, inverse, (((1,), (1,)), ((), ())), precision=HIGHEST)
    whitened = jnp.dot(inverse, summed[4096:], precision=HIGHEST)
    schur = lax.dot_general(solved, own_panel, (((1,), (1,)), ((), ())), precision=HIGHEST)
    below = row_global >= BLK
    top = jnp.where(leaf == 0, jnp.pad(lower, ((0, 1024 - BLK), (0, 0))), 0.0)
    pivot_part = jnp.where(below, solved, top)
    base = jnp.where(below, parent_front - schur, 0.0)
    trailing = jnp.where(below, base + assembled, 0.0)
    factor = jnp.where(col == 0, pivot_part, trailing)
    condensed = jnp.where(
        below, right_sides - jnp.dot(solved, whitened, precision=HIGHEST), 0.0
    )
    return factor, whitened, condensed


def solution(mesh):
    in_specs = (
        P("leaf", "col", None, None),
        P("leaf", "col", None, None, None),
        P("leaf", "col"),
        P(),
        P("leaf", None),
    )
    out_specs = (P("leaf", "col"), P(), P("leaf", None))
    return jax.shard_map(
        per_device, mesh=mesh, in_specs=in_specs, out_specs=out_specs, check_vma=False
    )
```

time: 1230 us -> 422 us (0.34)
  waiting for transfers between devices: 972 us -> 215 us
  local copies, waits for them, and re-layouts: 109 us -> 25.7 us
  matrix products: 67.8 us -> 6.85 us
  starting transfers between devices: 8.4 us -> 61.9 us
  Pallas kernels: 0 us -> 52.2 us
  blocking collectives: 25.5 us -> 0 us
  other arithmetic: 25.3 us -> 38 us
    all_to_all x1 -> x0, waiting for transfers between devices: 541 us -> none  [per_device(): lax.all_to_all(outgoing, 'col', split_axis=0, concat_axis=0, tiled=True)]
    psum x2 -> x1, waiting for transfers between devices: 317 us -> 108 us  [per_device(): lax.psum(jnp.concatenate([column.reshape(4096, BLK), rhs_rows], axis=0),...]
    reduce_scatter x1 -> x0, waiting for transfers between devices: 114 us -> none  [per_device(): assembled = lax.psum_scatter(whole, 'leaf', scatter_dimension=0, tiled=True)]
    ppermute x0 -> x42, waiting for transfers between devices: none -> 106 us  [send(): return lax.ppermute(value, AXES, pairs)]
    ppermute x0 -> x42, starting transfers between devices: none -> 61.8 us  [send(): return lax.ppermute(value, AXES, pairs)]
    dot_general x5, matrix products: 64.6 us -> 6.6 us  [the longest x1 1.65 us: per_device(): lax.dot_general(my_rows, inverse, (((1,), (1,)), ((), ())), precision=HIG...]
    pallas_call x0 -> x9, Pallas kernels: none -> 52.2 us  [the longest x4 34.9 us: make_update(): pl.pallas_call(functools.partial(body, sub), grid_spec=pltpu.PrefetchScal...]
    reshape x1 -> x0, local copies, waits for them, and re-layouts: 36.8 us -> none  [per_device(): jnp.einsum('bq,brc->qrc', routing, update, precision=highest)]
  transfers between devices with their start and end apart: 4 -> 43, of which waited for: 4 -> 19; matrix products, arithmetic and copies ran while one was open for 0% -> 12% of each run, Pallas kernels for 0% -> 10%
where the time goes in v1:
time: 422 us; the launch traced here: 414 us
  waiting for transfers between devices  215 us (51%)
  starting transfers between devices  61.9 us (15%)
  Pallas kernels  52.2 us (12%)
  other arithmetic  38 us (9%)
  local copies, waits for them, and re-layouts  25.7 us (6%)
  between operations  14.5 us (3%)
  matrix products  6.85 us (2%)
    psum x1, waiting for transfers between devices, per_device(): lax.psum(jnp.concatenate([column.reshape(4096, BLK), rhs_rows], axis=0),...  108 us
    ppermute x42, waiting for transfers between devices, send(): return lax.ppermute(value, AXES, pairs)  106 us
    ppermute x42, starting transfers between devices, send(): return lax.ppermute(value, AXES, pairs)  61.8 us
    pallas_call x4, Pallas kernels, make_update(): pl.pallas_call(functools.partial(body, sub), grid_spec=pltpu.PrefetchScal...  34.9 us
    unnamed x43, local copies, waits for them, and re-layouts  18.2 us
    pallas_call x4, Pallas kernels, make_expand(): pl.pallas_call(expand_columns if flow == 'y' else expand_rows, in_specs=[...  16 us
    another operation x3, other arithmetic, per_device(): lower = jnp.tril(lax.linalg.cholesky(pivot_block, symmetrize_input=False))  12.4 us
    another operation x2, other arithmetic, per_device(): lax.linalg.triangular_solve(lower, jnp.eye(BLK, dtype=jnp.float32), left_...  10.5 us
  transfers between devices with their start and end apart: 43, of which 19 were waited for; matrix products, arithmetic and copies ran while one was open for 12% of the time, Pallas kernels for 10%

profile of v1, /device:TPU:97, one launch (start us, length us, event | category | flops | bytes accessed | tf_op | source)
XLA Modules:
  0.0 413.9 jit_solution(16815509275567370584)
XLA Ops:
  10.0 9.3 %update_y.2 = (f32[4,16,32,128]{3,2,1,0:T(8,128)}, f32[4,16,32,128]{3,2,1,0:T(8,128)}, f32[4,16,32,128]{3,2,1,0:T(8,128)}, f32[4,16,32,128]{3,2,1,0:T(8,128)S(1)}) custom-call(s32[1]{0:T(128)} %bitcast.pos, bf16[16,128,1536]{2,1,0:T(8,128)(2,1)S(1)} %bitcast.247, f32[16,16,128,128]{3,2,1,0:T(8,128)} %bitcast.254), custom_call_target="tpu_custom_call" | custom-call | flops 3221225472 | bytes 14680064 | tf_op jit(solution)/shard_map/update_y/pallas_call | solution.py:99
  27.1 8.9 %update_z.2 = (f32[4,16,32,128]{3,2,1,0:T(8,128)}, f32[4,16,32,128]{3,2,1,0:T(8,128)}, f32[4,16,32,128]{3,2,1,0:T(8,128)}, f32[4,16,32,128]{3,2,1,0:T(8,128)S(1)}) custom-call(s32[1]{0:T(128)} %bitcast.2.pos, bf16[16,128,1536]{2,1,0:T(8,128)(2,1)S(1)} %bitcast.248, f32[16,16,128,128]{3,2,1,0:T(8,128)} %bitcast.255), custom_call_target="tpu_custom_call" | custom-call | flops 3221225472 | bytes 14680064 | tf_op jit(solution)/shard_map/update_z/pallas_call | solution.py:99
  43.4 8.8 %update_y.3 = (f32[4,16,32,128]{3,2,1,0:T(8,128)S(1)}, f32[4,16,32,128]{3,2,1,0:T(8,128)}, f32[4,16,32,128]{3,2,1,0:T(8,128)S(1)}, f32[4,16,32,128]{3,2,1,0:T(8,128)S(1)}) custom-call(s32[1]{0:T(128)} %bitcast.pos, bf16[16,128,1536]{2,1,0:T(8,128)(2,1)S(1)} %bitcast.250, f32[16,16,128,128]{3,2,1,0:T(8,128)} %bitcast.257), custom_call_target="tpu_custom_call" | custom-call | flops 3221225472 | bytes 14680064 | tf_op jit(solution)/shard_map/update_y/pallas_call | solution.py:99
  56.7 11.9 %collective-permute-done.1.far = f32[4,16,32,128]{3,2,1,0:T(8,128)} collective-permute-done((f32[4,16,32,128]{3,2,1,0:T(8,128)}, f32[4,16,32,128]{3,2,1,0:T(8,128)}, u32[]{:S(2)}, u32[]{:S(2)}) %collective-permute-start.1) | collective-permute-done | bytes 1048608 | tf_op jit(solution)/shard_map/ppermute | solution.py:41
  75.9 7.8 %update_z.3 = (f32[4,16,32,128]{3,2,1,0:T(8,128)S(1)}, f32[4,16,32,128]{3,2,1,0:T(8,128)S(1)}, f32[4,16,32,128]{3,2,1,0:T(8,128)S(1)}, f32[4,16,32,128]{3,2,1,0:T(8,128)S(1)}) custom-call(s32[1]{0:T(128)} %bitcast.2.pos, bf16[16,128,1536]{2,1,0:T(8,128)(2,1)S(1)} %bitcast.251, f32[16,16,128,128]{3,2,1,0:T(8,128)} %bitcast.258), custom_call_target="tpu_custom_call" | custom-call | flops 3221225472 | bytes 14680064 | tf_op jit(solution)/shard_map/update_z/pallas_call | solution.py:99
  88.9 6.7 %collective-permute-done.21.behind = f32[4,16,32,128]{3,2,1,0:T(8,128)} collective-permute-done((f32[4,16,32,128]{3,2,1,0:T(8,128)}, f32[4,16,32,128]{3,2,1,0:T(8,128)}, u32[]{:S(2)}, u32[]{:S(2)}) %collective-permute-start.21) | collective-permute-done | bytes 1048608 | tf_op jit(solution)/shard_map/ppermute | solution.py:41
  95.7 3.2 expand_y.2
  101.5 5.6 %expand_z.2 = f32[2,4,4,8,32,128]{5,4,3,2,1,0:T(8,128)S(1)} custom-call(s32[6]{0:T(128)S(1)} %stack.41.pos, s32[4,16]{1,0:T(4,128)S(1)} %pad_add_fusion.1.maps, f32[4,16,32,128]{3,2,1,0:T(8,128)S(1)} %copy-done.13, f32[4,16,32,128]{3,2,1,0:T(8,128)} %collective-permute-done.10.behind, f32[4,16,32,128]{3,2,1,0:T(8,128)} %collective-permute-done.11.far, ...), custom_call_target="tpu_custom_call" | custom-call | flops 1048576 | bytes 16777216 | tf_op jit(solution)/shard_map/expand_z/pallas_call | solution.py:155
  108.7 6.8 %collective-permute-done.22.far = f32[4,16,32,128]{3,2,1,0:T(8,128)S(1)} collective-permute-done((f32[4,16,32,128]{3,2,1,0:T(8,128)}, f32[4,16,32,128]{3,2,1,0:T(8,128)S(1)}, u32[]{:S(2)}, u32[]{:S(2)}) %collective-permute-start.22) | collective-permute-done | bytes 1048608 | tf_op jit(solution)/shard_map/ppermute | solution.py:41
  115.5 18.2 %collective-permute-start.3 = (f32[4,4,8,32,128]{4,3,2,1,0:T(8,128)}, f32[4,4,8,32,128]{4,3,2,1,0:T(8,128)}, u32[]{:S(2)}, u32[]{:S(2)}) collective-permute-start(f32[4,4,8,32,128]{4,3,2,1,0:T(8,128)} %slice_bitcast_fusion.3), channel_id=1, source_target_pairs={{0,32},{1,33},{2,34},{3,35},{4,36},{5,37},{6,38},{7,39},{8,40},{9,... | collective-permute-start | bytes 6291464 | tf_op jit(solution)/shard_map/ppermute | solution.py:41
  139.5 4.3 %expand_z.3 = f32[2,4,4,8,32,128]{5,4,3,2,1,0:T(8,128)S(1)} custom-call(s32[6]{0:T(128)S(1)} %stack.41.pos, s32[4,16]{1,0:T(4,128)S(1)} %pad_add_fusion.1.maps, f32[4,16,32,128]{3,2,1,0:T(8,128)S(1)} %get-tuple-element.31.own, f32[4,16,32,128]{3,2,1,0:T(8,128)S(1)} %collective-permute-done.31.behind, f32[4,16,32,128]{3,2,1,0:T(8,128)S(1)} %collective-permute-done.32.far, ...), custom_call_target="tpu_custom_call" | custom-call | flops 1048576 | bytes 16777216 | tf_op jit(solution)/shard_map/expand_z/pallas_call | solution.py:155
  148.2 108.5 %all-reduce.3.cloned.1.call-done = f32[4224,128]{1,0:T(8,128)} async-done(((f32[4224,128]{1,0:T(8,128)}), f32[4224,128]{1,0:T(8,128)}) %all-reduce.3.cloned.1.call-update) | async-done | bytes 2162704 | tf_op jit(solution)/shard_map/psum | solution.py:222
  257.5 11.7 %cholesky.18 = f32[128,128]{1,0:T(8,128)S(1)} custom-call(f32[128,128]{1,0:T(8,128)S(1)} %cholesky.37), custom_call_target="Cholesky" | custom-call | tf_op jit(solution)/shard_map/cholesky | solution.py:252
  270.6 9.8 %custom-call.5 = f32[1,128,128]{1,2,0:T(8,128)S(1)} custom-call(f32[1,128,128]{2,1,0:T(8,128)S(1)} %get-tuple-element.35), custom_call_target="InvertDiagBlocksLowerTriangular" | custom-call | tf_op jit(solution)/shard_map/triangular_solve | solution.py:253
  299.7 4.1 collective-permute-done.4
  303.8 11.1 %collective-permute-done.5 = f32[4,8,32,128]{3,2,1,0:T(8,128)S(1)} collective-permute-done((f32[4,8,32,128]{3,2,1,0:T(8,128)S(1)}, f32[4,8,32,128]{3,2,1,0:T(8,128)S(1)}, u32[]{:S(2)}, u32[]{:S(2)}) %collective-permute-start.5) | collective-permute-done | bytes 524320 | tf_op jit(solution)/shard_map/ppermute | solution.py:41
  319.0 7.3 %collective-permute-done.14 = f32[4,8,32,128]{3,2,1,0:T(8,128)S(1)} collective-permute-done((f32[4,8,32,128]{3,2,1,0:T(8,128)S(1)}, f32[4,8,32,128]{3,2,1,0:T(8,128)S(1)}, u32[]{:S(2)}, u32[]{:S(2)}) %collective-permute-start.14) | collective-permute-done | bytes 524320 | tf_op jit(solution)/shard_map/ppermute | solution.py:41
  326.3 11.1 %collective-permute-done.15 = f32[4,8,32,128]{3,2,1,0:T(8,128)S(1)} collective-permute-done((f32[4,8,32,128]{3,2,1,0:T(8,128)S(1)}, f32[4,8,32,128]{3,2,1,0:T(8,128)S(1)}, u32[]{:S(2)}, u32[]{:S(2)}) %collective-permute-start.15) | collective-permute-done | bytes 524320 | tf_op jit(solution)/shard_map/ppermute | solution.py:41
  341.2 7.5 %collective-permute-done.25 = f32[4,8,32,128]{3,2,1,0:T(8,128)S(1)} collective-permute-done((f32[4,8,32,128]{3,2,1,0:T(8,128)S(1)}, f32[4,8,32,128]{3,2,1,0:T(8,128)S(1)}, u32[]{:S(2)}, u32[]{:S(2)}) %collective-permute-start.25) | collective-permute-done | bytes 524320 | tf_op jit(solution)/shard_map/ppermute | solution.py:41
  348.8 11.0 %collective-permute-done.26 = f32[4,8,32,128]{3,2,1,0:T(8,128)S(1)} collective-permute-done((f32[4,8,32,128]{3,2,1,0:T(8,128)S(1)}, f32[4,8,32,128]{3,2,1,0:T(8,128)S(1)}, u32[]{:S(2)}, u32[]{:S(2)}) %collective-permute-start.26) | collective-permute-done | bytes 524320 | tf_op jit(solution)/shard_map/ppermute | solution.py:41
  364.9 6.4 %collective-permute-done.35 = f32[4,8,32,128]{3,2,1,0:T(8,128)S(1)} collective-permute-done((f32[4,8,32,128]{3,2,1,0:T(8,128)S(1)}, f32[4,8,32,128]{3,2,1,0:T(8,128)S(1)}, u32[]{:S(2)}, u32[]{:S(2)}) %collective-permute-start.35) | collective-permute-done | bytes 524320 | tf_op jit(solution)/shard_map/ppermute | solution.py:41
  372.0 10.2 %collective-permute-done.36 = f32[4,8,32,128]{3,2,1,0:T(8,128)S(1)} collective-permute-done((f32[4,8,32,128]{3,2,1,0:T(8,128)S(1)}, f32[4,8,32,128]{3,2,1,0:T(8,128)S(1)}, u32[]{:S(2)}, u32[]{:S(2)}) %collective-permute-start.36) | collective-permute-done | bytes 524320 | tf_op jit(solution)/shard_map/ppermute | solution.py:41
  392.3 3.0 collective-permute-done.39
  402.0 3.6 collective-permute-done.30
  (155 shorter events, 102.5 us)
Async XLA Ops:
  7.2 249.5 %all-reduce.3.cloned.1.call-start = ((), (), s32[]{:S(2)}) async-start(), calls=%async_computation | async-start | bytes 4325376 | tf_op jit(solution)/shard_map/psum | solution.py:222
  19.4 35.8 %collective-permute-start = (f32[4,16,32,128]{3,2,1,0:T(8,128)}, f32[4,16,32,128]{3,2,1,0:T(8,128)S(1)}, u32[]{:S(2)}, u32[]{:S(2)}) collective-permute-start(f32[4,16,32,128]{3,2,1,0:T(8,128)} %get-tuple-element.20), channel_id=1, source_target_pairs={{0,8},{1,9},{2,10},{3,11},{4,12},{5,13},{6,14},{7,15},{8,16},{9,17... | collective-permute-start | bytes 3145736 | tf_op jit(solution)/shard_map/ppermute | solution.py:41
  20.7 48.0 %collective-permute-start.1 = (f32[4,16,32,128]{3,2,1,0:T(8,128)}, f32[4,16,32,128]{3,2,1,0:T(8,128)}, u32[]{:S(2)}, u32[]{:S(2)}) collective-permute-start(f32[4,16,32,128]{3,2,1,0:T(8,128)} %get-tuple-element.21), channel_id=1, source_target_pairs={{0,16},{1,17},{2,18},{3,19},{4,20},{5,21},{6,22},{7,23},{8,24},{9,... | collective-permute-start | bytes 3145736 | tf_op jit(solution)/shard_map/ppermute | solution.py:41
  23.3 46.9 %collective-permute-start.2 = (f32[4,16,32,128]{3,2,1,0:T(8,128)}, f32[4,16,32,128]{3,2,1,0:T(8,128)}, u32[]{:S(2)}, u32[]{:S(2)}) collective-permute-start(f32[4,16,32,128]{3,2,1,0:T(8,128)} %get-tuple-element.22), channel_id=1, source_target_pairs={{0,24},{1,25},{2,26},{3,27},{4,28},{5,29},{6,30},{7,31},{8,0},{9,1... | collective-permute-start | bytes 3145736 | tf_op jit(solution)/shard_map/ppermute | solution.py:41
  37.1 46.6 %collective-permute-start.11 = (f32[4,16,32,128]{3,2,1,0:T(8,128)}, f32[4,16,32,128]{3,2,1,0:T(8,128)}, u32[]{:S(2)}, u32[]{:S(2)}) collective-permute-start(f32[4,16,32,128]{3,2,1,0:T(8,128)} %get-tuple-element.25), channel_id=1, source_target_pairs={{0,64},{1,65},{2,66},{3,67},{4,68},{5,69},{6,70},{7,71},{8,72},{9,... | collective-permute-start | bytes 3145736 | tf_op jit(solution)/shard_map/ppermute | solution.py:41
  70.2 45.3 %collective-permute-start.22 = (f32[4,16,32,128]{3,2,1,0:T(8,128)}, f32[4,16,32,128]{3,2,1,0:T(8,128)S(1)}, u32[]{:S(2)}, u32[]{:S(2)}) collective-permute-start(f32[4,16,32,128]{3,2,1,0:T(8,128)} %copy-done.17), channel_id=1, source_target_pairs={{0,16},{1,17},{2,18},{3,19},{4,20},{5,21},{6,22},{7,23},{8,24},{9,... | collective-permute-start | bytes 3145736 | tf_op jit(solution)/shard_map/ppermute | solution.py:41
  70.7 63.0 %collective-permute-start.23 = (f32[4,16,32,128]{3,2,1,0:T(8,128)}, f32[4,16,32,128]{3,2,1,0:T(8,128)S(1)}, u32[]{:S(2)}, u32[]{:S(2)}) collective-permute-start(f32[4,16,32,128]{3,2,1,0:T(8,128)} %copy-done.16), channel_id=1, source_target_pairs={{0,24},{1,25},{2,26},{3,27},{4,28},{5,29},{6,30},{7,31},{8,0},{9,1... | collective-permute-start | bytes 3145736 | tf_op jit(solution)/shard_map/ppermute | solution.py:41
  83.7 54.7 %collective-permute-start.31 = (f32[4,16,32,128]{3,2,1,0:T(8,128)S(1)}, f32[4,16,32,128]{3,2,1,0:T(8,128)S(1)}, u32[]{:S(2)}, u32[]{:S(2)}) collective-permute-start(f32[4,16,32,128]{3,2,1,0:T(8,128)S(1)} %get-tuple-element.32), channel_id=1, source_target_pairs={{0,1},{1,64},{2,3},{3,66},{4,5},{5,68},{6,7},{7,70},{8,9},{9,72},{... | collective-permute-start | bytes 3145736 | tf_op jit(solution)/shard_map/ppermute | solution.py:41
  86.9 52.5 %collective-permute-start.32 = (f32[4,16,32,128]{3,2,1,0:T(8,128)S(1)}, f32[4,16,32,128]{3,2,1,0:T(8,128)S(1)}, u32[]{:S(2)}, u32[]{:S(2)}) collective-permute-start(f32[4,16,32,128]{3,2,1,0:T(8,128)S(1)} %get-tuple-element.33), channel_id=1, source_target_pairs={{0,64},{1,65},{2,66},{3,67},{4,68},{5,69},{6,70},{7,71},{8,72},{9,... | collective-permute-start | bytes 3145736 | tf_op jit(solution)/shard_map/ppermute | solution.py:41
  95.6 43.9 %collective-permute-start.33 = (f32[4,16,32,128]{3,2,1,0:T(8,128)S(1)}, f32[4,16,32,128]{3,2,1,0:T(8,128)S(1)}, u32[]{:S(2)}, u32[]{:S(2)}) collective-permute-start(f32[4,16,32,128]{3,2,1,0:T(8,128)S(1)} %get-tuple-element.34), channel_id=1, source_target_pairs={{0,65},{1,0},{2,67},{3,2},{4,69},{5,4},{6,71},{7,6},{8,73},{9,8},{... | collective-permute-start | bytes 3145736 | tf_op jit(solution)/shard_map/ppermute | solution.py:41
  115.5 170.3 %collective-permute-start.3 = (f32[4,4,8,32,128]{4,3,2,1,0:T(8,128)}, f32[4,4,8,32,128]{4,3,2,1,0:T(8,128)}, u32[]{:S(2)}, u32[]{:S(2)}) collective-permute-start(f32[4,4,8,32,128]{4,3,2,1,0:T(8,128)} %slice_bitcast_fusion.3), channel_id=1, source_target_pairs={{0,32},{1,33},{2,34},{3,35},{4,36},{5,37},{6,38},{7,39},{8,40},{9,... | collective-permute-start | bytes 6291464 | tf_op jit(solution)/shard_map/ppermute | solution.py:41
  133.7 156.6 %collective-permute-start.13 = (f32[4,4,8,32,128]{4,3,2,1,0:T(8,128)}, f32[4,4,8,32,128]{4,3,2,1,0:T(8,128)}, u32[]{:S(2)}, u32[]{:S(2)}) collective-permute-start(f32[4,4,8,32,128]{4,3,2,1,0:T(8,128)} %slice_bitcast_fusion.2), channel_id=1, source_target_pairs={{0,32},{1,33},{2,34},{3,35},{4,36},{5,37},{6,38},{7,39},{8,40},{9,... | collective-permute-start | bytes 6291464 | tf_op jit(solution)/shard_map/ppermute | solution.py:41
  138.4 155.6 %collective-permute-start.24 = (f32[4,4,8,32,128]{4,3,2,1,0:T(8,128)}, f32[4,4,8,32,128]{4,3,2,1,0:T(8,128)}, u32[]{:S(2)}, u32[]{:S(2)}) collective-permute-start(f32[4,4,8,32,128]{4,3,2,1,0:T(8,128)} %slice_bitcast_fusion.1), channel_id=1, source_target_pairs={{0,32},{1,33},{2,34},{3,35},{4,36},{5,37},{6,38},{7,39},{8,40},{9,... | collective-permute-start | bytes 6291464 | tf_op jit(solution)/shard_map/ppermute | solution.py:41
  147.3 149.7 %collective-permute-start.34 = (f32[4,4,8,32,128]{4,3,2,1,0:T(8,128)}, f32[4,4,8,32,128]{4,3,2,1,0:T(8,128)}, u32[]{:S(2)}, u32[]{:S(2)}) collective-permute-start(f32[4,4,8,32,128]{4,3,2,1,0:T(8,128)} %slice_bitcast_fusion), channel_id=1, source_target_pairs={{0,32},{1,33},{2,34},{3,35},{4,36},{5,37},{6,38},{7,39},{8,40},{9,... | collective-permute-start | bytes 6291464 | tf_op jit(solution)/shard_map/ppermute | solution.py:41
  296.9 40.4 %collective-permute-start.15 = (f32[4,8,32,128]{3,2,1,0:T(8,128)S(1)}, f32[4,8,32,128]{3,2,1,0:T(8,128)S(1)}, u32[]{:S(2)}, u32[]{:S(2)}) collective-permute-start(f32[4,8,32,128]{3,2,1,0:T(8,128)S(1)} %get-tuple-element.42), channel_id=1, source_target_pairs={{0,2},{1,3},{2,4},{3,5},{4,6},{5,7},{6,0},{7,1},{8,10},{9,11},{10,... | collective-permute-start | bytes 1572872 | tf_op jit(solution)/shard_map/ppermute | solution.py:41
  303.8 36.1 %collective-permute-start.16 = (f32[4,8,32,128]{3,2,1,0:T(8,128)S(1)}, f32[4,8,32,128]{3,2,1,0:T(8,128)S(1)}, u32[]{:S(2)}, u32[]{:S(2)}) collective-permute-start(f32[4,8,32,128]{3,2,1,0:T(8,128)S(1)} %get-tuple-element.41), channel_id=1, source_target_pairs={{0,6},{1,7},{2,0},{3,1},{4,2},{5,3},{6,4},{7,5},{8,14},{9,15},{10,... | collective-permute-start | bytes 1572872 | tf_op jit(solution)/shard_map/ppermute | solution.py:41
  314.9 33.9 %collective-permute-start.25 = (f32[4,8,32,128]{3,2,1,0:T(8,128)S(1)}, f32[4,8,32,128]{3,2,1,0:T(8,128)S(1)}, u32[]{:S(2)}, u32[]{:S(2)}) collective-permute-start(f32[4,8,32,128]{3,2,1,0:T(8,128)S(1)} %get-tuple-element.43), channel_id=1, source_target_pairs={{0,4},{1,5},{2,6},{3,7},{4,0},{5,1},{6,2},{7,3},{8,12},{9,13},{10,... | collective-permute-start | bytes 1572872 | tf_op jit(solution)/shard_map/ppermute | solution.py:41
  317.4 42.4 %collective-permute-start.26 = (f32[4,8,32,128]{3,2,1,0:T(8,128)S(1)}, f32[4,8,32,128]{3,2,1,0:T(8,128)S(1)}, u32[]{:S(2)}, u32[]{:S(2)}) collective-permute-start(f32[4,8,32,128]{3,2,1,0:T(8,128)S(1)} %get-tuple-element.45), channel_id=1, source_target_pairs={{0,2},{1,3},{2,4},{3,5},{4,6},{5,7},{6,0},{7,1},{8,10},{9,11},{10,... | collective-permute-start | bytes 1572872 | tf_op jit(solution)/shard_map/ppermute | solution.py:41
  326.3 35.5 %collective-permute-start.27 = (f32[4,8,32,128]{3,2,1,0:T(8,128)S(1)}, f32[4,8,32,128]{3,2,1,0:T(8,128)S(1)}, u32[]{:S(2)}, u32[]{:S(2)}) collective-permute-start(f32[4,8,32,128]{3,2,1,0:T(8,128)S(1)} %get-tuple-element.44), channel_id=1, source_target_pairs={{0,6},{1,7},{2,0},{3,1},{4,2},{5,3},{6,4},{7,5},{8,14},{9,15},{10,... | collective-permute-start | bytes 1572872 | tf_op jit(solution)/shard_map/ppermute | solution.py:41
  337.3 34.0 %collective-permute-start.35 = (f32[4,8,32,128]{3,2,1,0:T(8,128)S(1)}, f32[4,8,32,128]{3,2,1,0:T(8,128)S(1)}, u32[]{:S(2)}, u32[]{:S(2)}) collective-permute-start(f32[4,8,32,128]{3,2,1,0:T(8,128)S(1)} %get-tuple-element.46), channel_id=1, source_target_pairs={{0,4},{1,5},{2,6},{3,7},{4,0},{5,1},{6,2},{7,3},{8,12},{9,13},{10,... | collective-permute-start | bytes 1572872 | tf_op jit(solution)/shard_map/ppermute | solution.py:41
  339.9 42.4 %collective-permute-start.36 = (f32[4,8,32,128]{3,2,1,0:T(8,128)S(1)}, f32[4,8,32,128]{3,2,1,0:T(8,128)S(1)}, u32[]{:S(2)}, u32[]{:S(2)}) collective-permute-start(f32[4,8,32,128]{3,2,1,0:T(8,128)S(1)} %get-tuple-element.48), channel_id=1, source_target_pairs={{0,2},{1,3},{2,4},{3,5},{4,6},{5,7},{6,0},{7,1},{8,10},{9,11},{10,... | collective-permute-start | bytes 1572872 | tf_op jit(solution)/shard_map/ppermute | solution.py:41
  348.8 34.5 %collective-permute-start.37 = (f32[4,8,32,128]{3,2,1,0:T(8,128)S(1)}, f32[4,8,32,128]{3,2,1,0:T(8,128)S(1)}, u32[]{:S(2)}, u32[]{:S(2)}) collective-permute-start(f32[4,8,32,128]{3,2,1,0:T(8,128)S(1)} %get-tuple-element.47), channel_id=1, source_target_pairs={{0,6},{1,7},{2,0},{3,1},{4,2},{5,3},{6,4},{7,5},{8,14},{9,15},{10,... | collective-permute-start | bytes 1572872 | tf_op jit(solution)/shard_map/ppermute | solution.py:41
  359.8 38.5 %collective-permute-start.7 = (f32[8,32,128]{2,1,0:T(8,128)S(1)}, f32[8,32,128]{2,1,0:T(8,128)S(1)}, u32[]{:S(2)}, u32[]{:S(2)}) collective-permute-start(f32[8,32,128]{2,1,0:T(8,128)S(1)} %get-tuple-element.49), channel_id=1, source_target_pairs={{0,64},{1,65},{2,66},{3,67},{4,68},{5,69},{6,70},{7,71},{8,72},{9,... | collective-permute-start | bytes 393224 | tf_op jit(solution)/shard_map/ppermute | solution.py:41
  361.8 36.6 %collective-permute-start.8 = (f32[8,32,128]{2,1,0:T(8,128)S(1)}, f32[8,32,128]{2,1,0:T(8,128)S(1)}, u32[]{:S(2)}, u32[]{:S(2)}) collective-permute-start(f32[8,32,128]{2,1,0:T(8,128)S(1)} %get-tuple-element.51), channel_id=1, source_target_pairs={{0,1},{1,64},{2,3},{3,66},{4,5},{5,68},{6,7},{7,70},{8,9},{9,72},{... | collective-permute-start | bytes 393224 | tf_op jit(solution)/shard_map/ppermute | solution.py:41
  (40 other events, 413.7 us)
Sparse Core Ops, SparseCore 0:
  70.3 186.3 all-reduce.2

commit v2 on v0

v2 whole, which is shorter than its diff:
```python
import functools

import jax
import jax.numpy as jnp
from jax import lax
from jax.experimental import pallas as pl
from jax.experimental.pallas import tpu as pltpu
from jax.sharding import PartitionSpec as P

BLK = 128
ORDER = (2, 1, 3, 0)
AXES = ("leaf", "col")
ROWS = {"x": (0, 48), "z": (48, 48), "y": (96, 32)}
UPDATE_VMEM = 52 << 20
EXPAND_VMEM = 56 << 20
HIGHEST = lax.Precision.HIGHEST


def links(move):
    pairs = []
    for source in range(128):
        zl, x, y = source % 2, source // 2 % 4, source // 8 % 4
        core, zh = source // 32 % 2, source // 64
        c, v, u, w = move(core, y, x, 2 * zh + zl)
        v, u, w = v % 4, u % 4, w % 4
        pairs.append((source, ((w // 2 * 2 + c) * 4 + v) * 8 + u * 2 + w % 2))
    return pairs


def along(axis, hop):
    if axis == "y":
        return links(lambda c, y, x, z: (c, y + hop, x, z))
    if axis == "x":
        return links(lambda c, y, x, z: (c, y, x + hop, z))
    return links(lambda c, y, x, z: (c, y, x, z + hop))


SIBLING = links(lambda c, y, x, z: (1 - c, y, x, z))
SWAP = links(lambda c, y, x, z: (z % 2, y, x, z // 2 * 2 + c))


PARENT = [(32 * leaf, 40 * leaf) for leaf in range(4)]
RANGE = links(lambda c, y, x, z: (y % 2, z // 2 * 2 + c, x, y // 2 * 2 + z % 2))
TURN = links(lambda c, y, x, z: (x % 2, y, z // 2 * 2 + c, x // 2 * 2 + z % 2))


def send(value, pairs):
    return lax.ppermute(value, AXES, pairs)


def product(lhs, rhs):
    return lax.dot_general(lhs, rhs, (((1,), (1,)), ((), ())), preferred_element_type=jnp.float32)


def update(pos, panel, front, pivot_front, parent, earlier, *refs):
    step = pl.program_id(0)
    pivots = panel.shape[2]
    by_column, scratch = refs[8], refs[9]
    lhs = panel[...].reshape(16 * BLK, pivots)
    rhs = panel[pl.ds(2 * step, 2)].reshape(2 * BLK, pivots)
    scratch[...] = product(lhs, rhs).reshape(16, BLK, 2 * BLK)
    for flow, me, outs in (("x", pos[1], refs[0:4]), ("z", pos[2], refs[4:8])):
        first, rows = ROWS[flow]
        for slot, out in zip(ORDER, outs):
            top = 4 * ((me + slot) % 4)
            for half in range(2):
                lanes = slice(half * BLK, (half + 1) * BLK)
                out[:, half] = (
                    front[half, pl.ds(top, 4), first : first + rows]
                    - scratch[pl.ds(top, 4), first : first + rows, lanes]
                )
    first, rows = ROWS["y"]
    for half in range(2):
        lanes = slice(half * BLK, (half + 1) * BLK)
        by_column[step // 2, pl.ds(32 * (step % 2) + 16 * half, 16)] = (
            front[half, :, first : first + rows] - scratch[:, first : first + rows, lanes]
        )

    @pl.when(step == 0)
    def _():
        column = pivot_front[...] - scratch[:, :, 0:BLK]
        corner = jnp.where(pos[4] == 1, column[0], 0.0) + jnp.where(pos[5] == 1, parent[...], 0.0)
        for n in range(4):
            by_column[n, 64:80] = column[4 * n : 4 * n + 4].reshape(16, rows, BLK)
            by_column[n, 80:84] = corner.reshape(4, rows, BLK)


def make_updates(pos, panel, front, parent_front, parent_column):
    pivots = panel.shape[2]
    rows_x, rows_z, rows_y = ROWS["x"][1], ROWS["z"][1], ROWS["y"][1]
    outs = pl.pallas_call(
        update,
        grid_spec=pltpu.PrefetchScalarGridSpec(
            num_scalar_prefetch=1,
            grid=(8,),
            in_specs=[
                pl.BlockSpec((16, BLK, pivots), lambda t, pos: (0, 0, 0)),
                pl.BlockSpec((2, 16, BLK, BLK), lambda t, pos: (t, 0, 0, 0)),
                pl.BlockSpec((pl.squeezed, 16, BLK, BLK), lambda t, pos: (0, 0, 0, 0)),
                pl.BlockSpec((BLK, BLK), lambda t, pos: (0, 0)),
                pl.BlockSpec(memory_space=pl.ANY),
            ],
            out_specs=[pl.BlockSpec((4, 2, rows_x, BLK), lambda t, pos: (0, t, 0, 0))] * 4
            + [pl.BlockSpec((4, 2, rows_z, BLK), lambda t, pos: (0, t, 0, 0))] * 4
            + [pl.BlockSpec((4, 84, rows_y, BLK), lambda t, pos: (0, 0, 0, 0))],
            scratch_shapes=[pltpu.VMEM((16, BLK, 2 * BLK), jnp.float32)],
        ),
        out_shape=[jax.ShapeDtypeStruct((4, 16, rows_x, BLK), jnp.float32)] * 4
        + [jax.ShapeDtypeStruct((4, 16, rows_z, BLK), jnp.float32)] * 4
        + [jax.ShapeDtypeStruct((4, 84, rows_y, BLK), jnp.float32)],
        compiler_params=pltpu.CompilerParams(vmem_limit_bytes=UPDATE_VMEM),
        cost_estimate=pl.CostEstimate(
            flops=2 * 2048 * 2048 * pivots, bytes_accessed=40 << 20, transcendentals=0
        ),
        name="update",
    )(pos, panel, front, front, parent_front, parent_column)
    return {
        "x": dict(zip(ORDER, [v.reshape(64, rows_x, BLK) for v in outs[0:4]])),
        "z": dict(zip(ORDER, [v.reshape(64, rows_z, BLK) for v in outs[4:8]])),
        "y": outs[8],
    }


def expand(pos, places, maps_y, maps_x, maps_z, parent, chunks_y, *refs):
    y, x, z, core = pos[0], pos[1], pos[2], pos[3]
    keep, away, out_x, out_z = refs[8:12]
    keep[0:128] = jnp.zeros_like(keep[0:128])
    away[0:128] = jnp.zeros_like(away[0:128])
    out_x[...] = jnp.zeros_like(out_x)
    out_z[...] = jnp.zeros_like(out_z)
    for s in range(4):

        def column(k, carry):
            q = maps_y[s, 4 * y + k] - 8 * y
            to = (q // 2 + 4 - x) % 4
            for zh in range(2):
                j = (zh * 2 + q % 2 + 4 - z) % 4
                at = 32 * j + 8 * to
                for n in range(4):
                    for out, side in ((keep, core), (away, 1 - core)):
                        block = 8 * zh + 4 * side + n
                        p = maps_y[s, block] - 8 * (2 * zh + side)
                        out[at + p] += chunks_y[s, 16 * k + block]
            return carry

        lax.fori_loop(0, 4, column, 0)
    has = [places[s, 0] == 0 for s in range(4)]
    for out, side in ((keep, core), (away, 1 - core)):

        def rows(n, carry):
            p = 4 * side + n
            down = [places[s, 8 * y + p] - 4 * y for s in range(4)]
            for i in range(4):
                total = parent[4 * p + i]
                for s in range(4):
                    there = has[s] & (down[s] >= 0)
                    block = chunks_y[s, 64 + 4 * jnp.maximum(down[s], 0) + i]
                    total += jnp.where(there, block, 0.0)
                out[128 + 4 * n + i] = total
            return carry

        lax.fori_loop(0, 4, rows, 0)
    for i in range(4):
        total = chunks_y[0, 80 + i] + chunks_y[1, 80 + i] + chunks_y[2, 80 + i] + chunks_y[3, 80 + i]
        keep[144 + i] = total
        away[144 + i] = total

    flows = (("x", maps_x, x, refs[0:4], out_x), ("z", maps_z, z, refs[4:8], out_z))
    for flow, maps, me, chunks, out in flows:
        for s, chunk in enumerate(chunks):

            def row(k, carry):
                p = maps[s, 4 * me + k] - 8 * me
                for block in range(16):
                    q = maps[s, block] - 8 * (block // 4)
                    if flow == "x":
                        j = block // 4
                        to = q // 4 * 2 + q % 2
                        side = q // 2 % 2
                    else:
                        j = (q // 2 + 4 - x) % 4
                        to = (block // 4 + 4 - y) % 4
                        side = q % 2
                    kept = jnp.where(core == side, 1, 0)
                    out[kept, 32 * j + 8 * to + p] += chunk[16 * k + block]
                return carry

            lax.fori_loop(0, 4, row, 0)


def make_expand(pos, places, maps, parent, chunks):
    vmem = pl.BlockSpec(memory_space=pltpu.VMEM)
    smem = pl.BlockSpec(memory_space=pltpu.SMEM)
    return pl.pallas_call(
        expand,
        in_specs=[smem] * 5 + [vmem] * 10,
        out_specs=[vmem] * 4,
        out_shape=[jax.ShapeDtypeStruct((148, ROWS["y"][1], BLK), jnp.float32)] * 2
        + [jax.ShapeDtypeStruct((2, 128, ROWS[flow][1], BLK), jnp.float32) for flow in "xz"],
        compiler_params=pltpu.CompilerParams(vmem_limit_bytes=EXPAND_VMEM),
        cost_estimate=pl.CostEstimate(flops=8 << 20, bytes_accessed=36 << 20, transcendentals=0),
        name="expand",
    )(pos, places, maps["y"], maps["x"], maps["z"], parent, *chunks)


def arrivals(slots, axis):
    return (
        send(slots[1], along(axis, 1)),
        send(slots[2], along(axis, 2)),
        send(slots[3], along(axis, -1)),
    )


def trade(value, groups):
    return lax.all_to_all(value, "col", 0, 0, axis_index_groups=groups, tiled=True)


Y_GROUPS = [[8 * k + n for k in range(4)] for n in range(8)]


def per_device(child_panels, child_fronts, parent_front, block_maps, right_sides):
    leaf, col = lax.axis_index("leaf"), lax.axis_index("col")
    core, y, x = leaf % 2, col // 8, col // 2 % 4
    z = leaf // 2 * 2 + col % 2
    panel = child_panels.reshape(16, BLK, child_panels.shape[3])
    front = child_fronts.reshape(16, 16, BLK, BLK)
    flat_maps = block_maps.reshape(128, 16)

    def map_at(core, y, x, z):
        index = ((z // 2 * 2 + core) * 4 + y) * 8 + x * 2 + z % 2
        return lax.dynamic_index_in_dim(flat_maps, index, 0, keepdims=False)

    def places_of(maps):
        hit = maps[:, :, None] == jnp.arange(32, dtype=jnp.int32)[None, None, :]
        rank = jnp.arange(1, 17, dtype=jnp.int32)[None, :, None]
        return jnp.sum(jnp.where(hit, rank, 0), axis=1).astype(jnp.int32) - 1

    my_map = map_at(core, y, x, z)
    at_corner = (leaf == 0) & (col == 0)
    pos = jnp.stack([y, x, z, core, my_map[0] == 0, at_corner]).astype(jnp.int32)
    maps = {
        "y": jnp.stack([map_at(core, d, x, z) for d in range(4)]),
        "x": jnp.stack([map_at(core, y, (x + d) % 4, z) for d in (0, 3, 2, 1)]),
        "z": jnp.stack([map_at(core, y, x, (z + d) % 4) for d in (0, 3, 2, 1)]),
    }
    places = places_of(maps["y"])
    parent_column = send(parent_front.reshape(32, 32, BLK), PARENT)

    slots = make_updates(pos, panel, front, parent_front, parent_column)
    chunks = [trade(slots["y"], Y_GROUPS)]
    for flow in "xz":
        chunks += [slots[flow][0], *arrivals(slots[flow], flow)]
    keep, away, dense_x, dense_z = make_expand(pos, places, maps, parent_column, chunks)
    halves_y = (keep + send(away, SIBLING)).reshape(148 * 32, BLK)
    halves_x = (dense_x[1] + send(dense_x[0], SIBLING)).reshape(4, 32 * 48, BLK)
    halves_z = (dense_z[1] + send(dense_z[0], SIBLING)).reshape(4, 32 * 48, BLK)

    rhs_mine = jnp.where((leaf == 0) & (col % 2 == 0), right_sides[0:BLK], 0.0)
    extra = jnp.concatenate([halves_y[128 * 32 :], rhs_mine])
    quarter = 32 * 32
    slots_y = [
        jnp.concatenate([halves_y[j * quarter : (j + 1) * quarter], extra]) for j in range(4)
    ]
    sum_x = jnp.sum(trade(halves_x, Y_GROUPS), axis=0)
    sum_y = slots_y[0] + sum(arrivals(slots_y, "z"))
    sum_z = halves_z[0] + sum(arrivals(halves_z, "x"))
    sum_x, sum_y, sum_z = lax.optimization_barrier((sum_x, sum_y, sum_z))

    extra = sum_y[quarter:]
    rhs_rows = extra[20 * 32 :]
    slots_y = [jnp.concatenate([sum_y[k * 256 : (k + 1) * 256], extra[0 : 20 * 32]]) for k in range(4)]
    slots_x = [lax.dynamic_slice_in_dim(sum_x, ((z + k) % 4) * 384, 384) for k in range(4)]
    slots_z = [sum_z[k * 384 : (k + 1) * 384] for k in range(4)]
    sum_y = slots_y[0] + sum(arrivals(slots_y, "x"))
    corner = sum_y[256 + 512 :]
    sum_x = slots_x[0] + sum(arrivals(slots_x, "z"))
    sum_z = slots_z[0] + sum(arrivals(slots_z, "y"))
    corner, sum_x, sum_y, sum_z = lax.optimization_barrier((corner, sum_x, sum_y, sum_z))
    strip_x = send(sum_x, TURN).reshape(8, 48, BLK)
    strip_z = send(sum_z, SWAP).reshape(8, 48, BLK)
    strip_y = sum_y[0:256].reshape(8, 32, BLK)
    assembled = jnp.concatenate([strip_x, strip_z, strip_y], axis=1).reshape(1024, BLK)

    mine = jnp.concatenate([sum_y[256 : 256 + 512], rhs_rows])
    other = send(mine, SIBLING)
    low, high = jnp.where(core == 0, mine, other), jnp.where(core == 0, other, mine)
    in_range = jnp.concatenate([low[0:512], high[0:512]])
    rhs_rows = low[512:]
    col_rows = lax.dynamic_index_in_dim(
        in_range.reshape(8, BLK, BLK), col % 8, 0, keepdims=False
    )
    my_rows = send(in_range, RANGE)

    lower = jnp.tril(lax.linalg.cholesky(corner, symmetrize_input=False))
    inverse = lax.linalg.triangular_solve(
        lower, jnp.eye(BLK, dtype=jnp.float32), left_side=True, lower=True
    )
    row_global = (leaf * 1024 + jnp.arange(1024, dtype=jnp.int32))[:, None]
    solved = lax.dot_general(my_rows, inverse, (((1,), (1,)), ((), ())), precision=HIGHEST)
    own_panel = lax.dot_general(col_rows, inverse, (((1,), (1,)), ((), ())), precision=HIGHEST)
    whitened = jnp.dot(inverse, rhs_rows, precision=HIGHEST)
    schur = lax.dot_general(solved, own_panel, (((1,), (1,)), ((), ())), precision=HIGHEST)
    below = row_global >= BLK
    top = jnp.where(leaf == 0, jnp.pad(lower, ((0, 1024 - BLK), (0, 0))), 0.0)
    pivot_part = jnp.where(below, solved, top)
    trailing = jnp.where(below, parent_front - schur + assembled, 0.0)
    factor = jnp.where(col == 0, pivot_part, trailing)
    condensed = jnp.where(
        below, right_sides - jnp.dot(solved, whitened, precision=HIGHEST), 0.0
    )
    return factor, whitened, condensed


def solution(mesh):
    in_specs = (
        P("leaf", "col", None, None),
        P("leaf", "col", None, None, None),
        P("leaf", "col"),
        P(),
        P("leaf", None),
    )
    out_specs = (P("leaf", "col"), P(), P("leaf", None))
    return jax.shard_map(
        per_device, mesh=mesh, in_specs=in_specs, out_specs=out_specs, check_vma=False
    )
```

time: 1230 us -> 342 us (0.28)
  waiting for transfers between devices: 972 us -> 118 us
  starting transfers between devices: 8.4 us -> 106 us
  local copies, waits for them, and re-layouts: 109 us -> 15.7 us
  matrix products: 67.8 us -> 4.07 us
  Pallas kernels: 0 us -> 45.9 us
  blocking collectives: 25.5 us -> 0 us
  other arithmetic: 25.3 us -> 47.7 us
  between operations: 13.9 us -> 1.57 us
    all_to_all x1 -> x2, waiting for transfers between devices: 541 us -> 0.01 us  [trade(): lax.all_to_all(value, 'col', 0, 0, axis_index_groups=groups, tiled=True)]
    psum x2 -> x0, waiting for transfers between devices: 317 us -> none  [from_root(): return lax.psum(jnp.where(mine, value, jnp.zeros_like(value)), axis)]
    ppermute x0 -> x29, waiting for transfers between devices: none -> 118 us  [send(): return lax.ppermute(value, AXES, pairs)]
    reduce_scatter x1 -> x0, waiting for transfers between devices: 114 us -> none  [per_device(): assembled = lax.psum_scatter(whole, 'leaf', scatter_dimension=0, tiled=True)]
    ppermute x0 -> x29, starting transfers between devices: none -> 96.6 us  [send(): return lax.ppermute(value, AXES, pairs)]
    dot_general x5, matrix products: 64.6 us -> 3.82 us  [the longest x1 1.41 us: per_device(): lax.dot_general(solved, own_panel, (((1,), (1,)), ((), ())), precision=HI...]
    pallas_call x0 -> x2, Pallas kernels: none -> 45.9 us  [the longest x1 24.3 us: make_updates(): pl.pallas_call(update, grid_spec=pltpu.PrefetchScalarGridSpec(num_scalar_...]
    reshape x1 -> x0, local copies, waits for them, and re-layouts: 36.8 us -> none  [per_device(): jnp.einsum('bq,brc->qrc', routing, update, precision=highest)]
  transfers between devices with their start and end apart: 4 -> 31, of which waited for: 4 -> 11; matrix products, arithmetic and copies ran while one was open for 0% -> 13% of each run, Pallas kernels for 0% -> 0%
where the time goes in v2:
time: 342 us; the launch traced here: 340 us
  waiting for transfers between devices  118 us (35%)
  starting transfers between devices  106 us (31%)
  other arithmetic  47.7 us (14%)
  Pallas kernels  45.9 us (13%)
  local copies, waits for them, and re-layouts  15.7 us (5%)
  matrix products  4.07 us (1%)
    ppermute x29, waiting for transfers between devices, send(): return lax.ppermute(value, AXES, pairs)  118 us
    ppermute x29, starting transfers between devices, send(): return lax.ppermute(value, AXES, pairs)  96.6 us
    pallas_call x1, Pallas kernels, make_updates(): pl.pallas_call(update, grid_spec=pltpu.PrefetchScalarGridSpec(num_scalar_...  24.3 us
    pallas_call x1, Pallas kernels, make_expand(): pl.pallas_call(expand, in_specs=[smem] * 5 + [vmem] * 10, out_specs=[vmem...  21.6 us
    another operation x3, other arithmetic, per_device(): lower = jnp.tril(lax.linalg.cholesky(corner, symmetrize_input=False))  12.4 us
    another operation x2, other arithmetic, per_device(): lax.linalg.triangular_solve(lower, jnp.eye(BLK, dtype=jnp.float32), left_...  10.5 us
    all_to_all x2, starting transfers between devices, trade(): lax.all_to_all(value, 'col', 0, 0, axis_index_groups=groups, tiled=True)  9.53 us
  transfers between devices with their start and end apart: 31, of which 11 were waited for; matrix products, arithmetic and copies ran while one was open for 13% of the time, Pallas kernels for 0%

profile of v2, /device:TPU:97, one launch (start us, length us, event | category | flops | bytes accessed | tf_op | source)
XLA Modules:
  0.0 339.5 jit_solution(13783136272713958143)
XLA Ops:
  4.1 24.3 %update.1 = (f32[4,16,48,128]{3,2,1,0:T(8,128)}, f32[4,16,48,128]{3,2,1,0:T(8,128)}, f32[4,16,48,128]{3,2,1,0:T(8,128)}, f32[4,16,48,128]{3,2,1,0:T(8,128)}, f32...) custom-call(s32[6]{0:T(128)S(1)} %stack.56.pos, ...), custom_call_target="tpu_custom_call" | custom-call | flops 12884901888 | bytes 41943040 | tf_op jit(solution)/shard_map/update/pallas_call | solution.py:91
  28.4 5.1 %all-to-all-start = ((f32[4,84,32,128]{3,2,1,0:T(8,128)}), f32[4,84,32,128]{3,2,1,0:T(8,128)}, u32[]{:S(2)}, u32[]{:S(2)}) async-start(f32[4,84,32,128]{3,2,1,0:T(8,128)} %get-tuple-element.23), calls=%async_computation | async-start | bytes 11010048 | tf_op jit(solution)/shard_map/all_to_all | solution.py:215
  38.4 4.2 %collective-permute-start.4 = (f32[64,48,128]{2,1,0:T(8,128)}, f32[64,48,128]{2,1,0:T(8,128)}, u32[]{:S(2)}, u32[]{:S(2)}) collective-permute-start(f32[64,48,128]{2,1,0:T(8,128)} %bitcast.87), channel_id=1, source_target_pairs={{0,1},{1,64},{2,3},{3,66},{4,5},{5,68},{6,7},{7,70},{8,9},{9,72},{... | collective-permute-start | bytes 4718600 | tf_op jit(solution)/shard_map/ppermute | solution.py:48
  42.6 4.4 %collective-permute-start.5 = (f32[64,48,128]{2,1,0:T(8,128)}, f32[64,48,128]{2,1,0:T(8,128)}, u32[]{:S(2)}, u32[]{:S(2)}) collective-permute-start(f32[64,48,128]{2,1,0:T(8,128)} %bitcast.86), channel_id=1, source_target_pairs={{0,64},{1,65},{2,66},{3,67},{4,68},{5,69},{6,70},{7,71},{8,72},{9,... | collective-permute-start | bytes 4718600 | tf_op jit(solution)/shard_map/ppermute | solution.py:48
  47.0 23.3 %collective-permute-done.1.refs_1_ = f32[64,48,128]{2,1,0:T(8,128)S(1)} collective-permute-done((f32[64,48,128]{2,1,0:T(8,128)}, f32[64,48,128]{2,1,0:T(8,128)S(1)}, u32[]{:S(2)}, u32[]{:S(2)}) %collective-permute-start.1) | collective-permute-done | bytes 1572896 | tf_op jit(solution)/shard_map/ppermute | solution.py:48
  70.4 41.5 %collective-permute-start.6 = (f32[64,48,128]{2,1,0:T(8,128)}, f32[64,48,128]{2,1,0:T(8,128)}, u32[]{:S(2)}, u32[]{:S(2)}) collective-permute-start(f32[64,48,128]{2,1,0:T(8,128)} %bitcast.85), channel_id=1, source_target_pairs={{0,65},{1,0},{2,67},{3,2},{4,69},{5,4},{6,71},{7,6},{8,73},{9,8},{... | collective-permute-start | bytes 4718600 | tf_op jit(solution)/shard_map/ppermute | solution.py:48
  113.8 29.5 %collective-permute-done.6.refs_7_ = f32[64,48,128]{2,1,0:T(8,128)} collective-permute-done((f32[64,48,128]{2,1,0:T(8,128)}, f32[64,48,128]{2,1,0:T(8,128)}, u32[]{:S(2)}, u32[]{:S(2)}) %collective-permute-start.6) | collective-permute-done | bytes 1572896 | tf_op jit(solution)/shard_map/ppermute | solution.py:48
  143.3 21.6 %expand.1 = (f32[148,32,128]{2,1,0:T(8,128)}, f32[148,32,128]{2,1,0:T(8,128)}, f32[2,128,48,128]{3,2,1,0:T(8,128)}, f32[2,128,48,128]{3,2,1,0:T(8,128)}) custom-call(s32[6]{0:T(128)} %copy-done.3, s32[4,32]{1,0:T(4,128)} %broadcast_add_fusion.places, s32[4,16]{1,0:T(4,128)} %copy-done.12, s32[4,16]{1,0:T(4,128)} %get-tuple-element.81.maps_x, ...), custom_call_target="tpu_custom_call" | custom-call | flops 8388608 | bytes 37748736 | tf_op jit(solution)/shard_map/expand/pallas_call | solution.py:194
  164.8 3.9 %slice_bitcast_fusion.1 = f32[128,48,128]{2,1,0:T(8,128)} fusion(f32[2,128,48,128]{3,2,1,0:T(8,128)} %get-tuple-element.32), kind=kLoop, calls=%fused_computation.3 | loop fusion | bytes 6291456 | tf_op jit(solution)/shard_map/squeeze | solution.py:255
  168.8 3.6 %collective-permute-start.7 = (f32[128,48,128]{2,1,0:T(8,128)}, f32[128,48,128]{2,1,0:T(8,128)}, u32[]{:S(2)}, u32[]{:S(2)}) collective-permute-start(f32[128,48,128]{2,1,0:T(8,128)} %slice_bitcast_fusion.1), channel_id=1, source_target_pairs={{0,32},{1,33},{2,34},{3,35},{4,36},{5,37},{6,38},{7,39},{8,40},{9,... | collective-permute-start | bytes 9437192 | tf_op jit(solution)/shard_map/ppermute | solution.py:48
  176.0 5.5 %collective-permute-done.8 = f32[148,32,128]{2,1,0:T(8,128)} collective-permute-done((f32[148,32,128]{2,1,0:T(8,128)}, f32[148,32,128]{2,1,0:T(8,128)}, u32[]{:S(2)}, u32[]{:S(2)}) %collective-permute-start.8) | collective-permute-done | bytes 2424864 | tf_op jit(solution)/shard_map/ppermute | solution.py:48
  186.0 4.0 %bitcast_add_fusion.1 = f32[128,48,128]{2,1,0:T(8,128)} fusion(f32[128,48,128]{2,1,0:T(8,128)} %collective-permute-done.7, f32[2,128,48,128]{3,2,1,0:T(8,128)S(1)} %bitcast.67), kind=kLoop, calls=%fused_computation.1 | loop fusion | flops 786432 | bytes 9437184 | tf_op jit(solution)/shard_map/add | solution.py:255
  190.0 4.4 %all-to-all-start.1 = ((f32[4,1536,128]{2,1,0:T(8,128)}), f32[4,1536,128]{2,1,0:T(8,128)S(1)}, u32[]{:S(2)}, u32[]{:S(2)}) async-start(f32[4,1536,128]{2,1,0:T(8,128)} %bitcast.65), calls=%async_computation.1 | async-start | bytes 6291456 | tf_op jit(solution)/shard_map/all_to_all | solution.py:215
  202.4 3.2 bitcast_add_fusion
  207.9 12.0 %collective-permute-done.10 = f32[1792,128]{1,0:T(8,128)S(1)} collective-permute-done((f32[1792,128]{1,0:T(8,128)S(1)}, f32[1792,128]{1,0:T(8,128)S(1)}, u32[]{:S(2)}, u32[]{:S(2)}) %collective-permute-start.10) | collective-permute-done | bytes 917536 | tf_op jit(solution)/shard_map/ppermute | solution.py:48
  220.9 19.8 %collective-permute-done.11 = f32[1792,128]{1,0:T(8,128)} collective-permute-done((f32[1792,128]{1,0:T(8,128)}, f32[1792,128]{1,0:T(8,128)}, u32[]{:S(2)}, u32[]{:S(2)}) %collective-permute-start.11) | collective-permute-done | bytes 917536 | tf_op jit(solution)/shard_map/ppermute | solution.py:48
  260.5 3.1 collective-permute-start.17
  264.9 4.4 %collective-permute-start.18 = (f32[896,128]{1,0:T(8,128)S(1)}, f32[896,128]{1,0:T(8,128)S(1)}, u32[]{:S(2)}, u32[]{:S(2)}) collective-permute-start(f32[896,128]{1,0:T(8,128)S(1)} %concatenate.45), channel_id=1, source_target_pairs={{0,6},{1,7},{2,0},{3,1},{4,2},{5,3},{6,4},{7,5},{8,14},{9,15},{10,... | collective-permute-start | bytes 1376264 | tf_op jit(solution)/shard_map/ppermute | solution.py:48
  271.8 10.1 %collective-permute-done.17 = f32[896,128]{1,0:T(8,128)S(1)} collective-permute-done((f32[896,128]{1,0:T(8,128)S(1)}, f32[896,128]{1,0:T(8,128)S(1)}, u32[]{:S(2)}, u32[]{:S(2)}) %collective-permute-start.17) | collective-permute-done | bytes 458784 | tf_op jit(solution)/shard_map/ppermute | solution.py:48
  284.0 11.7 %cholesky.16 = f32[128,128]{1,0:T(8,128)S(1)} custom-call(f32[128,128]{1,0:T(8,128)S(1)} %slice.170), custom_call_target="Cholesky" | custom-call | tf_op jit(solution)/shard_map/cholesky | solution.py:294
  299.1 9.8 %custom-call.5 = f32[1,128,128]{1,2,0:T(8,128)S(1)} custom-call(f32[1,128,128]{2,1,0:T(8,128)S(1)} %get-tuple-element.43), custom_call_target="InvertDiagBlocksLowerTriangular" | custom-call | tf_op jit(solution)/shard_map/triangular_solve | solution.py:295
  308.9 6.3 %collective-permute-start.27 = (f32[384,128]{1,0:T(8,128)S(1)}, f32[384,128]{1,0:T(8,128)S(1)}, u32[]{:S(2)}, u32[]{:S(2)}) collective-permute-start(f32[384,128]{1,0:T(8,128)S(1)} %add_add_fusion.1), channel_id=1, source_target_pairs={{0,0},{1,1},{2,32},{3,33},{4,64},{5,65},{6,96},{7,97},{8,8},{9,9},... | collective-permute-start | bytes 589832 | tf_op jit(solution)/shard_map/ppermute | solution.py:48
  316.3 5.9 %collective-permute-start.26 = (f32[1024,128]{1,0:T(8,128)S(1)}, f32[1024,128]{1,0:T(8,128)S(1)}, u32[]{:S(2)}, u32[]{:S(2)}) collective-permute-start(f32[1024,128]{1,0:T(8,128)S(1)} %pad_maximum_fusion.11), channel_id=1, source_target_pairs={{0,0},{1,1},{2,2},{3,3},{4,4},{5,5},{6,6},{7,7},{8,32},{9,33},{10,... | collective-permute-start | bytes 1572872 | tf_op jit(solution)/shard_map/ppermute | solution.py:48
  322.8 13.4 %collective-permute-done.26 = f32[1024,128]{1,0:T(8,128)S(1)} collective-permute-done((f32[1024,128]{1,0:T(8,128)S(1)}, f32[1024,128]{1,0:T(8,128)S(1)}, u32[]{:S(2)}, u32[]{:S(2)}) %collective-permute-start.26) | collective-permute-done | bytes 524320 | tf_op jit(solution)/shard_map/ppermute | solution.py:48
  (123 shorter events, 62.9 us)
Async XLA Ops:
  28.4 114.8 %all-to-all-start = ((f32[4,84,32,128]{3,2,1,0:T(8,128)}), f32[4,84,32,128]{3,2,1,0:T(8,128)}, u32[]{:S(2)}, u32[]{:S(2)}) async-start(f32[4,84,32,128]{3,2,1,0:T(8,128)} %get-tuple-element.23), calls=%async_computation | async-start | bytes 11010048 | tf_op jit(solution)/shard_map/all_to_all | solution.py:215
  33.5 36.9 %collective-permute-start.1 = (f32[64,48,128]{2,1,0:T(8,128)}, f32[64,48,128]{2,1,0:T(8,128)S(1)}, u32[]{:S(2)}, u32[]{:S(2)}) collective-permute-start(f32[64,48,128]{2,1,0:T(8,128)} %bitcast.11), channel_id=1, source_target_pairs={{0,2},{1,3},{2,4},{3,5},{4,6},{5,7},{6,0},{7,1},{8,10},{9,11},{10,... | collective-permute-start | bytes 4718600 | tf_op jit(solution)/shard_map/ppermute | solution.py:48
  34.8 79.0 %collective-permute-start.2 = (f32[64,48,128]{2,1,0:T(8,128)}, f32[64,48,128]{2,1,0:T(8,128)S(1)}, u32[]{:S(2)}, u32[]{:S(2)}) collective-permute-start(f32[64,48,128]{2,1,0:T(8,128)} %bitcast.89), channel_id=1, source_target_pairs={{0,4},{1,5},{2,6},{3,7},{4,0},{5,1},{6,2},{7,3},{8,12},{9,13},{10,... | collective-permute-start | bytes 4718600 | tf_op jit(solution)/shard_map/ppermute | solution.py:48
  37.2 76.5 %collective-permute-start.3 = (f32[64,48,128]{2,1,0:T(8,128)}, f32[64,48,128]{2,1,0:T(8,128)}, u32[]{:S(2)}, u32[]{:S(2)}) collective-permute-start(f32[64,48,128]{2,1,0:T(8,128)} %bitcast.88), channel_id=1, source_target_pairs={{0,6},{1,7},{2,0},{3,1},{4,2},{5,3},{6,4},{7,5},{8,14},{9,15},{10,... | collective-permute-start | bytes 4718600 | tf_op jit(solution)/shard_map/ppermute | solution.py:48
  38.4 75.4 %collective-permute-start.4 = (f32[64,48,128]{2,1,0:T(8,128)}, f32[64,48,128]{2,1,0:T(8,128)}, u32[]{:S(2)}, u32[]{:S(2)}) collective-permute-start(f32[64,48,128]{2,1,0:T(8,128)} %bitcast.87), channel_id=1, source_target_pairs={{0,1},{1,64},{2,3},{3,66},{4,5},{5,68},{6,7},{7,70},{8,9},{9,72},{... | collective-permute-start | bytes 4718600 | tf_op jit(solution)/shard_map/ppermute | solution.py:48
  42.6 71.2 %collective-permute-start.5 = (f32[64,48,128]{2,1,0:T(8,128)}, f32[64,48,128]{2,1,0:T(8,128)}, u32[]{:S(2)}, u32[]{:S(2)}) collective-permute-start(f32[64,48,128]{2,1,0:T(8,128)} %bitcast.86), channel_id=1, source_target_pairs={{0,64},{1,65},{2,66},{3,67},{4,68},{5,69},{6,70},{7,71},{8,72},{9,... | collective-permute-start | bytes 4718600 | tf_op jit(solution)/shard_map/ppermute | solution.py:48
  70.4 72.9 %collective-permute-start.6 = (f32[64,48,128]{2,1,0:T(8,128)}, f32[64,48,128]{2,1,0:T(8,128)}, u32[]{:S(2)}, u32[]{:S(2)}) collective-permute-start(f32[64,48,128]{2,1,0:T(8,128)} %bitcast.85), channel_id=1, source_target_pairs={{0,65},{1,0},{2,67},{3,2},{4,69},{5,4},{6,71},{7,6},{8,73},{9,8},{... | collective-permute-start | bytes 4718600 | tf_op jit(solution)/shard_map/ppermute | solution.py:48
  168.8 17.2 %collective-permute-start.7 = (f32[128,48,128]{2,1,0:T(8,128)}, f32[128,48,128]{2,1,0:T(8,128)}, u32[]{:S(2)}, u32[]{:S(2)}) collective-permute-start(f32[128,48,128]{2,1,0:T(8,128)} %slice_bitcast_fusion.1), channel_id=1, source_target_pairs={{0,32},{1,33},{2,34},{3,35},{4,36},{5,37},{6,38},{7,39},{8,40},{9,... | collective-permute-start | bytes 9437192 | tf_op jit(solution)/shard_map/ppermute | solution.py:48
  174.2 28.2 %collective-permute-start.12 = (f32[128,48,128]{2,1,0:T(8,128)}, f32[128,48,128]{2,1,0:T(8,128)}, u32[]{:S(2)}, u32[]{:S(2)}) collective-permute-start(f32[128,48,128]{2,1,0:T(8,128)} %slice_bitcast_fusion), channel_id=1, source_target_pairs={{0,32},{1,33},{2,34},{3,35},{4,36},{5,37},{6,38},{7,39},{8,40},{9,... | collective-permute-start | bytes 9437192 | tf_op jit(solution)/shard_map/ppermute | solution.py:48
  190.0 57.4 %all-to-all-start.1 = ((f32[4,1536,128]{2,1,0:T(8,128)}), f32[4,1536,128]{2,1,0:T(8,128)S(1)}, u32[]{:S(2)}, u32[]{:S(2)}) async-start(f32[4,1536,128]{2,1,0:T(8,128)} %bitcast.65), calls=%async_computation.1 | async-start | bytes 6291456 | tf_op jit(solution)/shard_map/all_to_all | solution.py:215
  197.2 22.8 %collective-permute-start.10 = (f32[1792,128]{1,0:T(8,128)S(1)}, f32[1792,128]{1,0:T(8,128)S(1)}, u32[]{:S(2)}, u32[]{:S(2)}) collective-permute-start(f32[1792,128]{1,0:T(8,128)S(1)} %get-tuple-element.62), channel_id=1, source_target_pairs={{0,64},{1,65},{2,66},{3,67},{4,68},{5,69},{6,70},{7,71},{8,72},{9,... | collective-permute-start | bytes 2752520 | tf_op jit(solution)/shard_map/ppermute | solution.py:48
  199.7 41.0 %collective-permute-start.11 = (f32[1792,128]{1,0:T(8,128)}, f32[1792,128]{1,0:T(8,128)}, u32[]{:S(2)}, u32[]{:S(2)}) collective-permute-start(f32[1792,128]{1,0:T(8,128)} %get-tuple-element.64), channel_id=1, source_target_pairs={{0,65},{1,0},{2,67},{3,2},{4,69},{5,4},{6,71},{7,6},{8,73},{9,8},{... | collective-permute-start | bytes 2752520 | tf_op jit(solution)/shard_map/ppermute | solution.py:48
  199.7 41.0 %collective-permute-start.9 = (f32[1792,128]{1,0:T(8,128)}, f32[1792,128]{1,0:T(8,128)}, u32[]{:S(2)}, u32[]{:S(2)}) collective-permute-start(f32[1792,128]{1,0:T(8,128)} %get-tuple-element.63), channel_id=1, source_target_pairs={{0,1},{1,64},{2,3},{3,66},{4,5},{5,68},{6,7},{7,70},{8,9},{9,72},{... | collective-permute-start | bytes 2752520 | tf_op jit(solution)/shard_map/ppermute | solution.py:48
  207.4 36.4 %collective-permute-start.13 = (f32[1536,128]{1,0:T(8,128)}, f32[1536,128]{1,0:T(8,128)}, u32[]{:S(2)}, u32[]{:S(2)}) collective-permute-start(f32[1536,128]{1,0:T(8,128)} %bitcast.29), channel_id=1, source_target_pairs={{0,2},{1,3},{2,4},{3,5},{4,6},{5,7},{6,0},{7,1},{8,10},{9,11},{10,... | collective-permute-start | bytes 2359304 | tf_op jit(solution)/shard_map/ppermute | solution.py:48
  207.4 36.4 %collective-permute-start.14 = (f32[1536,128]{1,0:T(8,128)}, f32[1536,128]{1,0:T(8,128)}, u32[]{:S(2)}, u32[]{:S(2)}) collective-permute-start(f32[1536,128]{1,0:T(8,128)} %bitcast.30), channel_id=1, source_target_pairs={{0,4},{1,5},{2,6},{3,7},{4,0},{5,1},{6,2},{7,3},{8,12},{9,13},{10,... | collective-permute-start | bytes 2359304 | tf_op jit(solution)/shard_map/ppermute | solution.py:48
  220.9 23.9 %collective-permute-start.15 = (f32[1536,128]{1,0:T(8,128)}, f32[1536,128]{1,0:T(8,128)}, u32[]{:S(2)}, u32[]{:S(2)}) collective-permute-start(f32[1536,128]{1,0:T(8,128)} %bitcast.31), channel_id=1, source_target_pairs={{0,6},{1,7},{2,0},{3,1},{4,2},{5,3},{6,4},{7,5},{8,14},{9,15},{10,... | collective-permute-start | bytes 2359304 | tf_op jit(solution)/shard_map/ppermute | solution.py:48
  256.7 13.7 %collective-permute-start.23 = (f32[384,128]{1,0:T(8,128)S(1)}, f32[384,128]{1,0:T(8,128)S(1)}, u32[]{:S(2)}, u32[]{:S(2)}) collective-permute-start(f32[384,128]{1,0:T(8,128)S(1)} %get-tuple-element.56), channel_id=1, source_target_pairs={{0,16},{1,17},{2,18},{3,19},{4,20},{5,21},{6,22},{7,23},{8,24},{9,... | collective-permute-start | bytes 589832 | tf_op jit(solution)/shard_map/ppermute | solution.py:48
  259.2 11.1 %collective-permute-start.24 = (f32[384,128]{1,0:T(8,128)S(1)}, f32[384,128]{1,0:T(8,128)S(1)}, u32[]{:S(2)}, u32[]{:S(2)}) collective-permute-start(f32[384,128]{1,0:T(8,128)S(1)} %get-tuple-element.57), channel_id=1, source_target_pairs={{0,24},{1,25},{2,26},{3,27},{4,28},{5,29},{6,30},{7,31},{8,0},{9,1... | collective-permute-start | bytes 589832 | tf_op jit(solution)/shard_map/ppermute | solution.py:48
  260.5 11.3 %collective-permute-start.16 = (f32[896,128]{1,0:T(8,128)S(1)}, f32[896,128]{1,0:T(8,128)S(1)}, u32[]{:S(2)}, u32[]{:S(2)}) collective-permute-start(f32[896,128]{1,0:T(8,128)S(1)} %get-tuple-element.66), channel_id=1, source_target_pairs={{0,2},{1,3},{2,4},{3,5},{4,6},{5,7},{6,0},{7,1},{8,10},{9,11},{10,... | collective-permute-start | bytes 1376264 | tf_op jit(solution)/shard_map/ppermute | solution.py:48
  260.5 21.4 %collective-permute-start.17 = (f32[896,128]{1,0:T(8,128)S(1)}, f32[896,128]{1,0:T(8,128)S(1)}, u32[]{:S(2)}, u32[]{:S(2)}) collective-permute-start(f32[896,128]{1,0:T(8,128)S(1)} %get-tuple-element.65), channel_id=1, source_target_pairs={{0,4},{1,5},{2,6},{3,7},{4,0},{5,1},{6,2},{7,3},{8,12},{9,13},{10,... | collective-permute-start | bytes 1376264 | tf_op jit(solution)/shard_map/ppermute | solution.py:48
  264.9 18.9 %collective-permute-start.18 = (f32[896,128]{1,0:T(8,128)S(1)}, f32[896,128]{1,0:T(8,128)S(1)}, u32[]{:S(2)}, u32[]{:S(2)}) collective-permute-start(f32[896,128]{1,0:T(8,128)S(1)} %concatenate.45), channel_id=1, source_target_pairs={{0,6},{1,7},{2,0},{3,1},{4,2},{5,3},{6,4},{7,5},{8,14},{9,15},{10,... | collective-permute-start | bytes 1376264 | tf_op jit(solution)/shard_map/ppermute | solution.py:48
  296.4 19.7 %collective-permute-start.25 = (f32[640,128]{1,0:T(8,128)S(1)}, f32[640,128]{1,0:T(8,128)S(1)}, u32[]{:S(2)}, u32[]{:S(2)}) collective-permute-start(f32[640,128]{1,0:T(8,128)S(1)} %pad_maximum_fusion.13), channel_id=1, source_target_pairs={{0,32},{1,33},{2,34},{3,35},{4,36},{5,37},{6,38},{7,39},{8,40},{9,... | collective-permute-start | bytes 983048 | tf_op jit(solution)/shard_map/ppermute | solution.py:48
  308.9 13.3 %collective-permute-start.27 = (f32[384,128]{1,0:T(8,128)S(1)}, f32[384,128]{1,0:T(8,128)S(1)}, u32[]{:S(2)}, u32[]{:S(2)}) collective-permute-start(f32[384,128]{1,0:T(8,128)S(1)} %add_add_fusion.1), channel_id=1, source_target_pairs={{0,0},{1,1},{2,32},{3,33},{4,64},{5,65},{6,96},{7,97},{8,8},{9,9},... | collective-permute-start | bytes 589832 | tf_op jit(solution)/shard_map/ppermute | solution.py:48
  316.3 19.9 %collective-permute-start.26 = (f32[1024,128]{1,0:T(8,128)S(1)}, f32[1024,128]{1,0:T(8,128)S(1)}, u32[]{:S(2)}, u32[]{:S(2)}) collective-permute-start(f32[1024,128]{1,0:T(8,128)S(1)} %pad_maximum_fusion.11), channel_id=1, source_target_pairs={{0,0},{1,1},{2,2},{3,3},{4,4},{5,5},{6,6},{7,7},{8,32},{9,33},{10,... | collective-permute-start | bytes 1572872 | tf_op jit(solution)/shard_map/ppermute | solution.py:48
  (22 other events, 372.1 us)

commit v3 on v2

--- a/solution.py
+++ b/solution.py
@@ -8,7 +8,6 @@
 from jax.sharding import PartitionSpec as P
 
 BLK = 128
-ORDER = (2, 1, 3, 0)
 AXES = ("leaf", "col")
 ROWS = {"x": (0, 48), "z": (48, 48), "y": (96, 32)}
 UPDATE_VMEM = 52 << 20
@@ -52,22 +51,29 @@
     return lax.dot_general(lhs, rhs, (((1,), (1,)), ((), ())), preferred_element_type=jnp.float32)
 
 
-def update(pos, panel, front, pivot_front, parent, earlier, *refs):
+def update(pos, panel, front, pivot_front, parent, *refs):
     step = pl.program_id(0)
     pivots = panel.shape[2]
-    by_column, scratch = refs[8], refs[9]
+    by_column, scratch = refs[6], refs[7]
     lhs = panel[...].reshape(16 * BLK, pivots)
     rhs = panel[pl.ds(2 * step, 2)].reshape(2 * BLK, pivots)
     scratch[...] = product(lhs, rhs).reshape(16, BLK, 2 * BLK)
-    for flow, me, outs in (("x", pos[1], refs[0:4]), ("z", pos[2], refs[4:8])):
+    for flow, me, outs in (("x", pos[1], refs[0:3]), ("z", pos[2], refs[3:6])):
         first, rows = ROWS[flow]
-        for slot, out in zip(ORDER, outs):
-            top = 4 * ((me + slot) % 4)
+        own, plus, minus = outs
+        away = 4 * ((me + 2) % 4)
+        for out, at, top, count in (
+            (own, 0, 4 * me, 4),
+            (plus, 0, 4 * ((me + 1) % 4), 4),
+            (plus, 4, away, 2),
+            (minus, 0, 4 * ((me + 3) % 4), 4),
+            (minus, 4, away + 2, 2),
+        ):
             for half in range(2):
                 lanes = slice(half * BLK, (half + 1) * BLK)
-                out[:, half] = (
-                    front[half, pl.ds(top, 4), first : first + rows]
-                    - scratch[pl.ds(top, 4), first : first + rows, lanes]
+                out[at : at + count, half] = (
+                    front[half, pl.ds(top, count), first : first + rows]
+                    - scratch[pl.ds(top, count), first : first + rows, lanes]
                 )
     first, rows = ROWS["y"]
     for half in range(2):
@@ -85,7 +91,7 @@
             by_column[n, 80:84] = corner.reshape(4, rows, BLK)
 
 
-def make_updates(pos, panel, front, parent_front, parent_column):
+def make_updates(pos, panel, front, parent_front):
     pivots = panel.shape[2]
     rows_x, rows_z, rows_y = ROWS["x"][1], ROWS["z"][1], ROWS["y"][1]
     outs = pl.pallas_call(
@@ -98,44 +104,81 @@
                 pl.BlockSpec((2, 16, BLK, BLK), lambda t, pos: (t, 0, 0, 0)),
                 pl.BlockSpec((pl.squeezed, 16, BLK, BLK), lambda t, pos: (0, 0, 0, 0)),
                 pl.BlockSpec((BLK, BLK), lambda t, pos: (0, 0)),
-                pl.BlockSpec(memory_space=pl.ANY),
             ],
-            out_specs=[pl.BlockSpec((4, 2, rows_x, BLK), lambda t, pos: (0, t, 0, 0))] * 4
-            + [pl.BlockSpec((4, 2, rows_z, BLK), lambda t, pos: (0, t, 0, 0))] * 4
+            out_specs=[
+                pl.BlockSpec((count, 2, rows, BLK), lambda t, pos: (0, t, 0, 0))
+                for rows in (rows_x, rows_z)
+                for count in (4, 6, 6)
+            ]
             + [pl.BlockSpec((4, 84, rows_y, BLK), lambda t, pos: (0, 0, 0, 0))],
             scratch_shapes=[pltpu.VMEM((16, BLK, 2 * BLK), jnp.float32)],
         ),
-        out_shape=[jax.ShapeDtypeStruct((4, 16, rows_x, BLK), jnp.float32)] * 4
-        + [jax.ShapeDtypeStruct((4, 16, rows_z, BLK), jnp.float32)] * 4
+        out_shape=[
+            jax.ShapeDtypeStruct((count, 16, rows, BLK), jnp.float32)
+            for rows in (rows_x, rows_z)
+            for count in (4, 6, 6)
+        ]
         + [jax.ShapeDtypeStruct((4, 84, rows_y, BLK), jnp.float32)],
         compiler_params=pltpu.CompilerParams(vmem_limit_bytes=UPDATE_VMEM),
         cost_estimate=pl.CostEstimate(
             flops=2 * 2048 * 2048 * pivots, bytes_accessed=40 << 20, transcendentals=0
         ),
         name="update",
-    )(pos, panel, front, front, parent_front, parent_column)
-    return {
-        "x": dict(zip(ORDER, [v.reshape(64, rows_x, BLK) for v in outs[0:4]])),
-        "z": dict(zip(ORDER, [v.reshape(64, rows_z, BLK) for v in outs[4:8]])),
-        "y": outs[8],
-    }
-
-
-def expand(pos, places, maps_y, maps_x, maps_z, parent, chunks_y, *refs):
+    )(pos, panel, front, front, parent_front)
+    flat = [v.reshape(-1, v.shape[2], BLK) for v in outs[0:6]]
+    return {"x": flat[0:3], "z": flat[3:6], "y": outs[6]}
+
+
+def add_rows(flow, pos, maps, out, chunks):
     y, x, z, core = pos[0], pos[1], pos[2], pos[3]
-    keep, away, out_x, out_z = refs[8:12]
+    me = x if flow == "x" else z
+    for s, chunk, first, count in chunks:
+
+        def row(k, carry):
+            p = maps[s, 4 * me + first + k] - 8 * me
+            for block in range(16):
+                q = maps[s, block] - 8 * (block // 4)
+                if flow == "x":
+                    j = (q // 4 * 2 + q % 2 + 4 - z) % 4
+                    to = block // 4
+                    side = q // 2 % 2
+                else:
+                    j = (block // 4 + 4 - y) % 4
+                    to = (q // 2 + 4 - x) % 4
+                    side = q % 2
+                kept = jnp.where(core == side, 1, 0)
+                out[kept, 32 * j + 8 * to + p] += chunk[16 * k + block]
+            return carry
+
+        lax.fori_loop(0, count, row, 0)
+
+
+def expand_near(pos, maps_x, maps_z, parent, *refs):
+    for flow, maps, chunks, out in (
+        ("x", maps_x, refs[0:3], refs[6]),
+        ("z", maps_z, refs[3:6], refs[7]),
+    ):
+        out[...] = jnp.zeros_like(out)
+        own, behind, ahead = chunks
+        add_rows(flow, pos, maps, out, ((0, own, 0, 4), (1, behind, 0, 4), (3, ahead, 0, 4)))
+
+
+def expand_rest(pos, places, maps_y, maps_x, maps_z, parent, chunks_y, *refs):
+    y, z, core = pos[0], pos[2], pos[3]
+    near_x, near_z, far_x, far_z = refs[0], refs[1], refs[2:4], refs[4:6]
+    keep, away, out_x, out_z = refs[6:10]
     keep[0:128] = jnp.zeros_like(keep[0:128])
     away[0:128] = jnp.zeros_like(away[0:128])
-    out_x[...] = jnp.zeros_like(out_x)
-    out_z[...] = jnp.zeros_like(out_z)
+    out_x[...] = near_x[...]
+    out_z[...] = near_z[...]
+    add_rows("x", pos, maps_x, out_x, ((2, far_x[0], 0, 2), (2, far_x[1], 2, 2)))
+    add_rows("z", pos, maps_z, out_z, ((2, far_z[0], 0, 2), (2, far_z[1], 2, 2)))
     for s in range(4):
 
         def column(k, carry):
             q = maps_y[s, 4 * y + k] - 8 * y
-            to = (q // 2 + 4 - x) % 4
             for zh in range(2):
-                j = (zh * 2 + q % 2 + 4 - z) % 4
-                at = 32 * j + 8 * to
+                at = 32 * (q // 2) + 8 * ((zh * 2 + q % 2 + 4 - z) % 4)
                 for n in range(4):
                     for out, side in ((keep, core), (away, 1 - core)):
                         block = 8 * zh + 4 * side + n
@@ -165,42 +208,35 @@
         keep[144 + i] = total
         away[144 + i] = total
 
-    flows = (("x", maps_x, x, refs[0:4], out_x), ("z", maps_z, z, refs[4:8], out_z))
-    for flow, maps, me, chunks, out in flows:
-        for s, chunk in enumerate(chunks):
-
-            def row(k, carry):
-                p = maps[s, 4 * me + k] - 8 * me
-                for block in range(16):
-                    q = maps[s, block] - 8 * (block // 4)
-                    if flow == "x":
-                        j = block // 4
-                        to = q // 4 * 2 + q % 2
-                        side = q // 2 % 2
-                    else:
-                        j = (q // 2 + 4 - x) % 4
-                        to = (block // 4 + 4 - y) % 4
-                        side = q % 2
-                    kept = jnp.where(core == side, 1, 0)
-                    out[kept, 32 * j + 8 * to + p] += chunk[16 * k + block]
-                return carry
-
-            lax.fori_loop(0, 4, row, 0)
-
-
-def make_expand(pos, places, maps, parent, chunks):
+
+def make_expands(pos, places, maps, parent, own, behind, ahead):
     vmem = pl.BlockSpec(memory_space=pltpu.VMEM)
     smem = pl.BlockSpec(memory_space=pltpu.SMEM)
-    return pl.pallas_call(
-        expand,
-        in_specs=[smem] * 5 + [vmem] * 10,
-        out_specs=[vmem] * 4,
-        out_shape=[jax.ShapeDtypeStruct((148, ROWS["y"][1], BLK), jnp.float32)] * 2
-        + [jax.ShapeDtypeStruct((2, 128, ROWS[flow][1], BLK), jnp.float32) for flow in "xz"],
-        compiler_params=pltpu.CompilerParams(vmem_limit_bytes=EXPAND_VMEM),
-        cost_estimate=pl.CostEstimate(flops=8 << 20, bytes_accessed=36 << 20, transcendentals=0),
-        name="expand",
-    )(pos, places, maps["y"], maps["x"], maps["z"], parent, *chunks)
+    params = pltpu.CompilerParams(vmem_limit_bytes=EXPAND_VMEM)
+    cost = pl.CostEstimate(flops=8 << 20, bytes_accessed=30 << 20, transcendentals=0)
+    dense = [jax.ShapeDtypeStruct((2, 128, ROWS[flow][1], BLK), jnp.float32) for flow in "xz"]
+    near = pl.pallas_call(
+        expand_near,
+        in_specs=[smem] * 3 + [pl.BlockSpec(memory_space=pl.ANY)] + [vmem] * 6,
+        out_specs=[vmem] * 2,
+        out_shape=dense,
+        compiler_params=params,
+        cost_estimate=cost,
+        name="expand_near",
+    )(pos, maps["x"], maps["z"], parent, *(v[flow] for flow in "xz" for v in (own, behind, ahead)))
+
+    def rest(chunks_y, far_x, far_z):
+        return pl.pallas_call(
+            expand_rest,
+            in_specs=[smem] * 5 + [vmem] * 8,
+            out_specs=[vmem] * 4,
+            out_shape=[jax.ShapeDtypeStruct((148, ROWS["y"][1], BLK), jnp.float32)] * 2 + dense,
+            compiler_params=params,
+            cost_estimate=cost,
+            name="expand_rest",
+        )(pos, places, maps["y"], maps["x"], maps["z"], parent, chunks_y, *near, *far_x, *far_z)
+
+    return rest
 
 
 def arrivals(slots, axis):
@@ -211,11 +247,21 @@
     )
 
 
+def ring_scatter(slots, axis):
+    half = slots.shape[1] // 2
+    behind = send(slots[2, :half], along(axis, 1))
+    ahead = send(slots[2, half:], along(axis, -1))
+    plus = jnp.concatenate([slots[1, :half] + behind, slots[1, half:]])
+    minus = jnp.concatenate([slots[3, :half], slots[3, half:] + ahead])
+    return slots[0] + send(plus, along(axis, 1)) + send(minus, along(axis, -1))
+
+
 def trade(value, groups):
     return lax.all_to_all(value, "col", 0, 0, axis_index_groups=groups, tiled=True)
 
 
 Y_GROUPS = [[8 * k + n for k in range(4)] for n in range(8)]
+X_GROUPS = [[8 * y + 2 * k + zl for k in range(4)] for y in range(4) for zl in range(2)]
 
 
 def per_device(child_panels, child_fronts, parent_front, block_maps, right_sides):
@@ -246,40 +292,45 @@
     places = places_of(maps["y"])
     parent_column = send(parent_front.reshape(32, 32, BLK), PARENT)
 
-    slots = make_updates(pos, panel, front, parent_front, parent_column)
-    chunks = [trade(slots["y"], Y_GROUPS)]
+    slots = make_updates(pos, panel, front, parent_front)
+    chunks_y = trade(slots["y"], Y_GROUPS)
+    own, behind, ahead, far = {}, {}, {}, {}
     for flow in "xz":
-        chunks += [slots[flow][0], *arrivals(slots[flow], flow)]
-    keep, away, dense_x, dense_z = make_expand(pos, places, maps, parent_column, chunks)
+        own[flow], plus, minus = slots[flow]
+        behind[flow] = send(plus, along(flow, 1))
+        ahead[flow] = send(minus, along(flow, -1))
+        far[flow] = (
+            send(behind[flow][64:96], along(flow, 1)),
+            send(ahead[flow][64:96], along(flow, -1)),
+        )
+    rest = make_expands(pos, places, maps, parent_column, own, behind, ahead)
+    keep, away, dense_x, dense_z = rest(chunks_y, far["x"], far["z"])
     halves_y = (keep + send(away, SIBLING)).reshape(148 * 32, BLK)
     halves_x = (dense_x[1] + send(dense_x[0], SIBLING)).reshape(4, 32 * 48, BLK)
     halves_z = (dense_z[1] + send(dense_z[0], SIBLING)).reshape(4, 32 * 48, BLK)
 
+    extra = halves_y[128 * 32 :]
+    quarter = 32 * 32
+    slots_y = jnp.stack(
+        [jnp.concatenate([halves_y[j * quarter : (j + 1) * quarter], extra]) for j in range(4)]
+    )
+    sum_y = jnp.sum(trade(slots_y, X_GROUPS), axis=0)
+    sum_x = ring_scatter(halves_x, "z")
+    sum_z = ring_scatter(halves_z, "y")
+    sum_x, sum_y, sum_z = lax.optimization_barrier((sum_x, sum_y, sum_z))
+
     rhs_mine = jnp.where((leaf == 0) & (col % 2 == 0), right_sides[0:BLK], 0.0)
-    extra = jnp.concatenate([halves_y[128 * 32 :], rhs_mine])
-    quarter = 32 * 32
-    slots_y = [
-        jnp.concatenate([halves_y[j * quarter : (j + 1) * quarter], extra]) for j in range(4)
-    ]
-    sum_x = jnp.sum(trade(halves_x, Y_GROUPS), axis=0)
+    extra = jnp.concatenate([sum_y[quarter:], rhs_mine])
+    slots_y = [jnp.concatenate([sum_y[k * 256 : (k + 1) * 256], extra]) for k in range(4)]
+    slots_z = [sum_z[k * 384 : (k + 1) * 384] for k in range(4)]
     sum_y = slots_y[0] + sum(arrivals(slots_y, "z"))
-    sum_z = halves_z[0] + sum(arrivals(halves_z, "x"))
+    sum_x = jnp.sum(trade(sum_x.reshape(4, 384, BLK), Y_GROUPS), axis=0)
+    sum_z = slots_z[0] + sum(arrivals(slots_z, "x"))
     sum_x, sum_y, sum_z = lax.optimization_barrier((sum_x, sum_y, sum_z))
-
-    extra = sum_y[quarter:]
-    rhs_rows = extra[20 * 32 :]
-    slots_y = [jnp.concatenate([sum_y[k * 256 : (k + 1) * 256], extra[0 : 20 * 32]]) for k in range(4)]
-    slots_x = [lax.dynamic_slice_in_dim(sum_x, ((z + k) % 4) * 384, 384) for k in range(4)]
-    slots_z = [sum_z[k * 384 : (k + 1) * 384] for k in range(4)]
-    sum_y = slots_y[0] + sum(arrivals(slots_y, "x"))
-    corner = sum_y[256 + 512 :]
-    sum_x = slots_x[0] + sum(arrivals(slots_x, "z"))
-    sum_z = slots_z[0] + sum(arrivals(slots_z, "y"))
-    corner, sum_x, sum_y, sum_z = lax.optimization_barrier((corner, sum_x, sum_y, sum_z))
+    corner = sum_y[768:896]
+    rhs_rows = sum_y[896:1024]
     strip_x = send(sum_x, TURN).reshape(8, 48, BLK)
     strip_z = send(sum_z, SWAP).reshape(8, 48, BLK)
-    strip_y = sum_y[0:256].reshape(8, 32, BLK)
-    assembled = jnp.concatenate([strip_x, strip_z, strip_y], axis=1).reshape(1024, BLK)
 
     mine = jnp.concatenate([sum_y[256 : 256 + 512], rhs_rows])
     other = send(mine, SIBLING)
@@ -292,6 +343,9 @@
     my_rows = send(in_range, RANGE)
 
     lower = jnp.tril(lax.linalg.cholesky(corner, symmetrize_input=False))
+    lower, strip_x, strip_z, my_rows = lax.optimization_barrier((lower, strip_x, strip_z, my_rows))
+    strip_y = sum_y[0:256].reshape(8, 32, BLK)
+    assembled = jnp.concatenate([strip_x, strip_z, strip_y], axis=1).reshape(1024, BLK)
     inverse = lax.linalg.triangular_solve(
         lower, jnp.eye(BLK, dtype=jnp.float32), left_side=True, lower=True
     )

time: 342 us -> 284 us (0.83)
  starting transfers between devices: 106 us -> 57 us
  waiting for transfers between devices: 118 us -> 96.2 us
  Pallas kernels: 45.9 us -> 57.3 us
    ppermute x29 -> x30, starting transfers between devices: 96.6 us -> 43.4 us  [send(): return lax.ppermute(value, AXES, pairs)]
    ppermute x29 -> x30, waiting for transfers between devices: 118 us -> 96.2 us  [send(): return lax.ppermute(value, AXES, pairs)]
    pallas_call x1 -> x2, Pallas kernels: 21.6 us -> 33 us  [the longest x1 17.5 us: rest(): pl.pallas_call(expand_rest, in_specs=[smem] * 5 + [vmem] * 8, out_specs=[...]
    slice x5 -> x9, local copies, waits for them, and re-layouts: 1.8 us -> 6.47 us  [the longest x2 2.37 us: ring_scatter(): return slots[0] + send(plus, along(axis, 1)) + send(minus, along(axis, -1))]
    all_to_all x2 -> x3, starting transfers between devices: 9.53 us -> 13.6 us  [trade(): lax.all_to_all(value, 'col', 0, 0, axis_index_groups=groups, tiled=True)]
  transfers between devices with their start and end apart: 31 -> 33, of which waited for: 11 -> 10; matrix products, arithmetic and copies ran while one was open for 13% -> 16% of each run, Pallas kernels for 0% -> 6%
where the time goes in v3:
time: 284 us; the launch traced here: 282 us
  waiting for transfers between devices  96.2 us (34%)
  Pallas kernels  57.3 us (20%)
  starting transfers between devices  57 us (20%)
  other arithmetic  46.7 us (16%)
  local copies, waits for them, and re-layouts  18.9 us (7%)
  matrix products  4.08 us (1%)
    ppermute x30, waiting for transfers between devices, send(): return lax.ppermute(value, AXES, pairs)  96.2 us
    ppermute x30, starting transfers between devices, send(): return lax.ppermute(value, AXES, pairs)  43.4 us
    pallas_call x1, Pallas kernels, make_updates(): pl.pallas_call(update, grid_spec=pltpu.PrefetchScalarGridSpec(num_scalar_...  24.3 us
    pallas_call x1, Pallas kernels, rest(): pl.pallas_call(expand_rest, in_specs=[smem] * 5 + [vmem] * 8, out_specs=[...  17.5 us
    pallas_call x1, Pallas kernels, make_expands(): pl.pallas_call(expand_near, in_specs=[smem] * 3 + [pl.BlockSpec(memory_sp...  15.5 us
    all_to_all x3, starting transfers between devices, trade(): lax.all_to_all(value, 'col', 0, 0, axis_index_groups=groups, tiled=True)  13.6 us
    another operation x3, other arithmetic, per_device(): lower = jnp.tril(lax.linalg.cholesky(corner, symmetrize_input=False))  12.4 us
    another operation x2, other arithmetic, per_device(): lax.linalg.triangular_solve(lower, jnp.eye(BLK, dtype=jnp.float32), left_...  9.82 us
  transfers between devices with their start and end apart: 33, of which 10 were waited for; matrix products, arithmetic and copies ran while one was open for 16% of the time, Pallas kernels for 6%

profile of v3, /device:TPU:97, one launch (start us, length us, event | category | flops | bytes accessed | tf_op | source)
XLA Modules:
  0.0 281.9 jit_solution(3953887340432973220)
XLA Ops:
  3.2 24.3 %update.1 = (f32[4,16,48,128]{3,2,1,0:T(8,128)}, f32[6,16,48,128]{3,2,1,0:T(8,128)}, f32[6,16,48,128]{3,2,1,0:T(8,128)}, f32[4,16,48,128]{3,2,1,0:T(8,128)}, f32...) custom-call(s32[6]{0:T(128)S(1)} %stack.71.pos, bf16[16,128,1536]{2,1,0:T(8,128)(2,1)} %bitcast.123, ...), custom_call_target="tpu_custom_call" | custom-call | flops 12884901888 | bytes 41943040 | tf_op jit(solution)/shard_map/update/pallas_call | solution.py:97
  27.5 5.1 %all-to-all-start = ((f32[4,84,32,128]{3,2,1,0:T(8,128)}), f32[4,84,32,128]{3,2,1,0:T(8,128)}, u32[]{:S(2)}, u32[]{:S(2)}) async-start(f32[4,84,32,128]{3,2,1,0:T(8,128)} %get-tuple-element.26), calls=%async_computation | async-start | bytes 11010048 | tf_op jit(solution)/shard_map/all_to_all | solution.py:260
  36.8 49.5 %collective-permute-done.1.refs_1_ = f32[96,48,128]{2,1,0:T(8,128)S(1)} collective-permute-done((f32[96,48,128]{2,1,0:T(8,128)}, f32[96,48,128]{2,1,0:T(8,128)S(1)}, u32[]{:S(2)}, u32[]{:S(2)}) %collective-permute-start.1) | collective-permute-done | bytes 2359328 | tf_op jit(solution)/shard_map/ppermute | solution.py:47
  88.4 2.6 collective-permute-start.6
  97.9 15.5 %expand_near.1 = (f32[2,128,48,128]{3,2,1,0:T(8,128)}, f32[2,128,48,128]{3,2,1,0:T(8,128)}) custom-call(s32[6]{0:T(128)} %copy-done.2, s32[4,16]{1,0:T(4,128)} %get-tuple-element.94.maps_x, s32[4,16]{1,0:T(4,128)} %pad_add_fusion.2.maps_z, f32[32,32,128]{2,1,0:T(8,128)} %copy-done.11, f32[64,48,128]{2,1,0:T(8,128)} %bitcast.113, f32[96,48,128]{2,1,0:T(8,128)} %copy-done.6, ...), custom_call_target="tpu_custom_call" | custom-call | flops 8388608 | bytes 31457280 | tf_op jit(solution)/shard_map/expand_near/pallas_call | solution.py:218
  113.5 17.5 %expand_rest.1 = (f32[148,32,128]{2,1,0:T(8,128)}, f32[148,32,128]{2,1,0:T(8,128)}, f32[2,128,48,128]{3,2,1,0:T(8,128)}, f32[2,128,48,128]{3,2,1,0:T(8,128)}) custom-call(s32[6]{0:T(128)} %copy-done.2, s32[4,32]{1,0:T(4,128)} %broadcast_add_fusion.places, s32[4,16]{1,0:T(4,128)} %copy-done.18, s32[4,16]{1,0:T(4,128)} %get-tuple-element.94.maps_x, ...), custom_call_target="tpu_custom_call" | custom-call | flops 8388608 | bytes 31457280 | tf_op jit(solution)/shard_map/expand_rest/pallas_call | solution.py:229
  131.0 2.6 collective-permute-start.14
  133.6 3.9 %slice_bitcast_fusion = f32[128,48,128]{2,1,0:T(8,128)} fusion(f32[2,128,48,128]{3,2,1,0:T(8,128)} %get-tuple-element.38), kind=kLoop, calls=%fused_computation.3 | loop fusion | bytes 6291456 | tf_op jit(solution)/shard_map/squeeze | solution.py:310
  144.2 4.7 %all-to-all-start.1 = ((f32[4,1664,128]{2,1,0:T(8,128)}), f32[4,1664,128]{2,1,0:T(8,128)}, u32[]{:S(2)}, u32[]{:S(2)}) async-start(f32[4,1664,128]{2,1,0:T(8,128)} %pad_maximum_fusion), calls=%async_computation.1 | async-start | bytes 6815744 | tf_op jit(solution)/shard_map/all_to_all | solution.py:260
  149.0 3.2 %bitcast_add_fusion = f32[128,48,128]{2,1,0:T(8,128)S(1)} fusion(f32[128,48,128]{2,1,0:T(8,128)} %collective-permute-done.15, f32[2,128,48,128]{3,2,1,0:T(8,128)} %get-tuple-element.38), kind=kLoop, calls=%fused_computation.1 | loop fusion | flops 786432 | bytes 9437184 | tf_op jit(solution)/shard_map/add | solution.py:310
  155.2 3.2 %bitcast_add_fusion.1 = f32[128,48,128]{2,1,0:T(8,128)S(1)} fusion(f32[128,48,128]{2,1,0:T(8,128)} %collective-permute-done.9, f32[2,128,48,128]{3,2,1,0:T(8,128)} %get-tuple-element.35), kind=kLoop, calls=%fused_computation.2 | loop fusion | flops 786432 | bytes 9437184 | tf_op jit(solution)/shard_map/add | solution.py:309
  158.6 5.0 %collective-permute-start.10 = (f32[768,128]{1,0:T(8,128)S(1)}, f32[768,128]{1,0:T(8,128)S(1)}, u32[]{:S(2)}, u32[]{:S(2)}) collective-permute-start(f32[768,128]{1,0:T(8,128)S(1)} %get-tuple-element.57), channel_id=1, source_target_pairs={{0,1},{1,64},{2,3},{3,66},{4,5},{5,68},{6,7},{7,70},{8,9},{9,72},{... | collective-permute-start | bytes 1179656 | tf_op jit(solution)/shard_map/ppermute | solution.py:47
  163.6 4.4 %collective-permute-start.12 = (f32[768,128]{1,0:T(8,128)S(1)}, f32[768,128]{1,0:T(8,128)S(1)}, u32[]{:S(2)}, u32[]{:S(2)}) collective-permute-start(f32[768,128]{1,0:T(8,128)S(1)} %get-tuple-element.58), channel_id=1, source_target_pairs={{0,65},{1,0},{2,67},{3,2},{4,69},{5,4},{6,71},{7,6},{8,73},{9,8},{... | collective-permute-start | bytes 1179656 | tf_op jit(solution)/shard_map/ppermute | solution.py:47
  171.0 5.9 %collective-permute-done.10 = f32[768,128]{1,0:T(8,128)S(1)} collective-permute-done((f32[768,128]{1,0:T(8,128)S(1)}, f32[768,128]{1,0:T(8,128)S(1)}, u32[]{:S(2)}, u32[]{:S(2)}) %collective-permute-start.10) | collective-permute-done | bytes 393248 | tf_op jit(solution)/shard_map/ppermute | solution.py:47
  182.2 5.5 %collective-permute-done.17 = f32[1536,128]{1,0:T(8,128)} collective-permute-done((f32[1536,128]{1,0:T(8,128)S(1)}, f32[1536,128]{1,0:T(8,128)}, u32[]{:S(2)}, u32[]{:S(2)}) %collective-permute-start.17) | collective-permute-done | bytes 786464 | tf_op jit(solution)/shard_map/ppermute | solution.py:47
  189.2 6.1 %collective-permute-done.11 = f32[1536,128]{1,0:T(8,128)} collective-permute-done((f32[1536,128]{1,0:T(8,128)S(1)}, f32[1536,128]{1,0:T(8,128)}, u32[]{:S(2)}, u32[]{:S(2)}) %collective-permute-start.11) | collective-permute-done | bytes 786464 | tf_op jit(solution)/shard_map/ppermute | solution.py:47
  195.3 3.5 %collective-permute-done.13 = f32[1536,128]{1,0:T(8,128)} collective-permute-done((f32[1536,128]{1,0:T(8,128)}, f32[1536,128]{1,0:T(8,128)}, u32[]{:S(2)}, u32[]{:S(2)}) %collective-permute-start.13) | collective-permute-done | bytes 786464 | tf_op jit(solution)/shard_map/ppermute | solution.py:47
  198.8 2.4 fusion.8
  211.4 3.8 %all-to-all-start.2 = ((f32[4,384,128]{2,1,0:T(8,128)}), f32[4,384,128]{2,1,0:T(8,128)S(1)}, u32[]{:S(2)}, u32[]{:S(2)}) async-start(f32[4,384,128]{2,1,0:T(8,128)} %bitcast.45), calls=%async_computation.2 | async-start | bytes 1572864 | tf_op jit(solution)/shard_map/all_to_all | solution.py:260
  218.3 14.9 %collective-permute-done.22 = f32[1024,128]{1,0:T(8,128)} collective-permute-done((f32[1024,128]{1,0:T(8,128)}, f32[1024,128]{1,0:T(8,128)}, u32[]{:S(2)}, u32[]{:S(2)}) %collective-permute-start.22) | collective-permute-done | bytes 524320 | tf_op jit(solution)/shard_map/ppermute | solution.py:47
  237.6 5.0 %collective-permute-start.29 = (f32[1024,128]{1,0:T(8,128)S(1)}, f32[1024,128]{1,0:T(8,128)S(1)}, u32[]{:S(2)}, u32[]{:S(2)}) collective-permute-start(f32[1024,128]{1,0:T(8,128)S(1)} %pad_maximum_fusion.16), channel_id=1, source_target_pairs={{0,0},{1,1},{2,2},{3,3},{4,4},{5,5},{6,6},{7,7},{8,32},{9,33},{10,... | collective-permute-start | bytes 1572872 | tf_op jit(solution)/shard_map/ppermute | solution.py:47
  242.6 11.7 %cholesky.34 = f32[128,128]{1,0:T(8,128)S(1)} custom-call(f32[128,128]{1,0:T(8,128)S(1)} %get-tuple-element.72), custom_call_target="Cholesky" | custom-call | tf_op jit(solution)/shard_map/cholesky | solution.py:345
  259.2 8.1 %collective-permute-done.26 = f32[384,128]{1,0:T(8,128)S(1)} collective-permute-done((f32[384,128]{1,0:T(8,128)}, f32[384,128]{1,0:T(8,128)S(1)}, u32[]{:S(2)}, u32[]{:S(2)}) %collective-permute-start.26) | collective-permute-done | bytes 196640 | tf_op jit(solution)/shard_map/ppermute | solution.py:47
  267.9 9.8 %custom-call.5 = f32[1,128,128]{1,2,0:T(8,128)S(1)} custom-call(f32[1,128,128]{2,1,0:T(8,128)S(1)} %select_bitcast_fusion), custom_call_target="InvertDiagBlocksLowerTriangular" | custom-call | tf_op jit(solution)/shard_map/triangular_solve | solution.py:349
  (149 shorter events, 62.0 us)
Async XLA Ops:
  27.5 86.0 %all-to-all-start = ((f32[4,84,32,128]{3,2,1,0:T(8,128)}), f32[4,84,32,128]{3,2,1,0:T(8,128)}, u32[]{:S(2)}, u32[]{:S(2)}) async-start(f32[4,84,32,128]{3,2,1,0:T(8,128)} %get-tuple-element.26), calls=%async_computation | async-start | bytes 11010048 | tf_op jit(solution)/shard_map/all_to_all | solution.py:260
  32.6 53.7 %collective-permute-start.1 = (f32[96,48,128]{2,1,0:T(8,128)}, f32[96,48,128]{2,1,0:T(8,128)S(1)}, u32[]{:S(2)}, u32[]{:S(2)}) collective-permute-start(f32[96,48,128]{2,1,0:T(8,128)} %bitcast.11), channel_id=1, source_target_pairs={{0,2},{1,3},{2,4},{3,5},{4,6},{5,7},{6,0},{7,1},{8,10},{9,11},{10,... | collective-permute-start | bytes 7077896 | tf_op jit(solution)/shard_map/ppermute | solution.py:47
  33.9 53.4 %collective-permute-start.2 = (f32[96,48,128]{2,1,0:T(8,128)}, f32[96,48,128]{2,1,0:T(8,128)S(1)}, u32[]{:S(2)}, u32[]{:S(2)}) collective-permute-start(f32[96,48,128]{2,1,0:T(8,128)} %bitcast.12), channel_id=1, source_target_pairs={{0,6},{1,7},{2,0},{3,1},{4,2},{5,3},{6,4},{7,5},{8,14},{9,15},{10,... | collective-permute-start | bytes 7077896 | tf_op jit(solution)/shard_map/ppermute | solution.py:47
  35.4 55.7 %collective-permute-start.3 = (f32[96,48,128]{2,1,0:T(8,128)}, f32[96,48,128]{2,1,0:T(8,128)S(1)}, u32[]{:S(2)}, u32[]{:S(2)}) collective-permute-start(f32[96,48,128]{2,1,0:T(8,128)} %bitcast.125), channel_id=1, source_target_pairs={{0,1},{1,64},{2,3},{3,66},{4,5},{5,68},{6,7},{7,70},{8,9},{9,72},{... | collective-permute-start | bytes 7077896 | tf_op jit(solution)/shard_map/ppermute | solution.py:47
  35.4 56.7 %collective-permute-start.4 = (f32[96,48,128]{2,1,0:T(8,128)}, f32[96,48,128]{2,1,0:T(8,128)S(1)}, u32[]{:S(2)}, u32[]{:S(2)}) collective-permute-start(f32[96,48,128]{2,1,0:T(8,128)} %bitcast.124), channel_id=1, source_target_pairs={{0,65},{1,0},{2,67},{3,2},{4,69},{5,4},{6,71},{7,6},{8,73},{9,8},{... | collective-permute-start | bytes 7077896 | tf_op jit(solution)/shard_map/ppermute | solution.py:47
  87.3 26.1 %collective-permute-start.5 = (f32[32,48,128]{2,1,0:T(8,128)}, f32[32,48,128]{2,1,0:T(8,128)}, u32[]{:S(2)}, u32[]{:S(2)}) collective-permute-start(f32[32,48,128]{2,1,0:T(8,128)} %slice.211), channel_id=1, source_target_pairs={{0,2},{1,3},{2,4},{3,5},{4,6},{5,7},{6,0},{7,1},{8,10},{9,11},{10,... | collective-permute-start | bytes 2359304 | tf_op jit(solution)/shard_map/ppermute | solution.py:47
  88.4 25.1 %collective-permute-start.6 = (f32[32,48,128]{2,1,0:T(8,128)}, f32[32,48,128]{2,1,0:T(8,128)}, u32[]{:S(2)}, u32[]{:S(2)}) collective-permute-start(f32[32,48,128]{2,1,0:T(8,128)} %slice.212), channel_id=1, source_target_pairs={{0,6},{1,7},{2,0},{3,1},{4,2},{5,3},{6,4},{7,5},{8,14},{9,15},{10,... | collective-permute-start | bytes 2359304 | tf_op jit(solution)/shard_map/ppermute | solution.py:47
  92.1 21.4 %collective-permute-start.7 = (f32[32,48,128]{2,1,0:T(8,128)}, f32[32,48,128]{2,1,0:T(8,128)}, u32[]{:S(2)}, u32[]{:S(2)}) collective-permute-start(f32[32,48,128]{2,1,0:T(8,128)} %slice.213), channel_id=1, source_target_pairs={{0,1},{1,64},{2,3},{3,66},{4,5},{5,68},{6,7},{7,70},{8,9},{9,72},{... | collective-permute-start | bytes 2359304 | tf_op jit(solution)/shard_map/ppermute | solution.py:47
  93.1 20.4 %collective-permute-start.8 = (f32[32,48,128]{2,1,0:T(8,128)}, f32[32,48,128]{2,1,0:T(8,128)}, u32[]{:S(2)}, u32[]{:S(2)}) collective-permute-start(f32[32,48,128]{2,1,0:T(8,128)} %slice.214), channel_id=1, source_target_pairs={{0,65},{1,0},{2,67},{3,2},{4,69},{5,4},{6,71},{7,6},{8,73},{9,8},{... | collective-permute-start | bytes 2359304 | tf_op jit(solution)/shard_map/ppermute | solution.py:47
  140.3 14.9 %collective-permute-start.9 = (f32[128,48,128]{2,1,0:T(8,128)}, f32[128,48,128]{2,1,0:T(8,128)}, u32[]{:S(2)}, u32[]{:S(2)}) collective-permute-start(f32[128,48,128]{2,1,0:T(8,128)} %slice_bitcast_fusion.1), channel_id=1, source_target_pairs={{0,32},{1,33},{2,34},{3,35},{4,36},{5,37},{6,38},{7,39},{8,40},{9,... | collective-permute-start | bytes 9437192 | tf_op jit(solution)/shard_map/ppermute | solution.py:47
  144.2 57.0 %all-to-all-start.1 = ((f32[4,1664,128]{2,1,0:T(8,128)}), f32[4,1664,128]{2,1,0:T(8,128)}, u32[]{:S(2)}, u32[]{:S(2)}) async-start(f32[4,1664,128]{2,1,0:T(8,128)} %pad_maximum_fusion), calls=%async_computation.1 | async-start | bytes 6815744 | tf_op jit(solution)/shard_map/all_to_all | solution.py:260
  152.4 15.6 %collective-permute-start.16 = (f32[768,128]{1,0:T(8,128)S(1)}, f32[768,128]{1,0:T(8,128)S(1)}, u32[]{:S(2)}, u32[]{:S(2)}) collective-permute-start(f32[768,128]{1,0:T(8,128)S(1)} %get-tuple-element.51), channel_id=1, source_target_pairs={{0,8},{1,9},{2,10},{3,11},{4,12},{5,13},{6,14},{7,15},{8,16},{9,17... | collective-permute-start | bytes 1179656 | tf_op jit(solution)/shard_map/ppermute | solution.py:47
  153.8 14.2 %collective-permute-start.18 = (f32[768,128]{1,0:T(8,128)S(1)}, f32[768,128]{1,0:T(8,128)S(1)}, u32[]{:S(2)}, u32[]{:S(2)}) collective-permute-start(f32[768,128]{1,0:T(8,128)S(1)} %get-tuple-element.52), channel_id=1, source_target_pairs={{0,24},{1,25},{2,26},{3,27},{4,28},{5,29},{6,30},{7,31},{8,0},{9,1... | collective-permute-start | bytes 1179656 | tf_op jit(solution)/shard_map/ppermute | solution.py:47
  158.6 18.3 %collective-permute-start.10 = (f32[768,128]{1,0:T(8,128)S(1)}, f32[768,128]{1,0:T(8,128)S(1)}, u32[]{:S(2)}, u32[]{:S(2)}) collective-permute-start(f32[768,128]{1,0:T(8,128)S(1)} %get-tuple-element.57), channel_id=1, source_target_pairs={{0,1},{1,64},{2,3},{3,66},{4,5},{5,68},{6,7},{7,70},{8,9},{9,72},{... | collective-permute-start | bytes 1179656 | tf_op jit(solution)/shard_map/ppermute | solution.py:47
  163.6 13.4 %collective-permute-start.12 = (f32[768,128]{1,0:T(8,128)S(1)}, f32[768,128]{1,0:T(8,128)S(1)}, u32[]{:S(2)}, u32[]{:S(2)}) collective-permute-start(f32[768,128]{1,0:T(8,128)S(1)} %get-tuple-element.58), channel_id=1, source_target_pairs={{0,65},{1,0},{2,67},{3,2},{4,69},{5,4},{6,71},{7,6},{8,73},{9,8},{... | collective-permute-start | bytes 1179656 | tf_op jit(solution)/shard_map/ppermute | solution.py:47
  168.1 19.6 %collective-permute-start.17 = (f32[1536,128]{1,0:T(8,128)S(1)}, f32[1536,128]{1,0:T(8,128)}, u32[]{:S(2)}, u32[]{:S(2)}) collective-permute-start(f32[1536,128]{1,0:T(8,128)S(1)} %pad_maximum_fusion.11), channel_id=1, source_target_pairs={{0,8},{1,9},{2,10},{3,11},{4,12},{5,13},{6,14},{7,15},{8,16},{9,17... | collective-permute-start | bytes 2359304 | tf_op jit(solution)/shard_map/ppermute | solution.py:47
  169.0 18.8 %collective-permute-start.19 = (f32[1536,128]{1,0:T(8,128)S(1)}, f32[1536,128]{1,0:T(8,128)}, u32[]{:S(2)}, u32[]{:S(2)}) collective-permute-start(f32[1536,128]{1,0:T(8,128)S(1)} %pad_maximum_fusion.12), channel_id=1, source_target_pairs={{0,24},{1,25},{2,26},{3,27},{4,28},{5,29},{6,30},{7,31},{8,0},{9,1... | collective-permute-start | bytes 2359304 | tf_op jit(solution)/shard_map/ppermute | solution.py:47
  177.1 18.2 %collective-permute-start.11 = (f32[1536,128]{1,0:T(8,128)S(1)}, f32[1536,128]{1,0:T(8,128)}, u32[]{:S(2)}, u32[]{:S(2)}) collective-permute-start(f32[1536,128]{1,0:T(8,128)S(1)} %pad_maximum_fusion.9), channel_id=1, source_target_pairs={{0,1},{1,64},{2,3},{3,66},{4,5},{5,68},{6,7},{7,70},{8,9},{9,72},{... | collective-permute-start | bytes 2359304 | tf_op jit(solution)/shard_map/ppermute | solution.py:47
  179.8 19.0 %collective-permute-start.13 = (f32[1536,128]{1,0:T(8,128)}, f32[1536,128]{1,0:T(8,128)}, u32[]{:S(2)}, u32[]{:S(2)}) collective-permute-start(f32[1536,128]{1,0:T(8,128)} %pad_maximum_fusion.10), channel_id=1, source_target_pairs={{0,65},{1,0},{2,67},{3,2},{4,69},{5,4},{6,71},{7,6},{8,73},{9,8},{... | collective-permute-start | bytes 2359304 | tf_op jit(solution)/shard_map/ppermute | solution.py:47
  206.3 12.0 %collective-permute-start.21 = (f32[1024,128]{1,0:T(8,128)}, f32[1024,128]{1,0:T(8,128)}, u32[]{:S(2)}, u32[]{:S(2)}) collective-permute-start(f32[1024,128]{1,0:T(8,128)} %get-tuple-element.73), channel_id=1, source_target_pairs={{0,64},{1,65},{2,66},{3,67},{4,68},{5,69},{6,70},{7,71},{8,72},{9,... | collective-permute-start | bytes 1572872 | tf_op jit(solution)/shard_map/ppermute | solution.py:47
  207.2 26.0 %collective-permute-start.22 = (f32[1024,128]{1,0:T(8,128)}, f32[1024,128]{1,0:T(8,128)}, u32[]{:S(2)}, u32[]{:S(2)}) collective-permute-start(f32[1024,128]{1,0:T(8,128)} %get-tuple-element.79), channel_id=1, source_target_pairs={{0,65},{1,0},{2,67},{3,2},{4,69},{5,4},{6,71},{7,6},{8,73},{9,8},{... | collective-permute-start | bytes 1572872 | tf_op jit(solution)/shard_map/ppermute | solution.py:47
  211.4 23.3 %all-to-all-start.2 = ((f32[4,384,128]{2,1,0:T(8,128)}), f32[4,384,128]{2,1,0:T(8,128)S(1)}, u32[]{:S(2)}, u32[]{:S(2)}) async-start(f32[4,384,128]{2,1,0:T(8,128)} %bitcast.45), calls=%async_computation.2 | async-start | bytes 1572864 | tf_op jit(solution)/shard_map/all_to_all | solution.py:260
  237.6 29.7 %collective-permute-start.29 = (f32[1024,128]{1,0:T(8,128)S(1)}, f32[1024,128]{1,0:T(8,128)S(1)}, u32[]{:S(2)}, u32[]{:S(2)}) collective-permute-start(f32[1024,128]{1,0:T(8,128)S(1)} %pad_maximum_fusion.16), channel_id=1, source_target_pairs={{0,0},{1,1},{2,2},{3,3},{4,4},{5,5},{6,6},{7,7},{8,32},{9,33},{10,... | collective-permute-start | bytes 1572872 | tf_op jit(solution)/shard_map/ppermute | solution.py:47
  254.3 12.9 %collective-permute-start.26 = (f32[384,128]{1,0:T(8,128)}, f32[384,128]{1,0:T(8,128)S(1)}, u32[]{:S(2)}, u32[]{:S(2)}) collective-permute-start(f32[384,128]{1,0:T(8,128)} %reduce_sum.29), channel_id=1, source_target_pairs={{0,0},{1,1},{2,32},{3,33},{4,64},{5,65},{6,96},{7,97},{8,8},{9,9},... | collective-permute-start | bytes 589832 | tf_op jit(solution)/shard_map/ppermute | solution.py:47
  (29 other events, 308.2 us)

commit v4 on v3

--- a/solution.py
+++ b/solution.py
@@ -51,7 +51,7 @@
     return lax.dot_general(lhs, rhs, (((1,), (1,)), ((), ())), preferred_element_type=jnp.float32)
 
 
-def update(pos, panel, front, pivot_front, parent, *refs):
+def update(pos, panel, front, pivot_front, earlier, *refs):
     step = pl.program_id(0)
     pivots = panel.shape[2]
     by_column, scratch = refs[6], refs[7]
@@ -85,13 +85,39 @@
     @pl.when(step == 0)
     def _():
         column = pivot_front[...] - scratch[:, :, 0:BLK]
-        corner = jnp.where(pos[4] == 1, column[0], 0.0) + jnp.where(pos[5] == 1, parent[...], 0.0)
         for n in range(4):
             by_column[n, 64:80] = column[4 * n : 4 * n + 4].reshape(16, rows, BLK)
-            by_column[n, 80:84] = corner.reshape(4, rows, BLK)
-
-
-def make_updates(pos, panel, front, parent_front):
+
+
+def corner(pos, panel, front, parent, out):
+    value = front[...] - product(panel[...], panel[...])
+    out[...] = jnp.where(pos[4] == 1, value, 0.0) + jnp.where(pos[5] == 1, parent[...], 0.0)
+
+
+def make_corner(pos, panel, front, parent_front):
+    pivots = panel.shape[2]
+    return pl.pallas_call(
+        corner,
+        grid_spec=pltpu.PrefetchScalarGridSpec(
+            num_scalar_prefetch=1,
+            grid=(1,),
+            in_specs=[
+                pl.BlockSpec((pl.squeezed, BLK, pivots), lambda t, pos: (0, 0, 0)),
+                pl.BlockSpec((pl.squeezed, pl.squeezed, BLK, BLK), lambda t, pos: (0, 0, 0, 0)),
+                pl.BlockSpec((BLK, BLK), lambda t, pos: (0, 0)),
+            ],
+            out_specs=pl.BlockSpec((BLK, BLK), lambda t, pos: (0, 0)),
+        ),
+        out_shape=jax.ShapeDtypeStruct((BLK, BLK), jnp.float32),
+        compiler_params=pltpu.CompilerParams(vmem_limit_bytes=16 << 20),
+        cost_estimate=pl.CostEstimate(
+            flops=2 * BLK * BLK * pivots, bytes_accessed=1 << 19, transcendentals=0
+        ),
+        name="corner",
+    )(pos, panel, front, parent_front)
+
+
+def make_updates(pos, panel, front, earlier):
     pivots = panel.shape[2]
     rows_x, rows_z, rows_y = ROWS["x"][1], ROWS["z"][1], ROWS["y"][1]
     outs = pl.pallas_call(
@@ -103,14 +129,14 @@
                 pl.BlockSpec((16, BLK, pivots), lambda t, pos: (0, 0, 0)),
                 pl.BlockSpec((2, 16, BLK, BLK), lambda t, pos: (t, 0, 0, 0)),
                 pl.BlockSpec((pl.squeezed, 16, BLK, BLK), lambda t, pos: (0, 0, 0, 0)),
-                pl.BlockSpec((BLK, BLK), lambda t, pos: (0, 0)),
+                pl.BlockSpec(memory_space=pl.ANY),
             ],
             out_specs=[
                 pl.BlockSpec((count, 2, rows, BLK), lambda t, pos: (0, t, 0, 0))
                 for rows in (rows_x, rows_z)
                 for count in (4, 6, 6)
             ]
-            + [pl.BlockSpec((4, 84, rows_y, BLK), lambda t, pos: (0, 0, 0, 0))],
+            + [pl.BlockSpec((4, 80, rows_y, BLK), lambda t, pos: (0, 0, 0, 0))],
             scratch_shapes=[pltpu.VMEM((16, BLK, 2 * BLK), jnp.float32)],
         ),
         out_shape=[
@@ -118,72 +144,75 @@
             for rows in (rows_x, rows_z)
             for count in (4, 6, 6)
         ]
-        + [jax.ShapeDtypeStruct((4, 84, rows_y, BLK), jnp.float32)],
+        + [jax.ShapeDtypeStruct((4, 80, rows_y, BLK), jnp.float32)],
         compiler_params=pltpu.CompilerParams(vmem_limit_bytes=UPDATE_VMEM),
         cost_estimate=pl.CostEstimate(
             flops=2 * 2048 * 2048 * pivots, bytes_accessed=40 << 20, transcendentals=0
         ),
         name="update",
-    )(pos, panel, front, front, parent_front)
+    )(pos, panel, front, front, earlier)
     flat = [v.reshape(-1, v.shape[2], BLK) for v in outs[0:6]]
     return {"x": flat[0:3], "z": flat[3:6], "y": outs[6]}
 
 
-def add_rows(flow, pos, maps, out, chunks):
-    y, x, z, core = pos[0], pos[1], pos[2], pos[3]
-    me = x if flow == "x" else z
+def add_rows(flow, at, down, add, chunks):
     for s, chunk, first, count in chunks:
 
         def row(k, carry):
-            p = maps[s, 4 * me + first + k] - 8 * me
+            p = down[s, first + k]
             for block in range(16):
-                q = maps[s, block] - 8 * (block // 4)
-                if flow == "x":
-                    j = (q // 4 * 2 + q % 2 + 4 - z) % 4
-                    to = block // 4
-                    side = q // 2 % 2
-                else:
-                    j = (block // 4 + 4 - y) % 4
-                    to = (q // 2 + 4 - x) % 4
-                    side = q % 2
-                kept = jnp.where(core == side, 1, 0)
-                out[kept, 32 * j + 8 * to + p] += chunk[16 * k + block]
+                add(at[s, block] + p, chunk[16 * k + block])
             return carry
 
         lax.fori_loop(0, count, row, 0)
 
 
-def expand_near(pos, maps_x, maps_z, parent, *refs):
-    for flow, maps, chunks, out in (
-        ("x", maps_x, refs[0:3], refs[6]),
-        ("z", maps_z, refs[3:6], refs[7]),
+def expand_near(at_x, down_x, at_z, down_z, *refs):
+    for flow, at, down, chunks, out in (
+        ("x", at_x, down_x, refs[0:3], refs[6]),
+        ("z", at_z, down_z, refs[3:6], refs[7]),
     ):
         out[...] = jnp.zeros_like(out)
         own, behind, ahead = chunks
-        add_rows(flow, pos, maps, out, ((0, own, 0, 4), (1, behind, 0, 4), (3, ahead, 0, 4)))
-
-
-def expand_rest(pos, places, maps_y, maps_x, maps_z, parent, chunks_y, *refs):
-    y, z, core = pos[0], pos[2], pos[3]
+
+        def add(piece, value):
+            out[piece] += value
+
+        add_rows(flow, at, down, add, ((0, own, 0, 4), (1, behind, 0, 4), (3, ahead, 0, 4)))
+
+
+def expand_rest(pos, places, at_y, down_y, at_x, down_x, at_z, down_z, parent, chunks_y, *refs):
+    y, core = pos[0], pos[3]
     near_x, near_z, far_x, far_z = refs[0], refs[1], refs[2:4], refs[4:6]
-    keep, away, out_x, out_z = refs[6:10]
+    keep, away, keep_x, away_x, keep_z, away_z = refs[6:12]
+    for flow, at, down, near, far, kept, sent in (
+        ("x", at_x, down_x, near_x, far_x, keep_x, away_x),
+        ("z", at_z, down_z, near_z, far_z, keep_z, away_z),
+    ):
+        sent[...] = near[0:128]
+        kept[...] = near[128:256]
+
+        def add(piece, value):
+            @pl.when(piece >= 128)
+            def _():
+                kept[piece - 128] += value
+
+            @pl.when(piece < 128)
+            def _():
+                sent[piece] += value
+
+        add_rows(flow, at, down, add, ((2, far[0], 0, 2), (2, far[1], 2, 2)))
     keep[0:128] = jnp.zeros_like(keep[0:128])
     away[0:128] = jnp.zeros_like(away[0:128])
-    out_x[...] = near_x[...]
-    out_z[...] = near_z[...]
-    add_rows("x", pos, maps_x, out_x, ((2, far_x[0], 0, 2), (2, far_x[1], 2, 2)))
-    add_rows("z", pos, maps_z, out_z, ((2, far_z[0], 0, 2), (2, far_z[1], 2, 2)))
     for s in range(4):
 
         def column(k, carry):
-            q = maps_y[s, 4 * y + k] - 8 * y
             for zh in range(2):
-                at = 32 * (q // 2) + 8 * ((zh * 2 + q % 2 + 4 - z) % 4)
+                at = at_y[s, 2 * k + zh]
                 for n in range(4):
                     for out, side in ((keep, core), (away, 1 - core)):
                         block = 8 * zh + 4 * side + n
-                        p = maps_y[s, block] - 8 * (2 * zh + side)
-                        out[at + p] += chunks_y[s, 16 * k + block]
+                        out[at + down_y[s, block]] += chunks_y[s, 16 * k + block]
             return carry
 
         lax.fori_loop(0, 4, column, 0)
@@ -203,38 +232,40 @@
             return carry
 
         lax.fori_loop(0, 4, rows, 0)
-    for i in range(4):
-        total = chunks_y[0, 80 + i] + chunks_y[1, 80 + i] + chunks_y[2, 80 + i] + chunks_y[3, 80 + i]
-        keep[144 + i] = total
-        away[144 + i] = total
-
-
-def make_expands(pos, places, maps, parent, own, behind, ahead):
+
+
+def make_expands(pos, places, tables, parent, own, behind, ahead):
     vmem = pl.BlockSpec(memory_space=pltpu.VMEM)
     smem = pl.BlockSpec(memory_space=pltpu.SMEM)
     params = pltpu.CompilerParams(vmem_limit_bytes=EXPAND_VMEM)
     cost = pl.CostEstimate(flops=8 << 20, bytes_accessed=30 << 20, transcendentals=0)
-    dense = [jax.ShapeDtypeStruct((2, 128, ROWS[flow][1], BLK), jnp.float32) for flow in "xz"]
+
+    def pieces(count, flow):
+        return jax.ShapeDtypeStruct((count, ROWS[flow][1], BLK), jnp.float32)
+
     near = pl.pallas_call(
         expand_near,
-        in_specs=[smem] * 3 + [pl.BlockSpec(memory_space=pl.ANY)] + [vmem] * 6,
+        in_specs=[smem] * 4 + [vmem] * 6,
         out_specs=[vmem] * 2,
-        out_shape=dense,
+        out_shape=[pieces(256, "x"), pieces(256, "z")],
         compiler_params=params,
         cost_estimate=cost,
         name="expand_near",
-    )(pos, maps["x"], maps["z"], parent, *(v[flow] for flow in "xz" for v in (own, behind, ahead)))
+    )(*tables["x"], *tables["z"], *(v[flow] for flow in "xz" for v in (own, behind, ahead)))
 
     def rest(chunks_y, far_x, far_z):
         return pl.pallas_call(
             expand_rest,
-            in_specs=[smem] * 5 + [vmem] * 8,
-            out_specs=[vmem] * 4,
-            out_shape=[jax.ShapeDtypeStruct((148, ROWS["y"][1], BLK), jnp.float32)] * 2 + dense,
+            in_specs=[smem] * 8 + [vmem] * 8,
+            out_specs=[vmem] * 6,
+            out_shape=[pieces(144, "y")] * 2 + [pieces(128, "x")] * 2 + [pieces(128, "z")] * 2,
             compiler_params=params,
             cost_estimate=cost,
             name="expand_rest",
-        )(pos, places, maps["y"], maps["x"], maps["z"], parent, chunks_y, *near, *far_x, *far_z)
+        )(
+            pos, places, *tables["y"], *tables["x"], *tables["z"],
+            parent, chunks_y, *near, *far_x, *far_z,
+        )
 
     return rest
 
@@ -290,24 +321,42 @@
         "z": jnp.stack([map_at(core, y, x, (z + d) % 4) for d in (0, 3, 2, 1)]),
     }
     places = places_of(maps["y"])
+    local = {flow: maps[flow] % 8 for flow in maps}
+    ranges = (jnp.arange(16, dtype=jnp.int32) // 4)[None]
+    q = local["x"]
+    at_x = 32 * ((q // 4 * 2 + q % 2 + 4 - z) % 4) + 8 * ranges + 128 * (q // 2 % 2 == core)
+    q = local["z"]
+    at_z = 32 * ((ranges + 4 - y) % 4) + 8 * ((q // 2 + 4 - x) % 4) + 128 * (q % 2 == core)
+    q = lax.dynamic_slice_in_dim(local["y"], 4 * y, 4, 1)[:, :, None]
+    zh = jnp.arange(2, dtype=jnp.int32)[None, None]
+    at_y = (32 * (q // 2) + 8 * ((zh * 2 + q % 2 + 4 - z) % 4)).reshape(4, 8)
+    tables = {
+        "y": (at_y.astype(jnp.int32), local["y"]),
+        "x": (at_x.astype(jnp.int32), lax.dynamic_slice_in_dim(local["x"], 4 * x, 4, 1)),
+        "z": (at_z.astype(jnp.int32), lax.dynamic_slice_in_dim(local["z"], 4 * z, 4, 1)),
+    }
     parent_column = send(parent_front.reshape(32, 32, BLK), PARENT)
-
-    slots = make_updates(pos, panel, front, parent_front)
+    my_corner = make_corner(pos, panel, front, parent_front)
+    pivot_block = lax.psum(my_corner, AXES)
+
+    slots = make_updates(pos, panel, front, my_corner)
     chunks_y = trade(slots["y"], Y_GROUPS)
     own, behind, ahead, far = {}, {}, {}, {}
     for flow in "xz":
         own[flow], plus, minus = slots[flow]
         behind[flow] = send(plus, along(flow, 1))
         ahead[flow] = send(minus, along(flow, -1))
+        if flow == "x":
+            behind["x"], parent_column = lax.optimization_barrier((behind["x"], parent_column))
         far[flow] = (
             send(behind[flow][64:96], along(flow, 1)),
             send(ahead[flow][64:96], along(flow, -1)),
         )
-    rest = make_expands(pos, places, maps, parent_column, own, behind, ahead)
-    keep, away, dense_x, dense_z = rest(chunks_y, far["x"], far["z"])
-    halves_y = (keep + send(away, SIBLING)).reshape(148 * 32, BLK)
-    halves_x = (dense_x[1] + send(dense_x[0], SIBLING)).reshape(4, 32 * 48, BLK)
-    halves_z = (dense_z[1] + send(dense_z[0], SIBLING)).reshape(4, 32 * 48, BLK)
+    rest = make_expands(pos, places, tables, parent_column, own, behind, ahead)
+    keep_y, away_y, keep_x, away_x, keep_z, away_z = rest(chunks_y, far["x"], far["z"])
+    halves_y = (keep_y + send(away_y, SIBLING)).reshape(144 * 32, BLK)
+    halves_x = (keep_x + send(away_x, SIBLING)).reshape(4, 32 * 48, BLK)
+    halves_z = (keep_z + send(away_z, SIBLING)).reshape(4, 32 * 48, BLK)
 
     extra = halves_y[128 * 32 :]
     quarter = 32 * 32
@@ -326,9 +375,12 @@
     sum_y = slots_y[0] + sum(arrivals(slots_y, "z"))
     sum_x = jnp.sum(trade(sum_x.reshape(4, 384, BLK), Y_GROUPS), axis=0)
     sum_z = slots_z[0] + sum(arrivals(slots_z, "x"))
-    sum_x, sum_y, sum_z = lax.optimization_barrier((sum_x, sum_y, sum_z))
-    corner = sum_y[768:896]
-    rhs_rows = sum_y[896:1024]
+    lower = jnp.tril(lax.linalg.cholesky(pivot_block, symmetrize_input=False))
+    inverse = lax.linalg.triangular_solve(
+        lower, jnp.eye(BLK, dtype=jnp.float32), left_side=True, lower=True
+    )
+    sum_x, sum_y, sum_z, inverse = lax.optimization_barrier((sum_x, sum_y, sum_z, inverse))
+    rhs_rows = sum_y[768:896]
     strip_x = send(sum_x, TURN).reshape(8, 48, BLK)
     strip_z = send(sum_z, SWAP).reshape(8, 48, BLK)
 
@@ -342,13 +394,8 @@
     )
     my_rows = send(in_range, RANGE)
 
-    lower = jnp.tril(lax.linalg.cholesky(corner, symmetrize_input=False))
-    lower, strip_x, strip_z, my_rows = lax.optimization_barrier((lower, strip_x, strip_z, my_rows))
     strip_y = sum_y[0:256].reshape(8, 32, BLK)
     assembled = jnp.concatenate([strip_x, strip_z, strip_y], axis=1).reshape(1024, BLK)
-    inverse = lax.linalg.triangular_solve(
-        lower, jnp.eye(BLK, dtype=jnp.float32), left_side=True, lower=True
-    )
     row_global = (leaf * 1024 + jnp.arange(1024, dtype=jnp.int32))[:, None]
     solved = lax.dot_general(my_rows, inverse, (((1,), (1,)), ((), ())), precision=HIGHEST)
     own_panel = lax.dot_general(col_rows, inverse, (((1,), (1,)), ((), ())), precision=HIGHEST)

time: 284 us -> 436 us (1.54)
  waiting for transfers between devices: 96.2 us -> 225 us
  between operations: 1.6 us -> 15.1 us
  local copies, waits for them, and re-layouts: 18.9 us -> 25.4 us
    psum x0 -> x1, waiting for transfers between devices: none -> 136 us  [per_device(): pivot_block = lax.psum(my_corner, AXES)]
    unnamed x39 -> x33, local copies, waits for them, and re-layouts: 5.3 us -> 14.9 us
    ppermute x30, waiting for transfers between devices: 96.2 us -> 88.2 us  [send(): return lax.ppermute(value, AXES, pairs)]
    squeeze x2 -> x0, local copies, waits for them, and re-layouts: 5.75 us -> none  [the longest x1 3.9 us: per_device(): halves_z = (dense_z[1] + send(dense_z[0], SIBLING)).reshape(4, 32 * 48, BLK)]
    add x3 -> x6, other arithmetic: 7.04 us -> 9.42 us  [the longest x1 3.24 us: per_device(): halves_x = (keep_x + send(away_x, SIBLING)).reshape(4, 32 * 48, BLK)]
    pallas_call x2 -> x3, Pallas kernels: 33 us -> 30.7 us  [the longest x1 17.5 us: rest(): pl.pallas_call(expand_rest, in_specs=[smem] * 8 + [vmem] * 8, out_specs=[...]
    another operation x5 -> x3, other arithmetic: 13.6 us -> 13.2 us  [per_device(): lower = jnp.tril(lax.linalg.cholesky(pivot_block, symmetrize_input=False))]
  transfers between devices with their start and end apart: 33 -> 34, of which waited for: 10 -> 12; matrix products, arithmetic and copies ran while one was open for 16% -> 14% of each run, Pallas kernels for 6% -> 3%
where the time goes in v4:
time: 436 us; the launch traced here: 434 us
  waiting for transfers between devices  225 us (52%)
  starting transfers between devices  58.5 us (13%)
  Pallas kernels  54.7 us (13%)
  other arithmetic  50.8 us (12%)
  local copies, waits for them, and re-layouts  25.4 us (6%)
  between operations  15.1 us (3%)
  matrix products  4.92 us (1%)
    psum x1, waiting for transfers between devices, per_device(): pivot_block = lax.psum(my_corner, AXES)  136 us
    ppermute x30, waiting for transfers between devices, send(): return lax.ppermute(value, AXES, pairs)  88.2 us
    ppermute x30, starting transfers between devices, send(): return lax.ppermute(value, AXES, pairs)  45.1 us
    pallas_call x1, Pallas kernels, make_updates(): pl.pallas_call(update, grid_spec=pltpu.PrefetchScalarGridSpec(num_scalar_...  24 us
    pallas_call x1, Pallas kernels, rest(): pl.pallas_call(expand_rest, in_specs=[smem] * 8 + [vmem] * 8, out_specs=[...  17.5 us
    unnamed x33, local copies, waits for them, and re-layouts  14.9 us
    all_to_all x3, starting transfers between devices, trade(): lax.all_to_all(value, 'col', 0, 0, axis_index_groups=groups, tiled=True)  13.3 us
    another operation x3, other arithmetic, per_device(): lower = jnp.tril(lax.linalg.cholesky(pivot_block, symmetrize_input=False))  13.2 us
  transfers between devices with their start and end apart: 34, of which 12 were waited for; matrix products, arithmetic and copies ran while one was open for 14% of the time, Pallas kernels for 3%

profile of v4, /device:TPU:97, one launch (start us, length us, event | category | flops | bytes accessed | tf_op | source)
XLA Modules:
  0.0 434.0 jit_solution(6342253737374689137)
XLA Ops:
  8.6 5.8 %copy-done = f32[1,1,16,2048,128]{4,3,2,1,0:T(8,128)S(1)} copy-done((f32[1,1,16,2048,128]{4,3,2,1,0:T(8,128)S(1)}, f32[1,1,16,2048,128]{4,3,2,1,0:T(8,128)}, u32[]{:S(2)}) %copy-start) | copy-done | bytes 16777240
  14.4 2.8 copy-done.1
  19.7 24.0 %update.1 = (f32[4,16,48,128]{3,2,1,0:T(8,128)S(1)}, f32[6,16,48,128]{3,2,1,0:T(8,128)}, f32[6,16,48,128]{3,2,1,0:T(8,128)}, f32[4,16,48,128]{3,2,1,0:T(8,128)},...) custom-call(s32[6]{0:T(128)S(1)} %stack.71.pos, ...), custom_call_target="tpu_custom_call" | custom-call | flops 12884901888 | bytes 41943040 | tf_op jit(solution)/shard_map/update/pallas_call | solution.py:123
  44.9 5.2 %all-to-all-start = ((f32[4,80,32,128]{3,2,1,0:T(8,128)}), f32[4,80,32,128]{3,2,1,0:T(8,128)}, u32[]{:S(2)}, u32[]{:S(2)}) async-start(f32[4,80,32,128]{3,2,1,0:T(8,128)} %get-tuple-element.29), calls=%async_computation | async-start | bytes 10485760 | tf_op jit(solution)/shard_map/all_to_all | solution.py:291
  57.4 46.4 %collective-permute-done.refs_1_ = f32[96,48,128]{2,1,0:T(8,128)S(1)} collective-permute-done((f32[96,48,128]{2,1,0:T(8,128)}, f32[96,48,128]{2,1,0:T(8,128)S(1)}, u32[]{:S(2)}, u32[]{:S(2)}) %collective-permute-start) | collective-permute-done | bytes 2359328 | tf_op jit(solution)/shard_map/ppermute | solution.py:47
  109.1 6.9 %collective-permute-start.7 = (f32[32,48,128]{2,1,0:T(8,128)S(1)}, f32[32,48,128]{2,1,0:T(8,128)}, u32[]{:S(2)}, u32[]{:S(2)}) collective-permute-start(f32[32,48,128]{2,1,0:T(8,128)S(1)} %slice.188), channel_id=1, source_target_pairs={{0,1},{1,64},{2,3},{3,66},{4,5},{5,68},{6,7},{7,70},{8,9},{9,72},{... | collective-permute-start | bytes 2359304 | tf_op jit(solution)/shard_map/ppermute | solution.py:47
  121.2 11.7 %expand_near.1 = (f32[256,48,128]{2,1,0:T(8,128)}, f32[256,48,128]{2,1,0:T(8,128)}) custom-call(s32[4,16]{1,0:T(4,128)} %get-tuple-element.55.at_x, s32[4,4]{1,0:T(4,128)} %constant_dynamic-slice_fusion.5.down_x, s32[4,16]{1,0:T(4,128)} %get-tuple-element.53.at_z, s32[4,4]{1,0:T(4,128)} %constant_dynamic-slice_fusion.down_z, f32[64,48,128]{2,1,0:T(8,128)} %bitcast.107, ...), custom_call_target="tpu_custom_call" | custom-call | flops 8388608 | bytes 31457280 | tf_op jit(solution)/shard_map/expand_near/pallas_call | solution.py:246
  135.1 17.5 %expand_rest.1 = (f32[144,32,128]{2,1,0:T(8,128)}, f32[144,32,128]{2,1,0:T(8,128)}, f32[128,48,128]{2,1,0:T(8,128)}, f32[128,48,128]{2,1,0:T(8,128)}, f32[128,48,128]{2,1,0:T(8,128)}, /*index=5*/f32[128,48,128]{2,1,0:T(8,128)}) custom-call(s32[6]{0:T(128)} %copy-done.5, s32[4,32]{1,0:T(4,128)} %broadcast_add_fusion.places, s32[4,8]{1,0:T(4,128)} %fusion.26.at_y, ...), custom_call_target="tpu_custom_call" | custom-call | flops 8388608 | bytes 31457280 | tf_op jit(solution)/shard_map/expand_rest/pallas_call | solution.py:257
  155.2 136.5 %all-reduce.3.cloned.1.call-done = f32[128,128]{1,0:T(8,128)} async-done(((f32[128,128]{1,0:T(8,128)}), f32[128,128]{1,0:T(8,128)}) %all-reduce.3.cloned.1.call-update) | async-done | bytes 65552 | tf_op jit(solution)/shard_map/psum | solution.py:340
  291.7 12.5 %cholesky.16 = f32[128,128]{1,0:T(8,128)S(1)} custom-call(f32[128,128]{1,0:T(8,128)} %all-reduce.3.cloned.1.call-done), custom_call_target="Cholesky" | custom-call | tf_op jit(solution)/shard_map/cholesky | solution.py:378
  317.4 4.7 %all-to-all-start.1 = ((f32[4,1536,128]{2,1,0:T(8,128)}), f32[4,1536,128]{2,1,0:T(8,128)}, u32[]{:S(2)}, u32[]{:S(2)}) async-start(f32[4,1536,128]{2,1,0:T(8,128)} %pad_maximum_fusion), calls=%async_computation.1 | async-start | bytes 6291456 | tf_op jit(solution)/shard_map/all_to_all | solution.py:291
  322.0 3.2 add.616
  328.4 2.7 collective-permute-start.19
  331.1 5.5 %collective-permute-done.10 = f32[768,128]{1,0:T(8,128)S(1)} collective-permute-done((f32[768,128]{1,0:T(8,128)S(1)}, f32[768,128]{1,0:T(8,128)S(1)}, u32[]{:S(2)}, u32[]{:S(2)}) %collective-permute-start.10) | collective-permute-done | bytes 393248 | tf_op jit(solution)/shard_map/ppermute | solution.py:47
  343.4 11.3 %custom-call.5 = f32[1,128,128]{1,2,0:T(8,128)} custom-call(f32[1,128,128]{2,1,0:T(8,128)} %get-tuple-element.51), custom_call_target="InvertDiagBlocksLowerTriangular" | custom-call | tf_op jit(solution)/shard_map/triangular_solve | solution.py:379
  359.6 2.3 fusion.6
  367.5 2.6 collective-permute-start.24
  372.4 2.5 collective-permute-start.21
  374.8 3.5 all-to-all-start.2
  383.7 11.8 %collective-permute-done.22 = f32[896,128]{1,0:T(8,128)S(1)} collective-permute-done((f32[896,128]{1,0:T(8,128)S(1)}, f32[896,128]{1,0:T(8,128)S(1)}, u32[]{:S(2)}, u32[]{:S(2)}) %collective-permute-start.22) | collective-permute-done | bytes 458784 | tf_op jit(solution)/shard_map/ppermute | solution.py:47
  398.3 4.0 collective-permute-start.28
  404.1 2.7 collective-permute-start.27
  406.8 4.3 collective-permute-done.28
  411.7 12.1 %collective-permute-done.27 = f32[1024,128]{1,0:T(8,128)S(1)} collective-permute-done((f32[1024,128]{1,0:T(8,128)S(1)}, f32[1024,128]{1,0:T(8,128)S(1)}, u32[]{:S(2)}, u32[]{:S(2)}) %collective-permute-start.27) | collective-permute-done | bytes 524320 | tf_op jit(solution)/shard_map/ppermute | solution.py:47
  (156 shorter events, 76.3 us)
Async XLA Ops:
  44.9 90.3 %all-to-all-start = ((f32[4,80,32,128]{3,2,1,0:T(8,128)}), f32[4,80,32,128]{3,2,1,0:T(8,128)}, u32[]{:S(2)}, u32[]{:S(2)}) async-start(f32[4,80,32,128]{3,2,1,0:T(8,128)} %get-tuple-element.29), calls=%async_computation | async-start | bytes 10485760 | tf_op jit(solution)/shard_map/all_to_all | solution.py:291
  50.0 241.7 %all-reduce.3.cloned.1.call-start = ((), (), s32[]{:S(2)}) async-start(), calls=%async_computation.3 | async-start | bytes 131072 | tf_op jit(solution)/shard_map/psum | solution.py:340
  50.1 53.7 %collective-permute-start = (f32[96,48,128]{2,1,0:T(8,128)}, f32[96,48,128]{2,1,0:T(8,128)S(1)}, u32[]{:S(2)}, u32[]{:S(2)}) collective-permute-start(f32[96,48,128]{2,1,0:T(8,128)} %bitcast.129), channel_id=1, source_target_pairs={{0,2},{1,3},{2,4},{3,5},{4,6},{5,7},{6,0},{7,1},{8,10},{9,11},{10,... | collective-permute-start | bytes 7077896 | tf_op jit(solution)/shard_map/ppermute | solution.py:47
  51.4 52.6 %collective-permute-start.2 = (f32[96,48,128]{2,1,0:T(8,128)}, f32[96,48,128]{2,1,0:T(8,128)}, u32[]{:S(2)}, u32[]{:S(2)}) collective-permute-start(f32[96,48,128]{2,1,0:T(8,128)} %bitcast.128), channel_id=1, source_target_pairs={{0,6},{1,7},{2,0},{3,1},{4,2},{5,3},{6,4},{7,5},{8,14},{9,15},{10,... | collective-permute-start | bytes 7077896 | tf_op jit(solution)/shard_map/ppermute | solution.py:47
  52.8 55.0 %collective-permute-start.3 = (f32[96,48,128]{2,1,0:T(8,128)}, f32[96,48,128]{2,1,0:T(8,128)}, u32[]{:S(2)}, u32[]{:S(2)}) collective-permute-start(f32[96,48,128]{2,1,0:T(8,128)} %bitcast.127), channel_id=1, source_target_pairs={{0,1},{1,64},{2,3},{3,66},{4,5},{5,68},{6,7},{7,70},{8,9},{9,72},{... | collective-permute-start | bytes 7077896 | tf_op jit(solution)/shard_map/ppermute | solution.py:47
  52.8 63.1 %collective-permute-start.4 = (f32[96,48,128]{2,1,0:T(8,128)}, f32[96,48,128]{2,1,0:T(8,128)}, u32[]{:S(2)}, u32[]{:S(2)}) collective-permute-start(f32[96,48,128]{2,1,0:T(8,128)} %bitcast.126), channel_id=1, source_target_pairs={{0,65},{1,0},{2,67},{3,2},{4,69},{5,4},{6,71},{7,6},{8,73},{9,8},{... | collective-permute-start | bytes 7077896 | tf_op jit(solution)/shard_map/ppermute | solution.py:47
  103.9 29.0 %collective-permute-start.5 = (f32[32,48,128]{2,1,0:T(8,128)S(1)}, f32[32,48,128]{2,1,0:T(8,128)}, u32[]{:S(2)}, u32[]{:S(2)}) collective-permute-start(f32[32,48,128]{2,1,0:T(8,128)S(1)} %slice.145), channel_id=1, source_target_pairs={{0,2},{1,3},{2,4},{3,5},{4,6},{5,7},{6,0},{7,1},{8,10},{9,11},{10,... | collective-permute-start | bytes 2359304 | tf_op jit(solution)/shard_map/ppermute | solution.py:47
  105.7 27.1 %collective-permute-start.6 = (f32[32,48,128]{2,1,0:T(8,128)S(1)}, f32[32,48,128]{2,1,0:T(8,128)}, u32[]{:S(2)}, u32[]{:S(2)}) collective-permute-start(f32[32,48,128]{2,1,0:T(8,128)S(1)} %slice.187), channel_id=1, source_target_pairs={{0,6},{1,7},{2,0},{3,1},{4,2},{5,3},{6,4},{7,5},{8,14},{9,15},{10,... | collective-permute-start | bytes 2359304 | tf_op jit(solution)/shard_map/ppermute | solution.py:47
  109.1 25.9 %collective-permute-start.7 = (f32[32,48,128]{2,1,0:T(8,128)S(1)}, f32[32,48,128]{2,1,0:T(8,128)}, u32[]{:S(2)}, u32[]{:S(2)}) collective-permute-start(f32[32,48,128]{2,1,0:T(8,128)S(1)} %slice.188), channel_id=1, source_target_pairs={{0,1},{1,64},{2,3},{3,66},{4,5},{5,68},{6,7},{7,70},{8,9},{9,72},{... | collective-permute-start | bytes 2359304 | tf_op jit(solution)/shard_map/ppermute | solution.py:47
  117.2 17.9 %collective-permute-start.8 = (f32[32,48,128]{2,1,0:T(8,128)S(1)}, f32[32,48,128]{2,1,0:T(8,128)}, u32[]{:S(2)}, u32[]{:S(2)}) collective-permute-start(f32[32,48,128]{2,1,0:T(8,128)S(1)} %slice.189), channel_id=1, source_target_pairs={{0,65},{1,0},{2,67},{3,2},{4,69},{5,4},{6,71},{7,6},{8,73},{9,8},{... | collective-permute-start | bytes 2359304 | tf_op jit(solution)/shard_map/ppermute | solution.py:47
  152.7 154.4 %collective-permute-start.15 = (f32[128,48,128]{2,1,0:T(8,128)}, f32[128,48,128]{2,1,0:T(8,128)}, u32[]{:S(2)}, u32[]{:S(2)}) collective-permute-start(f32[128,48,128]{2,1,0:T(8,128)} %get-tuple-element.43), channel_id=1, source_target_pairs={{0,32},{1,33},{2,34},{3,35},{4,36},{5,37},{6,38},{7,39},{8,40},{9,... | collective-permute-start | bytes 9437192 | tf_op jit(solution)/shard_map/ppermute | solution.py:47
  154.6 149.7 %collective-permute-start.14 = (f32[144,32,128]{2,1,0:T(8,128)}, f32[144,32,128]{2,1,0:T(8,128)S(1)}, u32[]{:S(2)}, u32[]{:S(2)}) collective-permute-start(f32[144,32,128]{2,1,0:T(8,128)} %get-tuple-element.41), channel_id=1, source_target_pairs={{0,32},{1,33},{2,34},{3,35},{4,36},{5,37},{6,38},{7,39},{8,40},{9,... | collective-permute-start | bytes 7077896 | tf_op jit(solution)/shard_map/ppermute | solution.py:47
  154.7 167.3 %collective-permute-start.9 = (f32[128,48,128]{2,1,0:T(8,128)}, f32[128,48,128]{2,1,0:T(8,128)}, u32[]{:S(2)}, u32[]{:S(2)}) collective-permute-start(f32[128,48,128]{2,1,0:T(8,128)} %get-tuple-element.39), channel_id=1, source_target_pairs={{0,32},{1,33},{2,34},{3,35},{4,36},{5,37},{6,38},{7,39},{8,40},{9,... | collective-permute-start | bytes 9437192 | tf_op jit(solution)/shard_map/ppermute | solution.py:47
  312.7 14.2 %collective-permute-start.16 = (f32[768,128]{1,0:T(8,128)S(1)}, f32[768,128]{1,0:T(8,128)S(1)}, u32[]{:S(2)}, u32[]{:S(2)}) collective-permute-start(f32[768,128]{1,0:T(8,128)S(1)} %get-tuple-element.59), channel_id=1, source_target_pairs={{0,8},{1,9},{2,10},{3,11},{4,12},{5,13},{6,14},{7,15},{8,16},{9,17... | collective-permute-start | bytes 1179656 | tf_op jit(solution)/shard_map/ppermute | solution.py:47
  313.6 13.3 %collective-permute-start.18 = (f32[768,128]{1,0:T(8,128)S(1)}, f32[768,128]{1,0:T(8,128)S(1)}, u32[]{:S(2)}, u32[]{:S(2)}) collective-permute-start(f32[768,128]{1,0:T(8,128)S(1)} %get-tuple-element.60), channel_id=1, source_target_pairs={{0,24},{1,25},{2,26},{3,27},{4,28},{5,29},{6,30},{7,31},{8,0},{9,1... | collective-permute-start | bytes 1179656 | tf_op jit(solution)/shard_map/ppermute | solution.py:47
  317.4 44.6 %all-to-all-start.1 = ((f32[4,1536,128]{2,1,0:T(8,128)}), f32[4,1536,128]{2,1,0:T(8,128)}, u32[]{:S(2)}, u32[]{:S(2)}) async-start(f32[4,1536,128]{2,1,0:T(8,128)} %pad_maximum_fusion), calls=%async_computation.1 | async-start | bytes 6291456 | tf_op jit(solution)/shard_map/all_to_all | solution.py:291
  328.2 28.9 %collective-permute-start.17 = (f32[1536,128]{1,0:T(8,128)S(1)}, f32[1536,128]{1,0:T(8,128)}, u32[]{:S(2)}, u32[]{:S(2)}) collective-permute-start(f32[1536,128]{1,0:T(8,128)S(1)} %pad_maximum_fusion.11), channel_id=1, source_target_pairs={{0,8},{1,9},{2,10},{3,11},{4,12},{5,13},{6,14},{7,15},{8,16},{9,17... | collective-permute-start | bytes 2359304 | tf_op jit(solution)/shard_map/ppermute | solution.py:47
  328.4 28.7 %collective-permute-start.19 = (f32[1536,128]{1,0:T(8,128)S(1)}, f32[1536,128]{1,0:T(8,128)}, u32[]{:S(2)}, u32[]{:S(2)}) collective-permute-start(f32[1536,128]{1,0:T(8,128)S(1)} %pad_maximum_fusion.12), channel_id=1, source_target_pairs={{0,24},{1,25},{2,26},{3,27},{4,28},{5,29},{6,30},{7,31},{8,0},{9,1... | collective-permute-start | bytes 2359304 | tf_op jit(solution)/shard_map/ppermute | solution.py:47
  339.0 19.6 %collective-permute-start.11 = (f32[1536,128]{1,0:T(8,128)S(1)}, f32[1536,128]{1,0:T(8,128)}, u32[]{:S(2)}, u32[]{:S(2)}) collective-permute-start(f32[1536,128]{1,0:T(8,128)S(1)} %pad_maximum_fusion.9), channel_id=1, source_target_pairs={{0,1},{1,64},{2,3},{3,66},{4,5},{5,68},{6,7},{7,70},{8,9},{9,72},{... | collective-permute-start | bytes 2359304 | tf_op jit(solution)/shard_map/ppermute | solution.py:47
  340.0 19.6 %collective-permute-start.13 = (f32[1536,128]{1,0:T(8,128)}, f32[1536,128]{1,0:T(8,128)}, u32[]{:S(2)}, u32[]{:S(2)}) collective-permute-start(f32[1536,128]{1,0:T(8,128)} %pad_maximum_fusion.10), channel_id=1, source_target_pairs={{0,65},{1,0},{2,67},{3,2},{4,69},{5,4},{6,71},{7,6},{8,73},{9,8},{... | collective-permute-start | bytes 2359304 | tf_op jit(solution)/shard_map/ppermute | solution.py:47
  364.9 13.4 %collective-permute-start.23 = (f32[384,128]{1,0:T(8,128)}, f32[384,128]{1,0:T(8,128)}, u32[]{:S(2)}, u32[]{:S(2)}) collective-permute-start(f32[384,128]{1,0:T(8,128)} %get-tuple-element.75), channel_id=1, source_target_pairs={{0,2},{1,3},{2,4},{3,5},{4,6},{5,7},{6,0},{7,1},{8,10},{9,11},{10,... | collective-permute-start | bytes 589832 | tf_op jit(solution)/shard_map/ppermute | solution.py:47
  374.8 22.0 %all-to-all-start.2 = ((f32[4,384,128]{2,1,0:T(8,128)}), f32[4,384,128]{2,1,0:T(8,128)S(1)}, u32[]{:S(2)}, u32[]{:S(2)}) async-start(f32[4,384,128]{2,1,0:T(8,128)} %bitcast.43), calls=%async_computation.2 | async-start | bytes 1572864 | tf_op jit(solution)/shard_map/all_to_all | solution.py:291
  378.3 17.2 %collective-permute-start.22 = (f32[896,128]{1,0:T(8,128)S(1)}, f32[896,128]{1,0:T(8,128)S(1)}, u32[]{:S(2)}, u32[]{:S(2)}) collective-permute-start(f32[896,128]{1,0:T(8,128)S(1)} %get-tuple-element.85), channel_id=1, source_target_pairs={{0,65},{1,0},{2,67},{3,2},{4,69},{5,4},{6,71},{7,6},{8,73},{9,8},{... | collective-permute-start | bytes 1376264 | tf_op jit(solution)/shard_map/ppermute | solution.py:47
  404.1 19.7 %collective-permute-start.27 = (f32[1024,128]{1,0:T(8,128)S(1)}, f32[1024,128]{1,0:T(8,128)S(1)}, u32[]{:S(2)}, u32[]{:S(2)}) collective-permute-start(f32[1024,128]{1,0:T(8,128)S(1)} %pad_maximum_fusion.16), channel_id=1, source_target_pairs={{0,0},{1,1},{2,2},{3,3},{4,4},{5,5},{6,6},{7,7},{8,32},{9,33},{10,... | collective-permute-start | bytes 1572872 | tf_op jit(solution)/shard_map/ppermute | solution.py:47
  (26 other events, 332.8 us)
Sparse Core Ops, SparseCore 0:
  155.3 136.3 all-reduce.2

commit v5 on v4

--- a/solution.py
+++ b/solution.py
@@ -39,6 +39,7 @@
 
 
 PARENT = [(32 * leaf, 40 * leaf) for leaf in range(4)]
+PARENT_SIBLING = [(32 * leaf, 32 * (leaf ^ 1) + 8 * leaf) for leaf in range(4)]
 RANGE = links(lambda c, y, x, z: (y % 2, z // 2 * 2 + c, x, y // 2 * 2 + z % 2))
 TURN = links(lambda c, y, x, z: (x % 2, y, z // 2 * 2 + c, x // 2 * 2 + z % 2))
 
@@ -51,7 +52,7 @@
     return lax.dot_general(lhs, rhs, (((1,), (1,)), ((), ())), preferred_element_type=jnp.float32)
 
 
-def update(pos, panel, front, pivot_front, earlier, *refs):
+def update(pos, panel, front, pivot_front, parent, *refs):
     step = pl.program_id(0)
     pivots = panel.shape[2]
     by_column, scratch = refs[6], refs[7]
@@ -85,39 +86,13 @@
     @pl.when(step == 0)
     def _():
         column = pivot_front[...] - scratch[:, :, 0:BLK]
+        corner = jnp.where(pos[4] == 1, column[0], 0.0) + jnp.where(pos[5] == 1, parent[...], 0.0)
         for n in range(4):
             by_column[n, 64:80] = column[4 * n : 4 * n + 4].reshape(16, rows, BLK)
-
-
-def corner(pos, panel, front, parent, out):
-    value = front[...] - product(panel[...], panel[...])
-    out[...] = jnp.where(pos[4] == 1, value, 0.0) + jnp.where(pos[5] == 1, parent[...], 0.0)
-
-
-def make_corner(pos, panel, front, parent_front):
-    pivots = panel.shape[2]
-    return pl.pallas_call(
-        corner,
-        grid_spec=pltpu.PrefetchScalarGridSpec(
-            num_scalar_prefetch=1,
-            grid=(1,),
-            in_specs=[
-                pl.BlockSpec((pl.squeezed, BLK, pivots), lambda t, pos: (0, 0, 0)),
-                pl.BlockSpec((pl.squeezed, pl.squeezed, BLK, BLK), lambda t, pos: (0, 0, 0, 0)),
-                pl.BlockSpec((BLK, BLK), lambda t, pos: (0, 0)),
-            ],
-            out_specs=pl.BlockSpec((BLK, BLK), lambda t, pos: (0, 0)),
-        ),
-        out_shape=jax.ShapeDtypeStruct((BLK, BLK), jnp.float32),
-        compiler_params=pltpu.CompilerParams(vmem_limit_bytes=16 << 20),
-        cost_estimate=pl.CostEstimate(
-            flops=2 * BLK * BLK * pivots, bytes_accessed=1 << 19, transcendentals=0
-        ),
-        name="corner",
-    )(pos, panel, front, parent_front)
-
-
-def make_updates(pos, panel, front, earlier):
+            by_column[n, 80:84] = corner.reshape(4, rows, BLK)
+
+
+def make_updates(pos, panel, front, parent_front):
     pivots = panel.shape[2]
     rows_x, rows_z, rows_y = ROWS["x"][1], ROWS["z"][1], ROWS["y"][1]
     outs = pl.pallas_call(
@@ -129,14 +104,14 @@
                 pl.BlockSpec((16, BLK, pivots), lambda t, pos: (0, 0, 0)),
                 pl.BlockSpec((2, 16, BLK, BLK), lambda t, pos: (t, 0, 0, 0)),
                 pl.BlockSpec((pl.squeezed, 16, BLK, BLK), lambda t, pos: (0, 0, 0, 0)),
-                pl.BlockSpec(memory_space=pl.ANY),
+                pl.BlockSpec((BLK, BLK), lambda t, pos: (0, 0)),
             ],
             out_specs=[
                 pl.BlockSpec((count, 2, rows, BLK), lambda t, pos: (0, t, 0, 0))
                 for rows in (rows_x, rows_z)
                 for count in (4, 6, 6)
             ]
-            + [pl.BlockSpec((4, 80, rows_y, BLK), lambda t, pos: (0, 0, 0, 0))],
+            + [pl.BlockSpec((4, 84, rows_y, BLK), lambda t, pos: (0, 0, 0, 0))],
             scratch_shapes=[pltpu.VMEM((16, BLK, 2 * BLK), jnp.float32)],
         ),
         out_shape=[
@@ -144,13 +119,13 @@
             for rows in (rows_x, rows_z)
             for count in (4, 6, 6)
         ]
-        + [jax.ShapeDtypeStruct((4, 80, rows_y, BLK), jnp.float32)],
+        + [jax.ShapeDtypeStruct((4, 84, rows_y, BLK), jnp.float32)],
         compiler_params=pltpu.CompilerParams(vmem_limit_bytes=UPDATE_VMEM),
         cost_estimate=pl.CostEstimate(
             flops=2 * 2048 * 2048 * pivots, bytes_accessed=40 << 20, transcendentals=0
         ),
         name="update",
-    )(pos, panel, front, front, earlier)
+    )(pos, panel, front, front, parent_front)
     flat = [v.reshape(-1, v.shape[2], BLK) for v in outs[0:6]]
     return {"x": flat[0:3], "z": flat[3:6], "y": outs[6]}
 
@@ -181,7 +156,7 @@
         add_rows(flow, at, down, add, ((0, own, 0, 4), (1, behind, 0, 4), (3, ahead, 0, 4)))
 
 
-def expand_rest(pos, places, at_y, down_y, at_x, down_x, at_z, down_z, parent, chunks_y, *refs):
+def expand_rest(pos, places, at_y, down_y, at_x, down_x, at_z, down_z, chunks_y, *refs):
     y, core = pos[0], pos[3]
     near_x, near_z, far_x, far_z = refs[0], refs[1], refs[2:4], refs[4:6]
     keep, away, keep_x, away_x, keep_z, away_z = refs[6:12]
@@ -223,18 +198,19 @@
             p = 4 * side + n
             down = [places[s, 8 * y + p] - 4 * y for s in range(4)]
             for i in range(4):
-                total = parent[4 * p + i]
+                total = None
                 for s in range(4):
                     there = has[s] & (down[s] >= 0)
                     block = chunks_y[s, 64 + 4 * jnp.maximum(down[s], 0) + i]
-                    total += jnp.where(there, block, 0.0)
+                    block = jnp.where(there, block, 0.0)
+                    total = block if total is None else total + block
                 out[128 + 4 * n + i] = total
             return carry
 
         lax.fori_loop(0, 4, rows, 0)
 
 
-def make_expands(pos, places, tables, parent, own, behind, ahead):
+def make_expands(pos, places, tables, at_near, own, behind, ahead):
     vmem = pl.BlockSpec(memory_space=pltpu.VMEM)
     smem = pl.BlockSpec(memory_space=pltpu.SMEM)
     params = pltpu.CompilerParams(vmem_limit_bytes=EXPAND_VMEM)
@@ -251,12 +227,12 @@
         compiler_params=params,
         cost_estimate=cost,
         name="expand_near",
-    )(*tables["x"], *tables["z"], *(v[flow] for flow in "xz" for v in (own, behind, ahead)))
+    )(at_near, tables["x"][1], *tables["z"], *(v[flow] for flow in "xz" for v in (own, behind, ahead)))
 
     def rest(chunks_y, far_x, far_z):
         return pl.pallas_call(
             expand_rest,
-            in_specs=[smem] * 8 + [vmem] * 8,
+            in_specs=[smem] * 8 + [vmem] * 7,
             out_specs=[vmem] * 6,
             out_shape=[pieces(144, "y")] * 2 + [pieces(128, "x")] * 2 + [pieces(128, "z")] * 2,
             compiler_params=params,
@@ -264,7 +240,7 @@
             name="expand_rest",
         )(
             pos, places, *tables["y"], *tables["x"], *tables["z"],
-            parent, chunks_y, *near, *far_x, *far_z,
+            chunks_y, *near, *far_x, *far_z,
         )
 
     return rest
@@ -335,30 +311,34 @@
         "x": (at_x.astype(jnp.int32), lax.dynamic_slice_in_dim(local["x"], 4 * x, 4, 1)),
         "z": (at_z.astype(jnp.int32), lax.dynamic_slice_in_dim(local["z"], 4 * z, 4, 1)),
     }
-    parent_column = send(parent_front.reshape(32, 32, BLK), PARENT)
-    my_corner = make_corner(pos, panel, front, parent_front)
-    pivot_block = lax.psum(my_corner, AXES)
-
-    slots = make_updates(pos, panel, front, my_corner)
+
+    slots = make_updates(pos, panel, front, parent_front)
     chunks_y = trade(slots["y"], Y_GROUPS)
+    pivot_block = jnp.sum(chunks_y[:, 80:84], axis=0).reshape(BLK, BLK)
+    pivot_block = pivot_block + send(pivot_block, SIBLING)
+    at_near, pivot_block = lax.optimization_barrier((tables["x"][0], pivot_block))
+    pivot_block = pivot_block + sum(arrivals([pivot_block] * 4, "z"))
     own, behind, ahead, far = {}, {}, {}, {}
     for flow in "xz":
         own[flow], plus, minus = slots[flow]
         behind[flow] = send(plus, along(flow, 1))
         ahead[flow] = send(minus, along(flow, -1))
-        if flow == "x":
-            behind["x"], parent_column = lax.optimization_barrier((behind["x"], parent_column))
         far[flow] = (
             send(behind[flow][64:96], along(flow, 1)),
             send(ahead[flow][64:96], along(flow, -1)),
         )
-    rest = make_expands(pos, places, tables, parent_column, own, behind, ahead)
-    keep_y, away_y, keep_x, away_x, keep_z, away_z = rest(chunks_y, far["x"], far["z"])
+    far_z, pivot_block = lax.optimization_barrier((far["z"], pivot_block))
+    rest = make_expands(pos, places, tables, at_near, own, behind, ahead)
+    keep_y, away_y, keep_x, away_x, keep_z, away_z = rest(chunks_y, far["x"], far_z)
     halves_y = (keep_y + send(away_y, SIBLING)).reshape(144 * 32, BLK)
     halves_x = (keep_x + send(away_x, SIBLING)).reshape(4, 32 * 48, BLK)
     halves_z = (keep_z + send(away_z, SIBLING)).reshape(4, 32 * 48, BLK)
 
-    extra = halves_y[128 * 32 :]
+    pivot_rows = halves_y[128 * 32 :]
+    mine = lax.dynamic_slice_in_dim(parent_front, 512 * core, 512, 0)
+    theirs = lax.dynamic_slice_in_dim(parent_front, 512 * (1 - core), 512, 0)
+    pivot_rows = pivot_rows + send(mine, PARENT) + send(theirs, PARENT_SIBLING)
+    extra = jnp.concatenate([pivot_rows, pivot_block])
     quarter = 32 * 32
     slots_y = jnp.stack(
         [jnp.concatenate([halves_y[j * quarter : (j + 1) * quarter], extra]) for j in range(4)]
@@ -369,23 +349,27 @@
     sum_x, sum_y, sum_z = lax.optimization_barrier((sum_x, sum_y, sum_z))
 
     rhs_mine = jnp.where((leaf == 0) & (col % 2 == 0), right_sides[0:BLK], 0.0)
-    extra = jnp.concatenate([sum_y[quarter:], rhs_mine])
+    pivot_block = sum_y[quarter + 512 :]
+    extra = jnp.concatenate([sum_y[quarter : quarter + 512], rhs_mine])
     slots_y = [jnp.concatenate([sum_y[k * 256 : (k + 1) * 256], extra]) for k in range(4)]
     slots_z = [sum_z[k * 384 : (k + 1) * 384] for k in range(4)]
-    sum_y = slots_y[0] + sum(arrivals(slots_y, "z"))
+    from_z = arrivals(slots_y, "z")
+    from_z, pivot_block = lax.optimization_barrier((from_z, pivot_block))
+    sum_y = slots_y[0] + sum(from_z)
     sum_x = jnp.sum(trade(sum_x.reshape(4, 384, BLK), Y_GROUPS), axis=0)
     sum_z = slots_z[0] + sum(arrivals(slots_z, "x"))
     lower = jnp.tril(lax.linalg.cholesky(pivot_block, symmetrize_input=False))
-    inverse = lax.linalg.triangular_solve(
-        lower, jnp.eye(BLK, dtype=jnp.float32), left_side=True, lower=True
-    )
-    sum_x, sum_y, sum_z, inverse = lax.optimization_barrier((sum_x, sum_y, sum_z, inverse))
+    sum_x, sum_y, sum_z, lower = lax.optimization_barrier((sum_x, sum_y, sum_z, lower))
     rhs_rows = sum_y[768:896]
     strip_x = send(sum_x, TURN).reshape(8, 48, BLK)
     strip_z = send(sum_z, SWAP).reshape(8, 48, BLK)
 
     mine = jnp.concatenate([sum_y[256 : 256 + 512], rhs_rows])
     other = send(mine, SIBLING)
+    lower, other = lax.optimization_barrier((lower, other))
+    inverse = lax.linalg.triangular_solve(
+        lower, jnp.eye(BLK, dtype=jnp.float32), left_side=True, lower=True
+    )
     low, high = jnp.where(core == 0, mine, other), jnp.where(core == 0, other, mine)
     in_range = jnp.concatenate([low[0:512], high[0:512]])
     rhs_rows = low[512:]

time: 436 us -> 318 us (0.73)
  waiting for transfers between devices: 225 us -> 133 us
  between operations: 15.1 us -> 1.64 us
  local copies, waits for them, and re-layouts: 25.4 us -> 20.3 us
  starting transfers between devices: 58.5 us -> 54 us
    psum x1 -> x0, waiting for transfers between devices: 136 us -> none  [per_device(): pivot_block = lax.psum(my_corner, AXES)]
    all_to_all x3, waiting for transfers between devices: 0.01 us -> 56.5 us  [trade(): lax.all_to_all(value, 'col', 0, 0, axis_index_groups=groups, tiled=True)]
    ppermute x30 -> x35, waiting for transfers between devices: 88.2 us -> 76.6 us  [send(): return lax.ppermute(value, AXES, pairs)]
    unnamed x33 -> x27, local copies, waits for them, and re-layouts: 14.9 us -> 6.82 us
    ppermute x30 -> x35, starting transfers between devices: 45.1 us -> 39.7 us  [send(): return lax.ppermute(value, AXES, pairs)]
    pallas_call x2 -> x1, Pallas kernels: 19 us -> 17.2 us  [rest(): pl.pallas_call(expand_rest, in_specs=[smem] * 8 + [vmem] * 7, out_specs=[...]
  transfers between devices with their start and end apart: 34 -> 38, of which waited for: 12 -> 14; matrix products, arithmetic and copies ran while one was open for 14% -> 16% of each run, Pallas kernels for 3% -> 4%
where the time goes in v5:
time: 318 us; the launch traced here: 317 us
  waiting for transfers between devices  133 us (42%)
  starting transfers between devices  54 us (17%)
  Pallas kernels  53.3 us (17%)
  other arithmetic  50.4 us (16%)
  local copies, waits for them, and re-layouts  20.3 us (6%)
  matrix products  4.08 us (1%)
    ppermute x35, waiting for transfers between devices, send(): return lax.ppermute(value, AXES, pairs)  76.6 us
    all_to_all x3, waiting for transfers between devices, trade(): lax.all_to_all(value, 'col', 0, 0, axis_index_groups=groups, tiled=True)  56.5 us
    ppermute x35, starting transfers between devices, send(): return lax.ppermute(value, AXES, pairs)  39.7 us
    pallas_call x1, Pallas kernels, make_updates(): pl.pallas_call(update, grid_spec=pltpu.PrefetchScalarGridSpec(num_scalar_...  24.3 us
    pallas_call x1, Pallas kernels, rest(): pl.pallas_call(expand_rest, in_specs=[smem] * 8 + [vmem] * 7, out_specs=[...  17.2 us
    all_to_all x3, starting transfers between devices, trade(): lax.all_to_all(value, 'col', 0, 0, axis_index_groups=groups, tiled=True)  14.3 us
    another operation x3, other arithmetic, per_device(): lower = jnp.tril(lax.linalg.cholesky(pivot_block, symmetrize_input=False))  12.4 us
    pallas_call x1, Pallas kernels, make_expands(): pl.pallas_call(expand_near, in_specs=[smem] * 4 + [vmem] * 6, out_specs=[...  11.7 us
  transfers between devices with their start and end apart: 38, of which 14 were waited for; matrix products, arithmetic and copies ran while one was open for 16% of the time, Pallas kernels for 4%

profile of v5, /device:TPU:97, one launch (start us, length us, event | category | flops | bytes accessed | tf_op | source)
XLA Modules:
  0.0 316.8 jit_solution(17881249074688556206)
XLA Ops:
  3.2 24.3 %update.1 = (f32[4,16,48,128]{3,2,1,0:T(8,128)}, f32[6,16,48,128]{3,2,1,0:T(8,128)}, f32[6,16,48,128]{3,2,1,0:T(8,128)}, f32[4,16,48,128]{3,2,1,0:T(8,128)}, f32...) custom-call(s32[6]{0:T(128)S(1)} %stack.71.pos, bf16[16,128,1536]{2,1,0:T(8,128)(2,1)} %bitcast.126, ...), custom_call_target="tpu_custom_call" | custom-call | flops 12884901888 | bytes 41943040 | tf_op jit(solution)/shard_map/update/pallas_call | solution.py:98
  27.5 5.1 %all-to-all-start = ((f32[4,84,32,128]{3,2,1,0:T(8,128)}), f32[4,84,32,128]{3,2,1,0:T(8,128)}, u32[]{:S(2)}, u32[]{:S(2)}) async-start(f32[4,84,32,128]{3,2,1,0:T(8,128)} %get-tuple-element.36), calls=%async_computation | async-start | bytes 11010048 | tf_op jit(solution)/shard_map/all_to_all | solution.py:267
  39.2 55.7 %all-to-all-done.chunks_y = f32[4,84,32,128]{3,2,1,0:T(8,128)} async-done(((f32[4,84,32,128]{3,2,1,0:T(8,128)}), f32[4,84,32,128]{3,2,1,0:T(8,128)}, u32[]{:S(2)}, u32[]{:S(2)}) %all-to-all-start) | async-done | bytes 5505056 | tf_op jit(solution)/shard_map/all_to_all | solution.py:267
  110.2 11.6 %collective-permute-done.10 = f32[128,128]{1,0:T(8,128)S(1)} collective-permute-done((f32[128,128]{1,0:T(8,128)S(1)}, f32[128,128]{1,0:T(8,128)S(1)}, u32[]{:S(2)}, u32[]{:S(2)}) %collective-permute-start.10) | collective-permute-done | bytes 65568 | tf_op jit(solution)/shard_map/ppermute | solution.py:48
  122.4 3.7 %collective-permute-done.11 = f32[128,128]{1,0:T(8,128)S(1)} collective-permute-done((f32[128,128]{1,0:T(8,128)S(1)}, f32[128,128]{1,0:T(8,128)S(1)}, u32[]{:S(2)}, u32[]{:S(2)}) %collective-permute-start.11) | collective-permute-done | bytes 65568 | tf_op jit(solution)/shard_map/ppermute | solution.py:48
  127.2 11.7 %expand_near.1 = (f32[256,48,128]{2,1,0:T(8,128)}, f32[256,48,128]{2,1,0:T(8,128)}) custom-call(s32[4,16]{1,0:T(4,128)} %get-tuple-element.37.at_x, s32[4,4]{1,0:T(4,128)} %constant_dynamic-slice_fusion.7.down_x, s32[4,16]{1,0:T(4,128)} %get-tuple-element.69.at_z, s32[4,4]{1,0:T(4,128)} %constant_dynamic-slice_fusion.2.down_z, f32[64,48,128]{2,1,0:T(8,128)} %bitcast.113, ...), custom_call_target="tpu_custom_call" | custom-call | flops 8388608 | bytes 31457280 | tf_op jit(solution)/shard_map/expand_near/pallas_call | solution.py:222
  139.9 17.2 %expand_rest.1 = (f32[144,32,128]{2,1,0:T(8,128)}, f32[144,32,128]{2,1,0:T(8,128)}, f32[128,48,128]{2,1,0:T(8,128)}, f32[128,48,128]{2,1,0:T(8,128)}, f32[128,48,128]{2,1,0:T(8,128)}, /*index=5*/f32[128,48,128]{2,1,0:T(8,128)}) custom-call(s32[6]{0:T(128)} %copy-done.2, s32[4,32]{1,0:T(4,128)} %broadcast_add_fusion.places, s32[4,8]{1,0:T(4,128)} %fusion.27.at_y, ...), custom_call_target="tpu_custom_call" | custom-call | flops 8388608 | bytes 31457280 | tf_op jit(solution)/shard_map/expand_rest/pallas_call | solution.py:233
  160.8 4.9 %collective-permute-done.17 = f32[144,32,128]{2,1,0:T(8,128)S(1)} collective-permute-done((f32[144,32,128]{2,1,0:T(8,128)}, f32[144,32,128]{2,1,0:T(8,128)S(1)}, u32[]{:S(2)}, u32[]{:S(2)}) %collective-permute-start.17) | collective-permute-done | bytes 2359328 | tf_op jit(solution)/shard_map/ppermute | solution.py:48
  179.0 4.7 %all-to-all-start.1 = ((f32[4,1664,128]{2,1,0:T(8,128)}), f32[4,1664,128]{2,1,0:T(8,128)}, u32[]{:S(2)}, u32[]{:S(2)}) async-start(f32[4,1664,128]{2,1,0:T(8,128)} %pad_maximum_fusion), calls=%async_computation.1 | async-start | bytes 6815744 | tf_op jit(solution)/shard_map/all_to_all | solution.py:267
  183.7 3.2 %add.642 = f32[128,48,128]{2,1,0:T(8,128)S(1)} add(f32[128,48,128]{2,1,0:T(8,128)} %get-tuple-element.49, f32[128,48,128]{2,1,0:T(8,128)} %collective-permute-done.12) | non-fusion elementwise | flops 786432 | bytes 9437184 | tf_op jit(solution)/shard_map/add | solution.py:334
  191.1 2.4 collective-permute-start.24
  193.5 3.8 %collective-permute-done.13 = f32[768,128]{1,0:T(8,128)S(1)} collective-permute-done((f32[768,128]{1,0:T(8,128)S(1)}, f32[768,128]{1,0:T(8,128)S(1)}, u32[]{:S(2)}, u32[]{:S(2)}) %collective-permute-start.13) | collective-permute-done | bytes 393248 | tf_op jit(solution)/shard_map/ppermute | solution.py:48
  197.3 2.6 collective-permute-done.15
  204.9 4.3 %collective-permute-done.22 = f32[1536,128]{1,0:T(8,128)} collective-permute-done((f32[1536,128]{1,0:T(8,128)S(1)}, f32[1536,128]{1,0:T(8,128)}, u32[]{:S(2)}, u32[]{:S(2)}) %collective-permute-start.22) | collective-permute-done | bytes 786464 | tf_op jit(solution)/shard_map/ppermute | solution.py:48
  210.7 6.7 %collective-permute-done.14 = f32[1536,128]{1,0:T(8,128)} collective-permute-done((f32[1536,128]{1,0:T(8,128)S(1)}, f32[1536,128]{1,0:T(8,128)}, u32[]{:S(2)}, u32[]{:S(2)}) %collective-permute-start.14) | collective-permute-done | bytes 786464 | tf_op jit(solution)/shard_map/ppermute | solution.py:48
  217.4 2.7 collective-permute-done.16
  234.3 4.5 %all-to-all-start.2 = ((f32[4,384,128]{2,1,0:T(8,128)}), f32[4,384,128]{2,1,0:T(8,128)S(1)}, u32[]{:S(2)}, u32[]{:S(2)}) async-start(f32[4,384,128]{2,1,0:T(8,128)} %bitcast.43), calls=%async_computation.2 | async-start | bytes 1572864 | tf_op jit(solution)/shard_map/all_to_all | solution.py:267
  242.9 11.8 %collective-permute-done.27 = f32[896,128]{1,0:T(8,128)} collective-permute-done((f32[896,128]{1,0:T(8,128)}, f32[896,128]{1,0:T(8,128)}, u32[]{:S(2)}, u32[]{:S(2)}) %collective-permute-start.27) | collective-permute-done | bytes 458784 | tf_op jit(solution)/shard_map/ppermute | solution.py:48
  254.6 11.7 %cholesky.19 = f32[128,128]{1,0:T(8,128)S(1)} custom-call(f32[128,128]{1,0:T(8,128)S(1)} %slice.186), custom_call_target="Cholesky" | custom-call | tf_op jit(solution)/shard_map/cholesky | solution.py:361
  269.8 5.1 %collective-permute-start.33 = (f32[384,128]{1,0:T(8,128)S(1)}, f32[384,128]{1,0:T(8,128)S(1)}, u32[]{:S(2)}, u32[]{:S(2)}) collective-permute-start(f32[384,128]{1,0:T(8,128)S(1)} %reduce_sum.39), channel_id=1, source_target_pairs={{0,0},{1,1},{2,32},{3,33},{4,64},{5,65},{6,96},{7,97},{8,8},{9,9},... | collective-permute-start | bytes 589832 | tf_op jit(solution)/shard_map/ppermute | solution.py:48
  276.5 6.1 %collective-permute-done.33 = f32[384,128]{1,0:T(8,128)S(1)} collective-permute-done((f32[384,128]{1,0:T(8,128)S(1)}, f32[384,128]{1,0:T(8,128)S(1)}, u32[]{:S(2)}, u32[]{:S(2)}) %collective-permute-start.33) | collective-permute-done | bytes 196640 | tf_op jit(solution)/shard_map/ppermute | solution.py:48
  284.4 9.8 %custom-call.5 = f32[1,128,128]{1,2,0:T(8,128)S(1)} custom-call(f32[1,128,128]{2,1,0:T(8,128)S(1)} %select_bitcast_fusion), custom_call_target="InvertDiagBlocksLowerTriangular" | custom-call | tf_op jit(solution)/shard_map/triangular_solve | solution.py:370
  294.2 2.5 collective-permute-start.32
  297.5 16.0 %collective-permute-done.32 = f32[1024,128]{1,0:T(8,128)S(1)} collective-permute-done((f32[1024,128]{1,0:T(8,128)S(1)}, f32[1024,128]{1,0:T(8,128)S(1)}, u32[]{:S(2)}, u32[]{:S(2)}) %collective-permute-start.32) | collective-permute-done | bytes 524320 | tf_op jit(solution)/shard_map/ppermute | solution.py:48
  (163 shorter events, 82.8 us)
Async XLA Ops:
  27.5 67.4 %all-to-all-start = ((f32[4,84,32,128]{3,2,1,0:T(8,128)}), f32[4,84,32,128]{3,2,1,0:T(8,128)}, u32[]{:S(2)}, u32[]{:S(2)}) async-start(f32[4,84,32,128]{3,2,1,0:T(8,128)} %get-tuple-element.36), calls=%async_computation | async-start | bytes 11010048 | tf_op jit(solution)/shard_map/all_to_all | solution.py:267
  32.6 65.0 %collective-permute-start.3 = (f32[96,48,128]{2,1,0:T(8,128)}, f32[96,48,128]{2,1,0:T(8,128)S(1)}, u32[]{:S(2)}, u32[]{:S(2)}) collective-permute-start(f32[96,48,128]{2,1,0:T(8,128)} %bitcast.130), channel_id=1, source_target_pairs={{0,1},{1,64},{2,3},{3,66},{4,5},{5,68},{6,7},{7,70},{8,9},{9,72},{... | collective-permute-start | bytes 7077896 | tf_op jit(solution)/shard_map/ppermute | solution.py:48
  32.7 66.0 %collective-permute-start.4 = (f32[96,48,128]{2,1,0:T(8,128)}, f32[96,48,128]{2,1,0:T(8,128)}, u32[]{:S(2)}, u32[]{:S(2)}) collective-permute-start(f32[96,48,128]{2,1,0:T(8,128)} %bitcast.129), channel_id=1, source_target_pairs={{0,65},{1,0},{2,67},{3,2},{4,69},{5,4},{6,71},{7,6},{8,73},{9,8},{... | collective-permute-start | bytes 7077896 | tf_op jit(solution)/shard_map/ppermute | solution.py:48
  34.1 68.0 %collective-permute-start.1 = (f32[96,48,128]{2,1,0:T(8,128)}, f32[96,48,128]{2,1,0:T(8,128)}, u32[]{:S(2)}, u32[]{:S(2)}) collective-permute-start(f32[96,48,128]{2,1,0:T(8,128)} %bitcast.128), channel_id=1, source_target_pairs={{0,2},{1,3},{2,4},{3,5},{4,6},{5,7},{6,0},{7,1},{8,10},{9,11},{10,... | collective-permute-start | bytes 7077896 | tf_op jit(solution)/shard_map/ppermute | solution.py:48
  35.4 70.1 %collective-permute-start.2 = (f32[96,48,128]{2,1,0:T(8,128)}, f32[96,48,128]{2,1,0:T(8,128)}, u32[]{:S(2)}, u32[]{:S(2)}) collective-permute-start(f32[96,48,128]{2,1,0:T(8,128)} %bitcast.127), channel_id=1, source_target_pairs={{0,6},{1,7},{2,0},{3,1},{4,2},{5,3},{6,4},{7,5},{8,14},{9,15},{10,... | collective-permute-start | bytes 7077896 | tf_op jit(solution)/shard_map/ppermute | solution.py:48
  95.9 13.2 %collective-permute-start = (f32[128,128]{1,0:T(8,128)S(1)}, f32[128,128]{1,0:T(8,128)S(1)}, u32[]{:S(2)}, u32[]{:S(2)}) collective-permute-start(f32[128,128]{1,0:T(8,128)S(1)} %bitcast.117), channel_id=1, source_target_pairs={{0,32},{1,33},{2,34},{3,35},{4,36},{5,37},{6,38},{7,39},{8,40},{9,... | collective-permute-start | bytes 196616 | tf_op jit(solution)/shard_map/ppermute | solution.py:48
  98.6 40.3 %collective-permute-start.7 = (f32[32,48,128]{2,1,0:T(8,128)}, f32[32,48,128]{2,1,0:T(8,128)S(1)}, u32[]{:S(2)}, u32[]{:S(2)}) collective-permute-start(f32[32,48,128]{2,1,0:T(8,128)} %slice.198), channel_id=1, source_target_pairs={{0,1},{1,64},{2,3},{3,66},{4,5},{5,68},{6,7},{7,70},{8,9},{9,72},{... | collective-permute-start | bytes 2359304 | tf_op jit(solution)/shard_map/ppermute | solution.py:48
  100.7 38.3 %collective-permute-start.8 = (f32[32,48,128]{2,1,0:T(8,128)}, f32[32,48,128]{2,1,0:T(8,128)}, u32[]{:S(2)}, u32[]{:S(2)}) collective-permute-start(f32[32,48,128]{2,1,0:T(8,128)} %slice.199), channel_id=1, source_target_pairs={{0,65},{1,0},{2,67},{3,2},{4,69},{5,4},{6,71},{7,6},{8,73},{9,8},{... | collective-permute-start | bytes 2359304 | tf_op jit(solution)/shard_map/ppermute | solution.py:48
  104.3 34.8 %collective-permute-start.5 = (f32[32,48,128]{2,1,0:T(8,128)}, f32[32,48,128]{2,1,0:T(8,128)}, u32[]{:S(2)}, u32[]{:S(2)}) collective-permute-start(f32[32,48,128]{2,1,0:T(8,128)} %slice.196), channel_id=1, source_target_pairs={{0,2},{1,3},{2,4},{3,5},{4,6},{5,7},{6,0},{7,1},{8,10},{9,11},{10,... | collective-permute-start | bytes 2359304 | tf_op jit(solution)/shard_map/ppermute | solution.py:48
  107.6 31.4 %collective-permute-start.6 = (f32[32,48,128]{2,1,0:T(8,128)}, f32[32,48,128]{2,1,0:T(8,128)}, u32[]{:S(2)}, u32[]{:S(2)}) collective-permute-start(f32[32,48,128]{2,1,0:T(8,128)} %slice.197), channel_id=1, source_target_pairs={{0,6},{1,7},{2,0},{3,1},{4,2},{5,3},{6,4},{7,5},{8,14},{9,15},{10,... | collective-permute-start | bytes 2359304 | tf_op jit(solution)/shard_map/ppermute | solution.py:48
  126.2 12.8 %collective-permute-start.9 = (f32[128,128]{1,0:T(8,128)S(1)}, f32[128,128]{1,0:T(8,128)S(1)}, u32[]{:S(2)}, u32[]{:S(2)}) collective-permute-start(f32[128,128]{1,0:T(8,128)S(1)} %bitcast_add_fusion.4), channel_id=1, source_target_pairs={{0,1},{1,64},{2,3},{3,66},{4,5},{5,68},{6,7},{7,70},{8,9},{9,72},{... | collective-permute-start | bytes 196616 | tf_op jit(solution)/shard_map/ppermute | solution.py:48
  159.0 24.8 %collective-permute-start.12 = (f32[128,48,128]{2,1,0:T(8,128)}, f32[128,48,128]{2,1,0:T(8,128)}, u32[]{:S(2)}, u32[]{:S(2)}) collective-permute-start(f32[128,48,128]{2,1,0:T(8,128)} %get-tuple-element.50), channel_id=1, source_target_pairs={{0,32},{1,33},{2,34},{3,35},{4,36},{5,37},{6,38},{7,39},{8,40},{9,... | collective-permute-start | bytes 9437192 | tf_op jit(solution)/shard_map/ppermute | solution.py:48
  174.3 15.0 %collective-permute-start.21 = (f32[768,128]{1,0:T(8,128)S(1)}, f32[768,128]{1,0:T(8,128)S(1)}, u32[]{:S(2)}, u32[]{:S(2)}) collective-permute-start(f32[768,128]{1,0:T(8,128)S(1)} %get-tuple-element.75), channel_id=1, source_target_pairs={{0,8},{1,9},{2,10},{3,11},{4,12},{5,13},{6,14},{7,15},{8,16},{9,17... | collective-permute-start | bytes 1179656 | tf_op jit(solution)/shard_map/ppermute | solution.py:48
  174.8 14.6 %collective-permute-start.23 = (f32[768,128]{1,0:T(8,128)S(1)}, f32[768,128]{1,0:T(8,128)S(1)}, u32[]{:S(2)}, u32[]{:S(2)}) collective-permute-start(f32[768,128]{1,0:T(8,128)S(1)} %get-tuple-element.76), channel_id=1, source_target_pairs={{0,24},{1,25},{2,26},{3,27},{4,28},{5,29},{6,30},{7,31},{8,0},{9,1... | collective-permute-start | bytes 1179656 | tf_op jit(solution)/shard_map/ppermute | solution.py:48
  179.0 44.3 %all-to-all-start.1 = ((f32[4,1664,128]{2,1,0:T(8,128)}), f32[4,1664,128]{2,1,0:T(8,128)}, u32[]{:S(2)}, u32[]{:S(2)}) async-start(f32[4,1664,128]{2,1,0:T(8,128)} %pad_maximum_fusion), calls=%async_computation.1 | async-start | bytes 6815744 | tf_op jit(solution)/shard_map/all_to_all | solution.py:267
  190.6 18.6 %collective-permute-start.22 = (f32[1536,128]{1,0:T(8,128)S(1)}, f32[1536,128]{1,0:T(8,128)}, u32[]{:S(2)}, u32[]{:S(2)}) collective-permute-start(f32[1536,128]{1,0:T(8,128)S(1)} %pad_maximum_fusion.15), channel_id=1, source_target_pairs={{0,8},{1,9},{2,10},{3,11},{4,12},{5,13},{6,14},{7,15},{8,16},{9,17... | collective-permute-start | bytes 2359304 | tf_op jit(solution)/shard_map/ppermute | solution.py:48
  191.1 18.2 %collective-permute-start.24 = (f32[1536,128]{1,0:T(8,128)S(1)}, f32[1536,128]{1,0:T(8,128)}, u32[]{:S(2)}, u32[]{:S(2)}) collective-permute-start(f32[1536,128]{1,0:T(8,128)S(1)} %pad_maximum_fusion.16), channel_id=1, source_target_pairs={{0,24},{1,25},{2,26},{3,27},{4,28},{5,29},{6,30},{7,31},{8,0},{9,1... | collective-permute-start | bytes 2359304 | tf_op jit(solution)/shard_map/ppermute | solution.py:48
  200.1 17.3 %collective-permute-start.14 = (f32[1536,128]{1,0:T(8,128)S(1)}, f32[1536,128]{1,0:T(8,128)}, u32[]{:S(2)}, u32[]{:S(2)}) collective-permute-start(f32[1536,128]{1,0:T(8,128)S(1)} %pad_maximum_fusion.13), channel_id=1, source_target_pairs={{0,1},{1,64},{2,3},{3,66},{4,5},{5,68},{6,7},{7,70},{8,9},{9,72},{... | collective-permute-start | bytes 2359304 | tf_op jit(solution)/shard_map/ppermute | solution.py:48
  201.4 18.7 %collective-permute-start.16 = (f32[1536,128]{1,0:T(8,128)}, f32[1536,128]{1,0:T(8,128)}, u32[]{:S(2)}, u32[]{:S(2)}) collective-permute-start(f32[1536,128]{1,0:T(8,128)} %pad_maximum_fusion.14), channel_id=1, source_target_pairs={{0,65},{1,0},{2,67},{3,2},{4,69},{5,4},{6,71},{7,6},{8,73},{9,8},{... | collective-permute-start | bytes 2359304 | tf_op jit(solution)/shard_map/ppermute | solution.py:48
  228.5 14.4 %collective-permute-start.25 = (f32[896,128]{1,0:T(8,128)}, f32[896,128]{1,0:T(8,128)}, u32[]{:S(2)}, u32[]{:S(2)}) collective-permute-start(f32[896,128]{1,0:T(8,128)} %get-tuple-element.98), channel_id=1, source_target_pairs={{0,1},{1,64},{2,3},{3,66},{4,5},{5,68},{6,7},{7,70},{8,9},{9,72},{... | collective-permute-start | bytes 1376264 | tf_op jit(solution)/shard_map/ppermute | solution.py:48
  231.8 22.9 %collective-permute-start.27 = (f32[896,128]{1,0:T(8,128)}, f32[896,128]{1,0:T(8,128)}, u32[]{:S(2)}, u32[]{:S(2)}) collective-permute-start(f32[896,128]{1,0:T(8,128)} %get-tuple-element.103), channel_id=1, source_target_pairs={{0,65},{1,0},{2,67},{3,2},{4,69},{5,4},{6,71},{7,6},{8,73},{9,8},{... | collective-permute-start | bytes 1376264 | tf_op jit(solution)/shard_map/ppermute | solution.py:48
  234.3 34.9 %all-to-all-start.2 = ((f32[4,384,128]{2,1,0:T(8,128)}), f32[4,384,128]{2,1,0:T(8,128)S(1)}, u32[]{:S(2)}, u32[]{:S(2)}) async-start(f32[4,384,128]{2,1,0:T(8,128)} %bitcast.43), calls=%async_computation.2 | async-start | bytes 1572864 | tf_op jit(solution)/shard_map/all_to_all | solution.py:267
  269.2 15.0 %collective-permute-start.31 = (f32[640,128]{1,0:T(8,128)S(1)}, f32[640,128]{1,0:T(8,128)S(1)}, u32[]{:S(2)}, u32[]{:S(2)}) collective-permute-start(f32[640,128]{1,0:T(8,128)S(1)} %concatenate.68), channel_id=1, source_target_pairs={{0,32},{1,33},{2,34},{3,35},{4,36},{5,37},{6,38},{7,39},{8,40},{9,... | collective-permute-start | bytes 983048 | tf_op jit(solution)/shard_map/ppermute | solution.py:48
  294.2 19.2 %collective-permute-start.32 = (f32[1024,128]{1,0:T(8,128)S(1)}, f32[1024,128]{1,0:T(8,128)S(1)}, u32[]{:S(2)}, u32[]{:S(2)}) collective-permute-start(f32[1024,128]{1,0:T(8,128)S(1)} %pad_maximum_fusion.20), channel_id=1, source_target_pairs={{0,0},{1,1},{2,2},{3,3},{4,4},{5,5},{6,6},{7,7},{8,32},{9,33},{10,... | collective-permute-start | bytes 1572872 | tf_op jit(solution)/shard_map/ppermute | solution.py:48
  (27 other events, 303.7 us)

commit v6 on v5

--- a/solution.py
+++ b/solution.py
@@ -208,9 +208,13 @@
             return carry
 
         lax.fori_loop(0, 4, rows, 0)
-
-
-def make_expands(pos, places, tables, at_near, own, behind, ahead):
+    for i in range(4):
+        total = chunks_y[0, 80 + i] + chunks_y[1, 80 + i] + chunks_y[2, 80 + i] + chunks_y[3, 80 + i]
+        keep[144 + i] = total
+        away[144 + i] = total
+
+
+def make_expands(pos, places, tables, own, behind, ahead):
     vmem = pl.BlockSpec(memory_space=pltpu.VMEM)
     smem = pl.BlockSpec(memory_space=pltpu.SMEM)
     params = pltpu.CompilerParams(vmem_limit_bytes=EXPAND_VMEM)
@@ -227,14 +231,14 @@
         compiler_params=params,
         cost_estimate=cost,
         name="expand_near",
-    )(at_near, tables["x"][1], *tables["z"], *(v[flow] for flow in "xz" for v in (own, behind, ahead)))
+    )(*tables["x"], *tables["z"], *(v[flow] for flow in "xz" for v in (own, behind, ahead)))
 
     def rest(chunks_y, far_x, far_z):
         return pl.pallas_call(
             expand_rest,
             in_specs=[smem] * 8 + [vmem] * 7,
             out_specs=[vmem] * 6,
-            out_shape=[pieces(144, "y")] * 2 + [pieces(128, "x")] * 2 + [pieces(128, "z")] * 2,
+            out_shape=[pieces(148, "y")] * 2 + [pieces(128, "x")] * 2 + [pieces(128, "z")] * 2,
             compiler_params=params,
             cost_estimate=cost,
             name="expand_rest",
@@ -314,10 +318,6 @@
 
     slots = make_updates(pos, panel, front, parent_front)
     chunks_y = trade(slots["y"], Y_GROUPS)
-    pivot_block = jnp.sum(chunks_y[:, 80:84], axis=0).reshape(BLK, BLK)
-    pivot_block = pivot_block + send(pivot_block, SIBLING)
-    at_near, pivot_block = lax.optimization_barrier((tables["x"][0], pivot_block))
-    pivot_block = pivot_block + sum(arrivals([pivot_block] * 4, "z"))
     own, behind, ahead, far = {}, {}, {}, {}
     for flow in "xz":
         own[flow], plus, minus = slots[flow]
@@ -327,14 +327,13 @@
             send(behind[flow][64:96], along(flow, 1)),
             send(ahead[flow][64:96], along(flow, -1)),
         )
-    far_z, pivot_block = lax.optimization_barrier((far["z"], pivot_block))
-    rest = make_expands(pos, places, tables, at_near, own, behind, ahead)
-    keep_y, away_y, keep_x, away_x, keep_z, away_z = rest(chunks_y, far["x"], far_z)
-    halves_y = (keep_y + send(away_y, SIBLING)).reshape(144 * 32, BLK)
+    rest = make_expands(pos, places, tables, own, behind, ahead)
+    keep_y, away_y, keep_x, away_x, keep_z, away_z = rest(chunks_y, far["x"], far["z"])
+    halves_y = (keep_y + send(away_y, SIBLING)).reshape(148 * 32, BLK)
     halves_x = (keep_x + send(away_x, SIBLING)).reshape(4, 32 * 48, BLK)
     halves_z = (keep_z + send(away_z, SIBLING)).reshape(4, 32 * 48, BLK)
 
-    pivot_rows = halves_y[128 * 32 :]
+    pivot_rows, pivot_block = halves_y[128 * 32 : 144 * 32], halves_y[144 * 32 :]
     mine = lax.dynamic_slice_in_dim(parent_front, 512 * core, 512, 0)
     theirs = lax.dynamic_slice_in_dim(parent_front, 512 * (1 - core), 512, 0)
     pivot_rows = pivot_rows + send(mine, PARENT) + send(theirs, PARENT_SIBLING)
@@ -349,27 +348,23 @@
     sum_x, sum_y, sum_z = lax.optimization_barrier((sum_x, sum_y, sum_z))
 
     rhs_mine = jnp.where((leaf == 0) & (col % 2 == 0), right_sides[0:BLK], 0.0)
-    pivot_block = sum_y[quarter + 512 :]
-    extra = jnp.concatenate([sum_y[quarter : quarter + 512], rhs_mine])
+    extra = jnp.concatenate([sum_y[quarter:], rhs_mine])
     slots_y = [jnp.concatenate([sum_y[k * 256 : (k + 1) * 256], extra]) for k in range(4)]
     slots_z = [sum_z[k * 384 : (k + 1) * 384] for k in range(4)]
-    from_z = arrivals(slots_y, "z")
-    from_z, pivot_block = lax.optimization_barrier((from_z, pivot_block))
-    sum_y = slots_y[0] + sum(from_z)
+    sum_y = slots_y[0] + sum(arrivals(slots_y, "z"))
     sum_x = jnp.sum(trade(sum_x.reshape(4, 384, BLK), Y_GROUPS), axis=0)
     sum_z = slots_z[0] + sum(arrivals(slots_z, "x"))
-    lower = jnp.tril(lax.linalg.cholesky(pivot_block, symmetrize_input=False))
-    sum_x, sum_y, sum_z, lower = lax.optimization_barrier((sum_x, sum_y, sum_z, lower))
-    rhs_rows = sum_y[768:896]
+    sum_x, sum_y, sum_z = lax.optimization_barrier((sum_x, sum_y, sum_z))
+    pivot_block, rhs_rows = sum_y[768:896], sum_y[896:1024]
     strip_x = send(sum_x, TURN).reshape(8, 48, BLK)
     strip_z = send(sum_z, SWAP).reshape(8, 48, BLK)
 
     mine = jnp.concatenate([sum_y[256 : 256 + 512], rhs_rows])
     other = send(mine, SIBLING)
-    lower, other = lax.optimization_barrier((lower, other))
-    inverse = lax.linalg.triangular_solve(
-        lower, jnp.eye(BLK, dtype=jnp.float32), left_side=True, lower=True
-    )
+    pivot_block, strip_x, strip_z, other = lax.optimization_barrier(
+        (pivot_block, strip_x, strip_z, other)
+    )
+    lower = jnp.tril(lax.linalg.cholesky(pivot_block, symmetrize_input=False))
     low, high = jnp.where(core == 0, mine, other), jnp.where(core == 0, other, mine)
     in_range = jnp.concatenate([low[0:512], high[0:512]])
     rhs_rows = low[512:]
@@ -377,6 +372,10 @@
         in_range.reshape(8, BLK, BLK), col % 8, 0, keepdims=False
     )
     my_rows = send(in_range, RANGE)
+    lower, my_rows = lax.optimization_barrier((lower, my_rows))
+    inverse = lax.linalg.triangular_solve(
+        lower, jnp.eye(BLK, dtype=jnp.float32), left_side=True, lower=True
+    )
 
     strip_y = sum_y[0:256].reshape(8, 32, BLK)
     assembled = jnp.concatenate([strip_x, strip_z, strip_y], axis=1).reshape(1024, BLK)

time: 318 us -> 283 us (0.89); the launches traced: 317 us -> 278 us
  waiting for transfers between devices: 133 us -> 95.6 us
  local copies, waits for them, and re-layouts: 20.3 us -> 15.7 us
  starting transfers between devices: 54 us -> 57.4 us
    all_to_all x3, waiting for transfers between devices: 56.5 us -> 0.83 us  [trade(): lax.all_to_all(value, 'col', 0, 0, axis_index_groups=groups, tiled=True)]
    ppermute x35 -> x31, waiting for transfers between devices: 76.6 us -> 94.8 us  [send(): return lax.ppermute(value, AXES, pairs)]
    ppermute x35 -> x31, starting transfers between devices: 39.7 us -> 41.9 us  [send(): return lax.ppermute(value, AXES, pairs)]
    unnamed x27 -> x29, local copies, waits for them, and re-layouts: 6.82 us -> 5.92 us
  transfers between devices with their start and end apart: 38 -> 34, of which waited for: 14 -> 13; matrix products, arithmetic and copies ran while one was open for 16% -> 17% of each run, Pallas kernels for 4% -> 4%
where the time goes in v6:
time: 283 us; the launch traced here: 278 us
  waiting for transfers between devices  95.6 us (34%)
  starting transfers between devices  57.4 us (20%)
  Pallas kernels  53.4 us (19%)
  other arithmetic  50.3 us (18%)
  local copies, waits for them, and re-layouts  15.7 us (6%)
  matrix products  4.09 us (1%)
    ppermute x31, waiting for transfers between devices, send(): return lax.ppermute(value, AXES, pairs)  94.8 us
    ppermute x31, starting transfers between devices, send(): return lax.ppermute(value, AXES, pairs)  41.9 us
    pallas_call x1, Pallas kernels, make_updates(): pl.pallas_call(update, grid_spec=pltpu.PrefetchScalarGridSpec(num_scalar_...  24.3 us
    pallas_call x1, Pallas kernels, rest(): pl.pallas_call(expand_rest, in_specs=[smem] * 8 + [vmem] * 7, out_specs=[...  17.3 us
    all_to_all x3, starting transfers between devices, trade(): lax.all_to_all(value, 'col', 0, 0, axis_index_groups=groups, tiled=True)  15.5 us
    another operation x3, other arithmetic, per_device(): lower = jnp.tril(lax.linalg.cholesky(pivot_block, symmetrize_input=False))  12.4 us
    pallas_call x1, Pallas kernels, make_expands(): pl.pallas_call(expand_near, in_specs=[smem] * 4 + [vmem] * 6, out_specs=[...  11.7 us
    another operation x2, other arithmetic, per_device(): lax.linalg.triangular_solve(lower, jnp.eye(BLK, dtype=jnp.float32), left_...  9.82 us
  transfers between devices with their start and end apart: 34, of which 13 were waited for; matrix products, arithmetic and copies ran while one was open for 17% of the time, Pallas kernels for 4%

profile of v6, /device:TPU:97, one launch (start us, length us, event | category | flops | bytes accessed | tf_op | source)
XLA Modules:
  0.0 278.1 jit_solution(1976100852686796735)
XLA Ops:
  3.2 24.3 %update.1 = (f32[4,16,48,128]{3,2,1,0:T(8,128)}, f32[6,16,48,128]{3,2,1,0:T(8,128)}, f32[6,16,48,128]{3,2,1,0:T(8,128)}, f32[4,16,48,128]{3,2,1,0:T(8,128)}, f32...) custom-call(s32[6]{0:T(128)S(1)} %stack.71.pos, bf16[16,128,1536]{2,1,0:T(8,128)(2,1)} %bitcast.121, ...), custom_call_target="tpu_custom_call" | custom-call | flops 12884901888 | bytes 41943040 | tf_op jit(solution)/shard_map/update/pallas_call | solution.py:98
  27.5 5.1 %all-to-all-start = ((f32[4,84,32,128]{3,2,1,0:T(8,128)}), f32[4,84,32,128]{3,2,1,0:T(8,128)}, u32[]{:S(2)}, u32[]{:S(2)}) async-start(f32[4,84,32,128]{3,2,1,0:T(8,128)} %get-tuple-element.30), calls=%async_computation | async-start | bytes 11010048 | tf_op jit(solution)/shard_map/all_to_all | solution.py:271
  39.3 47.1 %collective-permute-done.refs_1_ = f32[96,48,128]{2,1,0:T(8,128)S(1)} collective-permute-done((f32[96,48,128]{2,1,0:T(8,128)}, f32[96,48,128]{2,1,0:T(8,128)S(1)}, u32[]{:S(2)}, u32[]{:S(2)}) %collective-permute-start) | collective-permute-done | bytes 2359328 | tf_op jit(solution)/shard_map/ppermute | solution.py:48
  96.3 11.7 %expand_near.1 = (f32[256,48,128]{2,1,0:T(8,128)}, f32[256,48,128]{2,1,0:T(8,128)}) custom-call(s32[4,16]{1,0:T(4,128)} %get-tuple-element.59.at_x, s32[4,4]{1,0:T(4,128)} %constant_dynamic-slice_fusion.7.down_x, s32[4,16]{1,0:T(4,128)} %get-tuple-element.57.at_z, s32[4,4]{1,0:T(4,128)} %constant_dynamic-slice_fusion.2.down_z, f32[64,48,128]{2,1,0:T(8,128)} %bitcast.108, ...), custom_call_target="tpu_custom_call" | custom-call | flops 8388608 | bytes 31457280 | tf_op jit(solution)/shard_map/expand_near/pallas_call | solution.py:226
  108.8 2.5 collective-permute-done.7.refs_5_
  111.3 17.3 %expand_rest.1 = (f32[148,32,128]{2,1,0:T(8,128)}, f32[148,32,128]{2,1,0:T(8,128)}, f32[128,48,128]{2,1,0:T(8,128)}, f32[128,48,128]{2,1,0:T(8,128)}, f32[128,48,128]{2,1,0:T(8,128)}, /*index=5*/f32[128,48,128]{2,1,0:T(8,128)}) custom-call(s32[6]{0:T(128)} %copy-done.2, s32[4,32]{1,0:T(4,128)} %broadcast_add_fusion.places, s32[4,8]{1,0:T(4,128)} %fusion.29.at_y, ...), custom_call_target="tpu_custom_call" | custom-call | flops 8388608 | bytes 31457280 | tf_op jit(solution)/shard_map/expand_rest/pallas_call | solution.py:237
  128.6 3.0 %collective-permute-start.13 = (f32[148,32,128]{2,1,0:T(8,128)}, f32[148,32,128]{2,1,0:T(8,128)S(1)}, u32[]{:S(2)}, u32[]{:S(2)}) collective-permute-start(f32[148,32,128]{2,1,0:T(8,128)} %get-tuple-element.42), channel_id=1, source_target_pairs={{0,32},{1,33},{2,34},{3,35},{4,36},{5,37},{6,38},{7,39},{8,40},{9,... | collective-permute-start | bytes 7274504 | tf_op jit(solution)/shard_map/ppermute | solution.py:48
  133.7 4.9 %collective-permute-done.13 = f32[148,32,128]{2,1,0:T(8,128)S(1)} collective-permute-done((f32[148,32,128]{2,1,0:T(8,128)}, f32[148,32,128]{2,1,0:T(8,128)S(1)}, u32[]{:S(2)}, u32[]{:S(2)}) %collective-permute-start.13) | collective-permute-done | bytes 2424864 | tf_op jit(solution)/shard_map/ppermute | solution.py:48
  152.0 4.7 %all-to-all-start.1 = ((f32[4,1664,128]{2,1,0:T(8,128)}), f32[4,1664,128]{2,1,0:T(8,128)}, u32[]{:S(2)}, u32[]{:S(2)}) async-start(f32[4,1664,128]{2,1,0:T(8,128)} %pad_maximum_fusion), calls=%async_computation.1 | async-start | bytes 6815744 | tf_op jit(solution)/shard_map/all_to_all | solution.py:271
  156.8 3.2 %add.626 = f32[128,48,128]{2,1,0:T(8,128)S(1)} add(f32[128,48,128]{2,1,0:T(8,128)} %get-tuple-element.39, f32[128,48,128]{2,1,0:T(8,128)} %collective-permute-done.8) | non-fusion elementwise | flops 786432 | bytes 9437184 | tf_op jit(solution)/shard_map/add | solution.py:333
  164.6 2.4 collective-permute-start.20
  167.0 4.3 %collective-permute-done.11 = f32[768,128]{1,0:T(8,128)S(1)} collective-permute-done((f32[768,128]{1,0:T(8,128)S(1)}, f32[768,128]{1,0:T(8,128)S(1)}, u32[]{:S(2)}, u32[]{:S(2)}) %collective-permute-start.11) | collective-permute-done | bytes 393248 | tf_op jit(solution)/shard_map/ppermute | solution.py:48
  171.5 2.4 collective-permute-start.10
  177.2 5.9 %collective-permute-done.18 = f32[1536,128]{1,0:T(8,128)} collective-permute-done((f32[1536,128]{1,0:T(8,128)S(1)}, f32[1536,128]{1,0:T(8,128)}, u32[]{:S(2)}, u32[]{:S(2)}) %collective-permute-start.18) | collective-permute-done | bytes 786464 | tf_op jit(solution)/shard_map/ppermute | solution.py:48
  184.6 4.2 %collective-permute-done.10 = f32[1536,128]{1,0:T(8,128)} collective-permute-done((f32[1536,128]{1,0:T(8,128)S(1)}, f32[1536,128]{1,0:T(8,128)}, u32[]{:S(2)}, u32[]{:S(2)}) %collective-permute-start.10) | collective-permute-done | bytes 786464 | tf_op jit(solution)/shard_map/ppermute | solution.py:48
  188.8 4.4 %collective-permute-done.12 = f32[1536,128]{1,0:T(8,128)} collective-permute-done((f32[1536,128]{1,0:T(8,128)}, f32[1536,128]{1,0:T(8,128)}, u32[]{:S(2)}, u32[]{:S(2)}) %collective-permute-start.12) | collective-permute-done | bytes 786464 | tf_op jit(solution)/shard_map/ppermute | solution.py:48
  201.1 3.2 %collective-permute-start.22 = (f32[1024,128]{1,0:T(8,128)}, f32[1024,128]{1,0:T(8,128)}, u32[]{:S(2)}, u32[]{:S(2)}) collective-permute-start(f32[1024,128]{1,0:T(8,128)} %get-tuple-element.87), channel_id=1, source_target_pairs={{0,64},{1,65},{2,66},{3,67},{4,68},{5,69},{6,70},{7,71},{8,72},{9,... | collective-permute-start | bytes 1572872 | tf_op jit(solution)/shard_map/ppermute | solution.py:48
  206.8 5.7 %all-to-all-start.2 = ((f32[4,384,128]{2,1,0:T(8,128)}), f32[4,384,128]{2,1,0:T(8,128)S(1)}, u32[]{:S(2)}, u32[]{:S(2)}) async-start(f32[4,384,128]{2,1,0:T(8,128)} %bitcast.43), calls=%async_computation.2 | async-start | bytes 1572864 | tf_op jit(solution)/shard_map/all_to_all | solution.py:271
  215.3 12.9 %collective-permute-done.23 = f32[1024,128]{1,0:T(8,128)} collective-permute-done((f32[1024,128]{1,0:T(8,128)}, f32[1024,128]{1,0:T(8,128)}, u32[]{:S(2)}, u32[]{:S(2)}) %collective-permute-start.23) | collective-permute-done | bytes 524320 | tf_op jit(solution)/shard_map/ppermute | solution.py:48
  231.0 5.4 %collective-permute-start.27 = (f32[384,128]{1,0:T(8,128)}, f32[384,128]{1,0:T(8,128)S(1)}, u32[]{:S(2)}, u32[]{:S(2)}) collective-permute-start(f32[384,128]{1,0:T(8,128)} %reduce_sum.29), channel_id=1, source_target_pairs={{0,0},{1,1},{2,32},{3,33},{4,64},{5,65},{6,96},{7,97},{8,8},{9,9},... | collective-permute-start | bytes 589832 | tf_op jit(solution)/shard_map/ppermute | solution.py:48
  238.0 6.0 %collective-permute-done.27 = f32[384,128]{1,0:T(8,128)S(1)} collective-permute-done((f32[384,128]{1,0:T(8,128)}, f32[384,128]{1,0:T(8,128)S(1)}, u32[]{:S(2)}, u32[]{:S(2)}) %collective-permute-start.27) | collective-permute-done | bytes 196640 | tf_op jit(solution)/shard_map/ppermute | solution.py:48
  244.8 4.4 %collective-permute-start.30 = (f32[1024,128]{1,0:T(8,128)S(1)}, f32[1024,128]{1,0:T(8,128)S(1)}, u32[]{:S(2)}, u32[]{:S(2)}) collective-permute-start(f32[1024,128]{1,0:T(8,128)S(1)} %pad_maximum_fusion.20), channel_id=1, source_target_pairs={{0,0},{1,1},{2,2},{3,3},{4,4},{5,5},{6,6},{7,7},{8,32},{9,33},{10,... | collective-permute-start | bytes 1572872 | tf_op jit(solution)/shard_map/ppermute | solution.py:48
  249.3 11.7 %cholesky.19 = f32[128,128]{1,0:T(8,128)S(1)} custom-call(f32[128,128]{1,0:T(8,128)S(1)} %get-tuple-element.51), custom_call_target="Cholesky" | custom-call | tf_op jit(solution)/shard_map/cholesky | solution.py:367
  264.2 9.8 %custom-call.5 = f32[1,128,128]{1,2,0:T(8,128)S(1)} custom-call(f32[1,128,128]{2,1,0:T(8,128)S(1)} %select_bitcast_fusion), custom_call_target="InvertDiagBlocksLowerTriangular" | custom-call | tf_op jit(solution)/shard_map/triangular_solve | solution.py:376
  (156 shorter events, 69.8 us)
Async XLA Ops:
  27.5 83.8 %all-to-all-start = ((f32[4,84,32,128]{3,2,1,0:T(8,128)}), f32[4,84,32,128]{3,2,1,0:T(8,128)}, u32[]{:S(2)}, u32[]{:S(2)}) async-start(f32[4,84,32,128]{3,2,1,0:T(8,128)} %get-tuple-element.30), calls=%async_computation | async-start | bytes 11010048 | tf_op jit(solution)/shard_map/all_to_all | solution.py:271
  32.6 53.7 %collective-permute-start = (f32[96,48,128]{2,1,0:T(8,128)}, f32[96,48,128]{2,1,0:T(8,128)S(1)}, u32[]{:S(2)}, u32[]{:S(2)}) collective-permute-start(f32[96,48,128]{2,1,0:T(8,128)} %bitcast.125), channel_id=1, source_target_pairs={{0,2},{1,3},{2,4},{3,5},{4,6},{5,7},{6,0},{7,1},{8,10},{9,11},{10,... | collective-permute-start | bytes 7077896 | tf_op jit(solution)/shard_map/ppermute | solution.py:48
  33.9 52.6 %collective-permute-start.1 = (f32[96,48,128]{2,1,0:T(8,128)}, f32[96,48,128]{2,1,0:T(8,128)}, u32[]{:S(2)}, u32[]{:S(2)}) collective-permute-start(f32[96,48,128]{2,1,0:T(8,128)} %bitcast.124), channel_id=1, source_target_pairs={{0,6},{1,7},{2,0},{3,1},{4,2},{5,3},{6,4},{7,5},{8,14},{9,15},{10,... | collective-permute-start | bytes 7077896 | tf_op jit(solution)/shard_map/ppermute | solution.py:48
  35.4 55.0 %collective-permute-start.2 = (f32[96,48,128]{2,1,0:T(8,128)}, f32[96,48,128]{2,1,0:T(8,128)}, u32[]{:S(2)}, u32[]{:S(2)}) collective-permute-start(f32[96,48,128]{2,1,0:T(8,128)} %bitcast.123), channel_id=1, source_target_pairs={{0,1},{1,64},{2,3},{3,66},{4,5},{5,68},{6,7},{7,70},{8,9},{9,72},{... | collective-permute-start | bytes 7077896 | tf_op jit(solution)/shard_map/ppermute | solution.py:48
  35.4 56.3 %collective-permute-start.3 = (f32[96,48,128]{2,1,0:T(8,128)}, f32[96,48,128]{2,1,0:T(8,128)}, u32[]{:S(2)}, u32[]{:S(2)}) collective-permute-start(f32[96,48,128]{2,1,0:T(8,128)} %bitcast.122), channel_id=1, source_target_pairs={{0,65},{1,0},{2,67},{3,2},{4,69},{5,4},{6,71},{7,6},{8,73},{9,8},{... | collective-permute-start | bytes 7077896 | tf_op jit(solution)/shard_map/ppermute | solution.py:48
  86.4 21.6 %collective-permute-start.4 = (f32[32,48,128]{2,1,0:T(8,128)S(1)}, f32[32,48,128]{2,1,0:T(8,128)S(1)}, u32[]{:S(2)}, u32[]{:S(2)}) collective-permute-start(f32[32,48,128]{2,1,0:T(8,128)S(1)} %slice.204), channel_id=1, source_target_pairs={{0,2},{1,3},{2,4},{3,5},{4,6},{5,7},{6,0},{7,1},{8,10},{9,11},{10,... | collective-permute-start | bytes 2359304 | tf_op jit(solution)/shard_map/ppermute | solution.py:48
  88.2 19.7 %collective-permute-start.5 = (f32[32,48,128]{2,1,0:T(8,128)S(1)}, f32[32,48,128]{2,1,0:T(8,128)}, u32[]{:S(2)}, u32[]{:S(2)}) collective-permute-start(f32[32,48,128]{2,1,0:T(8,128)S(1)} %slice.205), channel_id=1, source_target_pairs={{0,6},{1,7},{2,0},{3,1},{4,2},{5,3},{6,4},{7,5},{8,14},{9,15},{10,... | collective-permute-start | bytes 2359304 | tf_op jit(solution)/shard_map/ppermute | solution.py:48
  91.6 17.2 %collective-permute-start.6 = (f32[32,48,128]{2,1,0:T(8,128)S(1)}, f32[32,48,128]{2,1,0:T(8,128)}, u32[]{:S(2)}, u32[]{:S(2)}) collective-permute-start(f32[32,48,128]{2,1,0:T(8,128)S(1)} %slice.206), channel_id=1, source_target_pairs={{0,1},{1,64},{2,3},{3,66},{4,5},{5,68},{6,7},{7,70},{8,9},{9,72},{... | collective-permute-start | bytes 2359304 | tf_op jit(solution)/shard_map/ppermute | solution.py:48
  92.9 18.4 %collective-permute-start.7 = (f32[32,48,128]{2,1,0:T(8,128)S(1)}, f32[32,48,128]{2,1,0:T(8,128)}, u32[]{:S(2)}, u32[]{:S(2)}) collective-permute-start(f32[32,48,128]{2,1,0:T(8,128)S(1)} %slice.207), channel_id=1, source_target_pairs={{0,65},{1,0},{2,67},{3,2},{4,69},{5,4},{6,71},{7,6},{8,73},{9,8},{... | collective-permute-start | bytes 2359304 | tf_op jit(solution)/shard_map/ppermute | solution.py:48
  131.7 25.0 %collective-permute-start.8 = (f32[128,48,128]{2,1,0:T(8,128)}, f32[128,48,128]{2,1,0:T(8,128)}, u32[]{:S(2)}, u32[]{:S(2)}) collective-permute-start(f32[128,48,128]{2,1,0:T(8,128)} %get-tuple-element.40), channel_id=1, source_target_pairs={{0,32},{1,33},{2,34},{3,35},{4,36},{5,37},{6,38},{7,39},{8,40},{9,... | collective-permute-start | bytes 9437192 | tf_op jit(solution)/shard_map/ppermute | solution.py:48
  147.2 15.7 %collective-permute-start.17 = (f32[768,128]{1,0:T(8,128)S(1)}, f32[768,128]{1,0:T(8,128)S(1)}, u32[]{:S(2)}, u32[]{:S(2)}) collective-permute-start(f32[768,128]{1,0:T(8,128)S(1)} %get-tuple-element.63), channel_id=1, source_target_pairs={{0,8},{1,9},{2,10},{3,11},{4,12},{5,13},{6,14},{7,15},{8,16},{9,17... | collective-permute-start | bytes 1179656 | tf_op jit(solution)/shard_map/ppermute | solution.py:48
  148.3 14.6 %collective-permute-start.19 = (f32[768,128]{1,0:T(8,128)S(1)}, f32[768,128]{1,0:T(8,128)S(1)}, u32[]{:S(2)}, u32[]{:S(2)}) collective-permute-start(f32[768,128]{1,0:T(8,128)S(1)} %get-tuple-element.64), channel_id=1, source_target_pairs={{0,24},{1,25},{2,26},{3,27},{4,28},{5,29},{6,30},{7,31},{8,0},{9,1... | collective-permute-start | bytes 1179656 | tf_op jit(solution)/shard_map/ppermute | solution.py:48
  152.0 44.4 %all-to-all-start.1 = ((f32[4,1664,128]{2,1,0:T(8,128)}), f32[4,1664,128]{2,1,0:T(8,128)}, u32[]{:S(2)}, u32[]{:S(2)}) async-start(f32[4,1664,128]{2,1,0:T(8,128)} %pad_maximum_fusion), calls=%async_computation.1 | async-start | bytes 6815744 | tf_op jit(solution)/shard_map/all_to_all | solution.py:271
  164.1 19.0 %collective-permute-start.18 = (f32[1536,128]{1,0:T(8,128)S(1)}, f32[1536,128]{1,0:T(8,128)}, u32[]{:S(2)}, u32[]{:S(2)}) collective-permute-start(f32[1536,128]{1,0:T(8,128)S(1)} %pad_maximum_fusion.15), channel_id=1, source_target_pairs={{0,8},{1,9},{2,10},{3,11},{4,12},{5,13},{6,14},{7,15},{8,16},{9,17... | collective-permute-start | bytes 2359304 | tf_op jit(solution)/shard_map/ppermute | solution.py:48
  164.6 18.5 %collective-permute-start.20 = (f32[1536,128]{1,0:T(8,128)S(1)}, f32[1536,128]{1,0:T(8,128)}, u32[]{:S(2)}, u32[]{:S(2)}) collective-permute-start(f32[1536,128]{1,0:T(8,128)S(1)} %pad_maximum_fusion.16), channel_id=1, source_target_pairs={{0,24},{1,25},{2,26},{3,27},{4,28},{5,29},{6,30},{7,31},{8,0},{9,1... | collective-permute-start | bytes 2359304 | tf_op jit(solution)/shard_map/ppermute | solution.py:48
  171.5 17.3 %collective-permute-start.10 = (f32[1536,128]{1,0:T(8,128)S(1)}, f32[1536,128]{1,0:T(8,128)}, u32[]{:S(2)}, u32[]{:S(2)}) collective-permute-start(f32[1536,128]{1,0:T(8,128)S(1)} %pad_maximum_fusion.13), channel_id=1, source_target_pairs={{0,1},{1,64},{2,3},{3,66},{4,5},{5,68},{6,7},{7,70},{8,9},{9,72},{... | collective-permute-start | bytes 2359304 | tf_op jit(solution)/shard_map/ppermute | solution.py:48
  174.8 18.3 %collective-permute-start.12 = (f32[1536,128]{1,0:T(8,128)}, f32[1536,128]{1,0:T(8,128)}, u32[]{:S(2)}, u32[]{:S(2)}) collective-permute-start(f32[1536,128]{1,0:T(8,128)} %pad_maximum_fusion.14), channel_id=1, source_target_pairs={{0,65},{1,0},{2,67},{3,2},{4,69},{5,4},{6,71},{7,6},{8,73},{9,8},{... | collective-permute-start | bytes 2359304 | tf_op jit(solution)/shard_map/ppermute | solution.py:48
  201.1 14.2 %collective-permute-start.21 = (f32[1024,128]{1,0:T(8,128)}, f32[1024,128]{1,0:T(8,128)}, u32[]{:S(2)}, u32[]{:S(2)}) collective-permute-start(f32[1024,128]{1,0:T(8,128)} %get-tuple-element.88), channel_id=1, source_target_pairs={{0,1},{1,64},{2,3},{3,66},{4,5},{5,68},{6,7},{7,70},{8,9},{9,72},{... | collective-permute-start | bytes 1572872 | tf_op jit(solution)/shard_map/ppermute | solution.py:48
  201.1 14.2 %collective-permute-start.22 = (f32[1024,128]{1,0:T(8,128)}, f32[1024,128]{1,0:T(8,128)}, u32[]{:S(2)}, u32[]{:S(2)}) collective-permute-start(f32[1024,128]{1,0:T(8,128)} %get-tuple-element.87), channel_id=1, source_target_pairs={{0,64},{1,65},{2,66},{3,67},{4,68},{5,69},{6,70},{7,71},{8,72},{9,... | collective-permute-start | bytes 1572872 | tf_op jit(solution)/shard_map/ppermute | solution.py:48
  204.3 23.9 %collective-permute-start.23 = (f32[1024,128]{1,0:T(8,128)}, f32[1024,128]{1,0:T(8,128)}, u32[]{:S(2)}, u32[]{:S(2)}) collective-permute-start(f32[1024,128]{1,0:T(8,128)} %get-tuple-element.93), channel_id=1, source_target_pairs={{0,65},{1,0},{2,67},{3,2},{4,69},{5,4},{6,71},{7,6},{8,73},{9,8},{... | collective-permute-start | bytes 1572872 | tf_op jit(solution)/shard_map/ppermute | solution.py:48
  206.8 22.9 %all-to-all-start.2 = ((f32[4,384,128]{2,1,0:T(8,128)}), f32[4,384,128]{2,1,0:T(8,128)S(1)}, u32[]{:S(2)}, u32[]{:S(2)}) async-start(f32[4,384,128]{2,1,0:T(8,128)} %bitcast.43), calls=%async_computation.2 | async-start | bytes 1572864 | tf_op jit(solution)/shard_map/all_to_all | solution.py:271
  230.5 13.6 %collective-permute-start.29 = (f32[640,128]{1,0:T(8,128)S(1)}, f32[640,128]{1,0:T(8,128)S(1)}, u32[]{:S(2)}, u32[]{:S(2)}) collective-permute-start(f32[640,128]{1,0:T(8,128)S(1)} %pad_maximum_fusion.22), channel_id=1, source_target_pairs={{0,32},{1,33},{2,34},{3,35},{4,36},{5,37},{6,38},{7,39},{8,40},{9,... | collective-permute-start | bytes 983048 | tf_op jit(solution)/shard_map/ppermute | solution.py:48
  231.0 13.0 %collective-permute-start.27 = (f32[384,128]{1,0:T(8,128)}, f32[384,128]{1,0:T(8,128)S(1)}, u32[]{:S(2)}, u32[]{:S(2)}) collective-permute-start(f32[384,128]{1,0:T(8,128)} %reduce_sum.29), channel_id=1, source_target_pairs={{0,0},{1,1},{2,32},{3,33},{4,64},{5,65},{6,96},{7,97},{8,8},{9,9},... | collective-permute-start | bytes 589832 | tf_op jit(solution)/shard_map/ppermute | solution.py:48
  244.8 19.3 %collective-permute-start.30 = (f32[1024,128]{1,0:T(8,128)S(1)}, f32[1024,128]{1,0:T(8,128)S(1)}, u32[]{:S(2)}, u32[]{:S(2)}) collective-permute-start(f32[1024,128]{1,0:T(8,128)S(1)} %pad_maximum_fusion.20), channel_id=1, source_target_pairs={{0,0},{1,1},{2,2},{3,3},{4,4},{5,5},{6,6},{7,7},{8,32},{9,33},{10,... | collective-permute-start | bytes 1572872 | tf_op jit(solution)/shard_map/ppermute | solution.py:48
  (24 other events, 230.7 us)

commit v7 on v6

--- a/solution.py
+++ b/solution.py
@@ -267,6 +267,19 @@
     return slots[0] + send(plus, along(axis, 1)) + send(minus, along(axis, -1))
 
 
+def ring_sums(slots, extra, axis):
+    half, middle = slots.shape[1] // 2, extra.shape[0] // 2
+    behind = send(jnp.concatenate([slots[2, :half], extra]), along(axis, 1))
+    ahead = send(jnp.concatenate([slots[2, half:], extra]), along(axis, -1))
+    near = extra + behind[half:] + ahead[half:]
+    plus = [slots[1, :half] + behind[:half], slots[1, half:], behind[half : half + middle]]
+    minus = [slots[3, :half], slots[3, half:] + ahead[:half], ahead[half + middle :]]
+    behind = send(jnp.concatenate(plus), along(axis, 1))
+    ahead = send(jnp.concatenate(minus), along(axis, -1))
+    total = slots[0] + behind[: 2 * half] + ahead[: 2 * half]
+    return total, near + jnp.concatenate([behind[2 * half :], ahead[2 * half :]])
+
+
 def trade(value, groups):
     return lax.all_to_all(value, "col", 0, 0, axis_index_groups=groups, tiled=True)
 
@@ -349,17 +362,17 @@
 
     rhs_mine = jnp.where((leaf == 0) & (col % 2 == 0), right_sides[0:BLK], 0.0)
     extra = jnp.concatenate([sum_y[quarter:], rhs_mine])
-    slots_y = [jnp.concatenate([sum_y[k * 256 : (k + 1) * 256], extra]) for k in range(4)]
+    slots_y = sum_y[0:quarter].reshape(4, 256, BLK)
     slots_z = [sum_z[k * 384 : (k + 1) * 384] for k in range(4)]
-    sum_y = slots_y[0] + sum(arrivals(slots_y, "z"))
+    sum_y, extra = ring_sums(slots_y, extra, "z")
     sum_x = jnp.sum(trade(sum_x.reshape(4, 384, BLK), Y_GROUPS), axis=0)
     sum_z = slots_z[0] + sum(arrivals(slots_z, "x"))
-    sum_x, sum_y, sum_z = lax.optimization_barrier((sum_x, sum_y, sum_z))
-    pivot_block, rhs_rows = sum_y[768:896], sum_y[896:1024]
+    sum_x, sum_y, sum_z, extra = lax.optimization_barrier((sum_x, sum_y, sum_z, extra))
+    pivot_block, rhs_rows = extra[512:640], extra[640:768]
     strip_x = send(sum_x, TURN).reshape(8, 48, BLK)
     strip_z = send(sum_z, SWAP).reshape(8, 48, BLK)
 
-    mine = jnp.concatenate([sum_y[256 : 256 + 512], rhs_rows])
+    mine = jnp.concatenate([extra[0:512], rhs_rows])
     other = send(mine, SIBLING)
     pivot_block, strip_x, strip_z, other = lax.optimization_barrier(
         (pivot_block, strip_x, strip_z, other)
@@ -377,7 +390,7 @@
         lower, jnp.eye(BLK, dtype=jnp.float32), left_side=True, lower=True
     )
 
-    strip_y = sum_y[0:256].reshape(8, 32, BLK)
+    strip_y = sum_y.reshape(8, 32, BLK)
     assembled = jnp.concatenate([strip_x, strip_z, strip_y], axis=1).reshape(1024, BLK)
     row_global = (leaf * 1024 + jnp.arange(1024, dtype=jnp.int32))[:, None]
     solved = lax.dot_general(my_rows, inverse, (((1,), (1,)), ((), ())), precision=HIGHEST)

time: 283 us -> 283 us (level)
  local copies, waits for them, and re-layouts: 15.7 us -> 19.6 us
  waiting for transfers between devices: 95.6 us -> 91.7 us
  other arithmetic: 50.3 us -> 53.4 us
    ppermute x31 -> x32, waiting for transfers between devices: 94.8 us -> 90.6 us  [send(): return lax.ppermute(value, AXES, pairs)]
    slice x5 -> x7, local copies, waits for them, and re-layouts: 0.1 us -> 3.83 us  [the longest x1 0.94 us: ring_sums(): behind[half:half + middle]]
    ppermute x31 -> x32, starting transfers between devices: 41.9 us -> 40.5 us  [send(): return lax.ppermute(value, AXES, pairs)]
  transfers between devices with their start and end apart: 34 -> 35, of which waited for: 13 -> 15; matrix products, arithmetic and copies ran while one was open for 17% -> 18% of each run, Pallas kernels for 4% -> 4%
where the time goes in v7:
time: 283 us; the launch traced here: 279 us
  waiting for transfers between devices  91.7 us (32%)
  starting transfers between devices  55.2 us (20%)
  Pallas kernels  53.5 us (19%)
  other arithmetic  53.4 us (19%)
  local copies, waits for them, and re-layouts  19.6 us (7%)
  matrix products  4.08 us (1%)
    ppermute x32, waiting for transfers between devices, send(): return lax.ppermute(value, AXES, pairs)  90.6 us
    ppermute x32, starting transfers between devices, send(): return lax.ppermute(value, AXES, pairs)  40.5 us
    pallas_call x1, Pallas kernels, make_updates(): pl.pallas_call(update, grid_spec=pltpu.PrefetchScalarGridSpec(num_scalar_...  24.4 us
    pallas_call x1, Pallas kernels, rest(): pl.pallas_call(expand_rest, in_specs=[smem] * 8 + [vmem] * 7, out_specs=[...  17.4 us
    all_to_all x3, starting transfers between devices, trade(): lax.all_to_all(value, 'col', 0, 0, axis_index_groups=groups, tiled=True)  14.7 us
    another operation x3, other arithmetic, per_device(): lower = jnp.tril(lax.linalg.cholesky(pivot_block, symmetrize_input=False))  12.4 us
    pallas_call x1, Pallas kernels, make_expands(): pl.pallas_call(expand_near, in_specs=[smem] * 4 + [vmem] * 6, out_specs=[...  11.7 us
    another operation x2, other arithmetic, per_device(): lax.linalg.triangular_solve(lower, jnp.eye(BLK, dtype=jnp.float32), left_...  9.82 us
  transfers between devices with their start and end apart: 35, of which 15 were waited for; matrix products, arithmetic and copies ran while one was open for 18% of the time, Pallas kernels for 4%

profile of v7, /device:TPU:97, one launch (start us, length us, event | category | flops | bytes accessed | tf_op | source)
XLA Modules:
  0.0 279.1 jit_solution(262847302004797363)
XLA Ops:
  3.2 24.4 %update.1 = (f32[4,16,48,128]{3,2,1,0:T(8,128)}, f32[6,16,48,128]{3,2,1,0:T(8,128)}, f32[6,16,48,128]{3,2,1,0:T(8,128)}, f32[4,16,48,128]{3,2,1,0:T(8,128)}, f32...) custom-call(s32[6]{0:T(128)S(1)} %stack.71.pos, bf16[16,128,1536]{2,1,0:T(8,128)(2,1)} %bitcast.140, ...), custom_call_target="tpu_custom_call" | custom-call | flops 12884901888 | bytes 41943040 | tf_op jit(solution)/shard_map/update/pallas_call | solution.py:98
  27.6 5.1 %all-to-all-start = ((f32[4,84,32,128]{3,2,1,0:T(8,128)}), f32[4,84,32,128]{3,2,1,0:T(8,128)}, u32[]{:S(2)}, u32[]{:S(2)}) async-start(f32[4,84,32,128]{3,2,1,0:T(8,128)} %get-tuple-element.31), calls=%async_computation | async-start | bytes 11010048 | tf_op jit(solution)/shard_map/all_to_all | solution.py:284
  39.3 47.1 %collective-permute-done.refs_1_ = f32[96,48,128]{2,1,0:T(8,128)S(1)} collective-permute-done((f32[96,48,128]{2,1,0:T(8,128)}, f32[96,48,128]{2,1,0:T(8,128)S(1)}, u32[]{:S(2)}, u32[]{:S(2)}) %collective-permute-start) | collective-permute-done | bytes 2359328 | tf_op jit(solution)/shard_map/ppermute | solution.py:48
  96.3 11.7 %expand_near.1 = (f32[256,48,128]{2,1,0:T(8,128)}, f32[256,48,128]{2,1,0:T(8,128)}) custom-call(s32[4,16]{1,0:T(4,128)} %get-tuple-element.61.at_x, s32[4,4]{1,0:T(4,128)} %constant_dynamic-slice_fusion.7.down_x, s32[4,16]{1,0:T(4,128)} %get-tuple-element.59.at_z, s32[4,4]{1,0:T(4,128)} %constant_dynamic-slice_fusion.2.down_z, f32[64,48,128]{2,1,0:T(8,128)} %bitcast.127, ...), custom_call_target="tpu_custom_call" | custom-call | flops 8388608 | bytes 31457280 | tf_op jit(solution)/shard_map/expand_near/pallas_call | solution.py:226
  108.8 2.5 collective-permute-done.7.refs_5_
  111.4 17.4 %expand_rest.1 = (f32[148,32,128]{2,1,0:T(8,128)}, f32[148,32,128]{2,1,0:T(8,128)}, f32[128,48,128]{2,1,0:T(8,128)}, f32[128,48,128]{2,1,0:T(8,128)}, f32[128,48,128]{2,1,0:T(8,128)}, /*index=5*/f32[128,48,128]{2,1,0:T(8,128)}) custom-call(s32[6]{0:T(128)} %copy-done.2, s32[4,32]{1,0:T(4,128)} %broadcast_add_fusion.places, s32[4,8]{1,0:T(4,128)} %fusion.29.at_y, ...), custom_call_target="tpu_custom_call" | custom-call | flops 8388608 | bytes 31457280 | tf_op jit(solution)/shard_map/expand_rest/pallas_call | solution.py:237
  128.7 3.0 %collective-permute-start.13 = (f32[148,32,128]{2,1,0:T(8,128)}, f32[148,32,128]{2,1,0:T(8,128)S(1)}, u32[]{:S(2)}, u32[]{:S(2)}) collective-permute-start(f32[148,32,128]{2,1,0:T(8,128)} %get-tuple-element.43), channel_id=1, source_target_pairs={{0,32},{1,33},{2,34},{3,35},{4,36},{5,37},{6,38},{7,39},{8,40},{9,... | collective-permute-start | bytes 7274504 | tf_op jit(solution)/shard_map/ppermute | solution.py:48
  133.8 4.9 %collective-permute-done.13 = f32[148,32,128]{2,1,0:T(8,128)S(1)} collective-permute-done((f32[148,32,128]{2,1,0:T(8,128)}, f32[148,32,128]{2,1,0:T(8,128)S(1)}, u32[]{:S(2)}, u32[]{:S(2)}) %collective-permute-start.13) | collective-permute-done | bytes 2424864 | tf_op jit(solution)/shard_map/ppermute | solution.py:48
  152.1 4.7 %all-to-all-start.1 = ((f32[4,1664,128]{2,1,0:T(8,128)}), f32[4,1664,128]{2,1,0:T(8,128)}, u32[]{:S(2)}, u32[]{:S(2)}) async-start(f32[4,1664,128]{2,1,0:T(8,128)} %pad_maximum_fusion), calls=%async_computation.1 | async-start | bytes 6815744 | tf_op jit(solution)/shard_map/all_to_all | solution.py:284
  156.8 3.2 %add.638 = f32[128,48,128]{2,1,0:T(8,128)S(1)} add(f32[128,48,128]{2,1,0:T(8,128)} %get-tuple-element.40, f32[128,48,128]{2,1,0:T(8,128)} %collective-permute-done.8) | non-fusion elementwise | flops 786432 | bytes 9437184 | tf_op jit(solution)/shard_map/add | solution.py:346
  164.7 2.3 collective-permute-start.20
  167.1 4.2 %collective-permute-done.11 = f32[768,128]{1,0:T(8,128)S(1)} collective-permute-done((f32[768,128]{1,0:T(8,128)S(1)}, f32[768,128]{1,0:T(8,128)S(1)}, u32[]{:S(2)}, u32[]{:S(2)}) %collective-permute-start.11) | collective-permute-done | bytes 393248 | tf_op jit(solution)/shard_map/ppermute | solution.py:48
  171.5 2.4 collective-permute-start.10
  178.1 5.1 %collective-permute-done.18 = f32[1536,128]{1,0:T(8,128)} collective-permute-done((f32[1536,128]{1,0:T(8,128)S(1)}, f32[1536,128]{1,0:T(8,128)}, u32[]{:S(2)}, u32[]{:S(2)}) %collective-permute-start.18) | collective-permute-done | bytes 786464 | tf_op jit(solution)/shard_map/ppermute | solution.py:48
  184.6 4.1 %collective-permute-done.10 = f32[1536,128]{1,0:T(8,128)} collective-permute-done((f32[1536,128]{1,0:T(8,128)S(1)}, f32[1536,128]{1,0:T(8,128)}, u32[]{:S(2)}, u32[]{:S(2)}) %collective-permute-start.10) | collective-permute-done | bytes 786464 | tf_op jit(solution)/shard_map/ppermute | solution.py:48
  188.7 4.4 %collective-permute-done.12 = f32[1536,128]{1,0:T(8,128)} collective-permute-done((f32[1536,128]{1,0:T(8,128)}, f32[1536,128]{1,0:T(8,128)}, u32[]{:S(2)}, u32[]{:S(2)}) %collective-permute-start.12) | collective-permute-done | bytes 786464 | tf_op jit(solution)/shard_map/ppermute | solution.py:48
  193.1 2.4 fusion.8
  205.7 4.9 %all-to-all-start.2 = ((f32[4,384,128]{2,1,0:T(8,128)}), f32[4,384,128]{2,1,0:T(8,128)S(1)}, u32[]{:S(2)}, u32[]{:S(2)}) async-start(f32[4,384,128]{2,1,0:T(8,128)} %bitcast.43), calls=%async_computation.2 | async-start | bytes 1572864 | tf_op jit(solution)/shard_map/all_to_all | solution.py:284
  221.0 2.7 collective-permute-done.24
  227.0 5.4 %collective-permute-start.30 = (f32[640,128]{1,0:T(8,128)S(1)}, f32[640,128]{1,0:T(8,128)S(1)}, u32[]{:S(2)}, u32[]{:S(2)}) collective-permute-start(f32[640,128]{1,0:T(8,128)S(1)} %pad_maximum_fusion.19), channel_id=1, source_target_pairs={{0,32},{1,33},{2,34},{3,35},{4,36},{5,37},{6,38},{7,39},{8,40},{9,... | collective-permute-start | bytes 983048 | tf_op jit(solution)/shard_map/ppermute | solution.py:48
  235.1 10.0 %collective-permute-done.28 = f32[384,128]{1,0:T(8,128)S(1)} collective-permute-done((f32[384,128]{1,0:T(8,128)S(1)}, f32[384,128]{1,0:T(8,128)S(1)}, u32[]{:S(2)}, u32[]{:S(2)}) %collective-permute-start.28) | collective-permute-done | bytes 196640 | tf_op jit(solution)/shard_map/ppermute | solution.py:48
  248.1 11.7 %cholesky.19 = f32[128,128]{1,0:T(8,128)S(1)} custom-call(f32[128,128]{1,0:T(8,128)S(1)} %get-tuple-element.52), custom_call_target="Cholesky" | custom-call | tf_op jit(solution)/shard_map/cholesky | solution.py:380
  262.1 3.1 %collective-permute-done.31 = f32[1024,128]{1,0:T(8,128)S(1)} collective-permute-done((f32[1024,128]{1,0:T(8,128)S(1)}, f32[1024,128]{1,0:T(8,128)S(1)}, u32[]{:S(2)}, u32[]{:S(2)}) %collective-permute-start.31) | collective-permute-done | bytes 524320 | tf_op jit(solution)/shard_map/ppermute | solution.py:48
  265.2 9.8 %custom-call.5 = f32[1,128,128]{1,2,0:T(8,128)S(1)} custom-call(f32[1,128,128]{2,1,0:T(8,128)S(1)} %select_bitcast_fusion), custom_call_target="InvertDiagBlocksLowerTriangular" | custom-call | tf_op jit(solution)/shard_map/triangular_solve | solution.py:389
  (165 shorter events, 80.7 us)
Async XLA Ops:
  27.6 83.8 %all-to-all-start = ((f32[4,84,32,128]{3,2,1,0:T(8,128)}), f32[4,84,32,128]{3,2,1,0:T(8,128)}, u32[]{:S(2)}, u32[]{:S(2)}) async-start(f32[4,84,32,128]{3,2,1,0:T(8,128)} %get-tuple-element.31), calls=%async_computation | async-start | bytes 11010048 | tf_op jit(solution)/shard_map/all_to_all | solution.py:284
  32.7 53.7 %collective-permute-start = (f32[96,48,128]{2,1,0:T(8,128)}, f32[96,48,128]{2,1,0:T(8,128)S(1)}, u32[]{:S(2)}, u32[]{:S(2)}) collective-permute-start(f32[96,48,128]{2,1,0:T(8,128)} %bitcast.144), channel_id=1, source_target_pairs={{0,2},{1,3},{2,4},{3,5},{4,6},{5,7},{6,0},{7,1},{8,10},{9,11},{10,... | collective-permute-start | bytes 7077896 | tf_op jit(solution)/shard_map/ppermute | solution.py:48
  34.0 52.6 %collective-permute-start.1 = (f32[96,48,128]{2,1,0:T(8,128)}, f32[96,48,128]{2,1,0:T(8,128)}, u32[]{:S(2)}, u32[]{:S(2)}) collective-permute-start(f32[96,48,128]{2,1,0:T(8,128)} %bitcast.143), channel_id=1, source_target_pairs={{0,6},{1,7},{2,0},{3,1},{4,2},{5,3},{6,4},{7,5},{8,14},{9,15},{10,... | collective-permute-start | bytes 7077896 | tf_op jit(solution)/shard_map/ppermute | solution.py:48
  35.4 55.0 %collective-permute-start.2 = (f32[96,48,128]{2,1,0:T(8,128)}, f32[96,48,128]{2,1,0:T(8,128)}, u32[]{:S(2)}, u32[]{:S(2)}) collective-permute-start(f32[96,48,128]{2,1,0:T(8,128)} %bitcast.142), channel_id=1, source_target_pairs={{0,1},{1,64},{2,3},{3,66},{4,5},{5,68},{6,7},{7,70},{8,9},{9,72},{... | collective-permute-start | bytes 7077896 | tf_op jit(solution)/shard_map/ppermute | solution.py:48
  35.4 56.3 %collective-permute-start.3 = (f32[96,48,128]{2,1,0:T(8,128)}, f32[96,48,128]{2,1,0:T(8,128)}, u32[]{:S(2)}, u32[]{:S(2)}) collective-permute-start(f32[96,48,128]{2,1,0:T(8,128)} %bitcast.141), channel_id=1, source_target_pairs={{0,65},{1,0},{2,67},{3,2},{4,69},{5,4},{6,71},{7,6},{8,73},{9,8},{... | collective-permute-start | bytes 7077896 | tf_op jit(solution)/shard_map/ppermute | solution.py:48
  86.4 21.6 %collective-permute-start.4 = (f32[32,48,128]{2,1,0:T(8,128)S(1)}, f32[32,48,128]{2,1,0:T(8,128)S(1)}, u32[]{:S(2)}, u32[]{:S(2)}) collective-permute-start(f32[32,48,128]{2,1,0:T(8,128)S(1)} %slice.257), channel_id=1, source_target_pairs={{0,2},{1,3},{2,4},{3,5},{4,6},{5,7},{6,0},{7,1},{8,10},{9,11},{10,... | collective-permute-start | bytes 2359304 | tf_op jit(solution)/shard_map/ppermute | solution.py:48
  88.3 19.7 %collective-permute-start.5 = (f32[32,48,128]{2,1,0:T(8,128)S(1)}, f32[32,48,128]{2,1,0:T(8,128)}, u32[]{:S(2)}, u32[]{:S(2)}) collective-permute-start(f32[32,48,128]{2,1,0:T(8,128)S(1)} %slice.258), channel_id=1, source_target_pairs={{0,6},{1,7},{2,0},{3,1},{4,2},{5,3},{6,4},{7,5},{8,14},{9,15},{10,... | collective-permute-start | bytes 2359304 | tf_op jit(solution)/shard_map/ppermute | solution.py:48
  91.6 17.2 %collective-permute-start.6 = (f32[32,48,128]{2,1,0:T(8,128)S(1)}, f32[32,48,128]{2,1,0:T(8,128)}, u32[]{:S(2)}, u32[]{:S(2)}) collective-permute-start(f32[32,48,128]{2,1,0:T(8,128)S(1)} %slice.259), channel_id=1, source_target_pairs={{0,1},{1,64},{2,3},{3,66},{4,5},{5,68},{6,7},{7,70},{8,9},{9,72},{... | collective-permute-start | bytes 2359304 | tf_op jit(solution)/shard_map/ppermute | solution.py:48
  92.9 18.4 %collective-permute-start.7 = (f32[32,48,128]{2,1,0:T(8,128)S(1)}, f32[32,48,128]{2,1,0:T(8,128)}, u32[]{:S(2)}, u32[]{:S(2)}) collective-permute-start(f32[32,48,128]{2,1,0:T(8,128)S(1)} %slice.260), channel_id=1, source_target_pairs={{0,65},{1,0},{2,67},{3,2},{4,69},{5,4},{6,71},{7,6},{8,73},{9,8},{... | collective-permute-start | bytes 2359304 | tf_op jit(solution)/shard_map/ppermute | solution.py:48
  131.8 25.0 %collective-permute-start.8 = (f32[128,48,128]{2,1,0:T(8,128)}, f32[128,48,128]{2,1,0:T(8,128)}, u32[]{:S(2)}, u32[]{:S(2)}) collective-permute-start(f32[128,48,128]{2,1,0:T(8,128)} %get-tuple-element.41), channel_id=1, source_target_pairs={{0,32},{1,33},{2,34},{3,35},{4,36},{5,37},{6,38},{7,39},{8,40},{9,... | collective-permute-start | bytes 9437192 | tf_op jit(solution)/shard_map/ppermute | solution.py:48
  147.3 15.6 %collective-permute-start.17 = (f32[768,128]{1,0:T(8,128)S(1)}, f32[768,128]{1,0:T(8,128)S(1)}, u32[]{:S(2)}, u32[]{:S(2)}) collective-permute-start(f32[768,128]{1,0:T(8,128)S(1)} %get-tuple-element.65), channel_id=1, source_target_pairs={{0,8},{1,9},{2,10},{3,11},{4,12},{5,13},{6,14},{7,15},{8,16},{9,17... | collective-permute-start | bytes 1179656 | tf_op jit(solution)/shard_map/ppermute | solution.py:48
  148.4 14.5 %collective-permute-start.19 = (f32[768,128]{1,0:T(8,128)S(1)}, f32[768,128]{1,0:T(8,128)S(1)}, u32[]{:S(2)}, u32[]{:S(2)}) collective-permute-start(f32[768,128]{1,0:T(8,128)S(1)} %get-tuple-element.66), channel_id=1, source_target_pairs={{0,24},{1,25},{2,26},{3,27},{4,28},{5,29},{6,30},{7,31},{8,0},{9,1... | collective-permute-start | bytes 1179656 | tf_op jit(solution)/shard_map/ppermute | solution.py:48
  152.1 44.3 %all-to-all-start.1 = ((f32[4,1664,128]{2,1,0:T(8,128)}), f32[4,1664,128]{2,1,0:T(8,128)}, u32[]{:S(2)}, u32[]{:S(2)}) async-start(f32[4,1664,128]{2,1,0:T(8,128)} %pad_maximum_fusion), calls=%async_computation.1 | async-start | bytes 6815744 | tf_op jit(solution)/shard_map/all_to_all | solution.py:284
  164.2 19.0 %collective-permute-start.18 = (f32[1536,128]{1,0:T(8,128)S(1)}, f32[1536,128]{1,0:T(8,128)}, u32[]{:S(2)}, u32[]{:S(2)}) collective-permute-start(f32[1536,128]{1,0:T(8,128)S(1)} %pad_maximum_fusion.11), channel_id=1, source_target_pairs={{0,8},{1,9},{2,10},{3,11},{4,12},{5,13},{6,14},{7,15},{8,16},{9,17... | collective-permute-start | bytes 2359304 | tf_op jit(solution)/shard_map/ppermute | solution.py:48
  164.7 18.5 %collective-permute-start.20 = (f32[1536,128]{1,0:T(8,128)S(1)}, f32[1536,128]{1,0:T(8,128)}, u32[]{:S(2)}, u32[]{:S(2)}) collective-permute-start(f32[1536,128]{1,0:T(8,128)S(1)} %pad_maximum_fusion.12), channel_id=1, source_target_pairs={{0,24},{1,25},{2,26},{3,27},{4,28},{5,29},{6,30},{7,31},{8,0},{9,1... | collective-permute-start | bytes 2359304 | tf_op jit(solution)/shard_map/ppermute | solution.py:48
  171.5 17.3 %collective-permute-start.10 = (f32[1536,128]{1,0:T(8,128)S(1)}, f32[1536,128]{1,0:T(8,128)}, u32[]{:S(2)}, u32[]{:S(2)}) collective-permute-start(f32[1536,128]{1,0:T(8,128)S(1)} %pad_maximum_fusion.9), channel_id=1, source_target_pairs={{0,1},{1,64},{2,3},{3,66},{4,5},{5,68},{6,7},{7,70},{8,9},{9,72},{... | collective-permute-start | bytes 2359304 | tf_op jit(solution)/shard_map/ppermute | solution.py:48
  174.8 18.3 %collective-permute-start.12 = (f32[1536,128]{1,0:T(8,128)}, f32[1536,128]{1,0:T(8,128)}, u32[]{:S(2)}, u32[]{:S(2)}) collective-permute-start(f32[1536,128]{1,0:T(8,128)} %pad_maximum_fusion.10), channel_id=1, source_target_pairs={{0,65},{1,0},{2,67},{3,2},{4,69},{5,4},{6,71},{7,6},{8,73},{9,8},{... | collective-permute-start | bytes 2359304 | tf_op jit(solution)/shard_map/ppermute | solution.py:48
  202.1 14.7 %collective-permute-start.25 = (f32[384,128]{1,0:T(8,128)}, f32[384,128]{1,0:T(8,128)}, u32[]{:S(2)}, u32[]{:S(2)}) collective-permute-start(f32[384,128]{1,0:T(8,128)} %get-tuple-element.81), channel_id=1, source_target_pairs={{0,2},{1,3},{2,4},{3,5},{4,6},{5,7},{6,0},{7,1},{8,10},{9,11},{10,... | collective-permute-start | bytes 589832 | tf_op jit(solution)/shard_map/ppermute | solution.py:48
  202.4 14.4 %collective-permute-start.26 = (f32[384,128]{1,0:T(8,128)}, f32[384,128]{1,0:T(8,128)}, u32[]{:S(2)}, u32[]{:S(2)}) collective-permute-start(f32[384,128]{1,0:T(8,128)} %get-tuple-element.79), channel_id=1, source_target_pairs={{0,4},{1,5},{2,6},{3,7},{4,0},{5,1},{6,2},{7,3},{8,12},{9,13},{10,... | collective-permute-start | bytes 589832 | tf_op jit(solution)/shard_map/ppermute | solution.py:48
  204.5 12.3 %collective-permute-start.27 = (f32[384,128]{1,0:T(8,128)}, f32[384,128]{1,0:T(8,128)}, u32[]{:S(2)}, u32[]{:S(2)}) collective-permute-start(f32[384,128]{1,0:T(8,128)} %get-tuple-element.80), channel_id=1, source_target_pairs={{0,6},{1,7},{2,0},{3,1},{4,2},{5,3},{6,4},{7,5},{8,14},{9,15},{10,... | collective-permute-start | bytes 589832 | tf_op jit(solution)/shard_map/ppermute | solution.py:48
  205.7 13.2 %all-to-all-start.2 = ((f32[4,384,128]{2,1,0:T(8,128)}), f32[4,384,128]{2,1,0:T(8,128)S(1)}, u32[]{:S(2)}, u32[]{:S(2)}) async-start(f32[4,384,128]{2,1,0:T(8,128)} %bitcast.43), calls=%async_computation.2 | async-start | bytes 1572864 | tf_op jit(solution)/shard_map/all_to_all | solution.py:284
  227.0 18.1 %collective-permute-start.30 = (f32[640,128]{1,0:T(8,128)S(1)}, f32[640,128]{1,0:T(8,128)S(1)}, u32[]{:S(2)}, u32[]{:S(2)}) collective-permute-start(f32[640,128]{1,0:T(8,128)S(1)} %pad_maximum_fusion.19), channel_id=1, source_target_pairs={{0,32},{1,33},{2,34},{3,35},{4,36},{5,37},{6,38},{7,39},{8,40},{9,... | collective-permute-start | bytes 983048 | tf_op jit(solution)/shard_map/ppermute | solution.py:48
  232.4 12.7 %collective-permute-start.28 = (f32[384,128]{1,0:T(8,128)S(1)}, f32[384,128]{1,0:T(8,128)S(1)}, u32[]{:S(2)}, u32[]{:S(2)}) collective-permute-start(f32[384,128]{1,0:T(8,128)S(1)} %reduce_sum.29), channel_id=1, source_target_pairs={{0,0},{1,1},{2,32},{3,33},{4,64},{5,65},{6,96},{7,97},{8,8},{9,9},... | collective-permute-start | bytes 589832 | tf_op jit(solution)/shard_map/ppermute | solution.py:48
  245.9 19.3 %collective-permute-start.31 = (f32[1024,128]{1,0:T(8,128)S(1)}, f32[1024,128]{1,0:T(8,128)S(1)}, u32[]{:S(2)}, u32[]{:S(2)}) collective-permute-start(f32[1024,128]{1,0:T(8,128)S(1)} %pad_maximum_fusion.15), channel_id=1, source_target_pairs={{0,0},{1,1},{2,2},{3,3},{4,4},{5,5},{6,6},{7,7},{8,32},{9,33},{10,... | collective-permute-start | bytes 1572872 | tf_op jit(solution)/shard_map/ppermute | solution.py:48
  (25 other events, 289.2 us)
